TPU v7x, 128 devices: a whole 4x4x4 slice. The times are simulated.
128 devices in a mesh: expert: 32 (over y, z, core), shard: 4 (over x).
Axes of the slice: x: 4, y: 4, z: 4, core: 2. Of those that a mesh axis runs over, the one named last changes fastest.
Arguments:
- tokens: bfloat16 [32768, 1536], P(('expert', 'shard')), may hold values from -6 to 6
- lengths: int32 [32, 4], P('expert'), may hold values from 1 to 896, 1024 in all within a row
- top_experts: int32 [32768, 4], P(('expert', 'shard')), may hold values from 0 to 31, all different within a row; in each aligned block of 256 rows (0 to 255, 256 to 511, ...) at most 48 rows name the same one
- w_qkv: bfloat16 [1536, 2048], P(('expert', 'shard')), may hold values from -0.15625 to 0.15625
- w_out: bfloat16 [1536, 1536], P(None, ('expert', 'shard')), may hold values from -0.875 to 0.875
- gain_attn: bfloat16 [1536], P(('expert', 'shard')), may hold values from 0.5 to 1.5
- gain_ffn: bfloat16 [1536], P(('expert', 'shard')), may hold values from 0.5 to 1.5
- router: bfloat16 [1536, 32], P(('expert', 'shard')), may hold values from -0.078125 to 0.078125
- gate_up: bfloat16 [32, 1536, 1536], P('expert'), may hold values from -0.15625 to 0.15625
- down_proj: bfloat16 [32, 768, 1536], P('expert'), may hold values from -0.4375 to 0.4375
- cotangent: bfloat16 [32768, 1536], P(('expert', 'shard')), may hold values from -6 to 6
Outputs:
- output: bfloat16 [32768, 1536], P(('expert', 'shard'))
- grad_tokens: bfloat16 [32768, 1536], P(('expert', 'shard'))
- grad_qkv: float32 [1536, 2048], P(('expert', 'shard'))
- grad_out: float32 [1536, 1536], P(None, ('expert', 'shard'))
- grad_gain_attn: float32 [1536], P(('expert', 'shard'))
- grad_gain_ffn: float32 [1536], P(('expert', 'shard'))
- grad_router: float32 [1536, 32], P(('expert', 'shard'))
- grad_gate_up: float32 [32, 1536, 1536], P('expert', 'shard')
- grad_down: float32 [32, 768, 1536], P('expert', None, 'shard')
Inputs may be any that keep to these rules, and one draw needn't show every extreme that they name: The 4 lengths of a group sum to 1024; the longest is 896. `top_experts`: each row names 4 different experts. Among the rows of one device no expert is named more than 48 times; in some devices' rows one expert is named exactly 48 times.
All inputs are finite; a program needn't handle non-finite values.
Results may differ from a plain program's by a relative error of at most 0.02.
Values may be sent and summed in bfloat16 or wider, within the bound.
A program may use at most 192 MiB of HBM per device.

v0:
```python
import jax
import jax.numpy as jnp
from jax import lax
from jax.sharding import PartitionSpec as P

D = 1536
HEADS_Q = 12
HEADS_KV = 2
HEAD_DIM = 128
FF = 768
TOP = 4


norm_eps = 1e-06
rope_base = 1000000.0
precise = lax.Precision.HIGHEST


def rms_scale(values, gain_vec):
    return (
        values * lax.rsqrt(jnp.mean(values * values, axis=-1, keepdims=True) + norm_eps) * gain_vec
    )


def rope_tables(position, half_dim):
    frequency = rope_base ** (-jnp.arange(half_dim, dtype=jnp.float32) / half_dim)
    angles = position.astype(jnp.float32)[:, None] * frequency[None, :]
    return (jnp.cos(angles)[:, None, :], jnp.sin(angles)[:, None, :])


def rotate(values, cosine, sine_tab):
    half_dim = values.shape[-1] // 2
    lower_half = values[..., :half_dim]
    upper_half = values[..., half_dim:]
    return jnp.concatenate(
        [lower_half * cosine - upper_half * sine_tab, lower_half * sine_tab + upper_half * cosine],
        axis=-1,
    )


def unrotate(grads_in, cosine, sine_tab):
    half_dim = grads_in.shape[-1] // 2
    lower_half = grads_in[..., :half_dim]
    upper_half = grads_in[..., half_dim:]
    return jnp.concatenate(
        [lower_half * cosine + upper_half * sine_tab, upper_half * cosine - lower_half * sine_tab],
        axis=-1,
    )


def seq_layout(seq_lens, row_ids):
    seq_ends = jnp.cumsum(seq_lens)
    segment = jnp.sum((row_ids[:, None] >= seq_ends[None, :]).astype(jnp.int32), axis=1)
    seq_start = jnp.sum(
        jnp.where(seq_ends[None, :] <= row_ids[:, None], seq_lens[None, :], 0), axis=1
    )
    return (segment, row_ids - seq_start)


def slot_table(top_block, experts, capacity):
    flat_ids = top_block.reshape(-1)
    onehot = (flat_ids[:, None] == jnp.arange(experts, dtype=jnp.int32)[None, :]).astype(jnp.int32)
    before = jnp.cumsum(onehot, axis=0) - onehot
    target = jnp.sum(
        onehot * (before + jnp.arange(experts, dtype=jnp.int32)[None, :] * capacity), axis=1
    )
    slot_hits = target[:, None] == jnp.arange(experts * capacity, dtype=jnp.int32)[None, :]
    return slot_hits.reshape(top_block.shape[0], top_block.shape[1], experts * capacity)


def body(
    tokens,
    lengths,
    top_experts,
    w_qkv,
    w_out,
    gain_attn,
    gain_ffn,
    router,
    gate_up,
    down_proj,
    cotangent,
):
    tok_count = tokens.shape[0]
    experts = lax.axis_size("expert")
    capacity = 3 * tok_count * TOP // (2 * experts)
    width_q = HEADS_Q * HEAD_DIM
    width_kv = HEADS_KV * HEAD_DIM
    repeat = HEADS_Q // HEADS_KV
    scale = HEAD_DIM ** (-0.5)
    full_qkv, full_out, attn_gain, ffn_gain, full_router = (
        lax.all_gather(w_qkv, ("expert", "shard"), axis=0, tiled=True),
        lax.all_gather(w_out, ("expert", "shard"), axis=1, tiled=True),
        lax.all_gather(gain_attn, ("expert", "shard"), axis=0, tiled=True),
        lax.all_gather(gain_ffn, ("expert", "shard"), axis=0, tiled=True),
        lax.all_gather(router, ("expert", "shard"), axis=0, tiled=True),
    )
    tok_f = tokens.astype(jnp.float32)
    attn_g = attn_gain.astype(jnp.float32)
    normed = rms_scale(tok_f, attn_g).astype(jnp.bfloat16)
    projected = jnp.dot(normed, full_qkv, preferred_element_type=jnp.float32)
    shard_pos = lax.axis_index("shard")
    group_rows = lax.axis_size("shard") * tok_count
    all_ids = jnp.arange(group_rows, dtype=jnp.int32)
    key_segment, key_position = seq_layout(lengths[0], all_ids)
    own_ids = shard_pos * tok_count + jnp.arange(tok_count, dtype=jnp.int32)
    own_segment = lax.dynamic_slice_in_dim(key_segment, shard_pos * tok_count, tok_count)
    own_position = lax.dynamic_slice_in_dim(key_position, shard_pos * tok_count, tok_count)
    cosine, sine_tab = rope_tables(own_position, HEAD_DIM // 2)
    queries = rotate(
        projected[:, :width_q].reshape(tok_count, HEADS_Q, HEAD_DIM), cosine, sine_tab
    ).astype(jnp.bfloat16)
    keys_rot = rotate(
        projected[:, width_q : width_q + width_kv].reshape(tok_count, HEADS_KV, HEAD_DIM),
        cosine,
        sine_tab,
    ).astype(jnp.bfloat16)
    values = projected[:, width_q + width_kv :].astype(jnp.bfloat16)
    local_kv = jnp.concatenate([keys_rot.reshape(tok_count, width_kv), values], axis=1)
    group_kv = lax.all_gather(local_kv, "shard", axis=0, tiled=True)
    keys_all = group_kv[:, :width_kv].reshape(group_rows, HEADS_KV, HEAD_DIM)
    values_all = group_kv[:, width_kv:].reshape(group_rows, HEADS_KV, HEAD_DIM)
    grouped = queries.reshape(tok_count, HEADS_KV, repeat, HEAD_DIM)
    allowed = (own_segment[:, None] == key_segment[None, :]) & (
        all_ids[None, :] <= own_ids[:, None]
    )

    def attn_scores():
        raw_scores = (
            jnp.einsum("tgrd,kgd->grtk", grouped, keys_all, preferred_element_type=jnp.float32)
            * scale
        )
        return jnp.where(allowed, raw_scores, -1e30)

    masked = attn_scores()
    top_score = jnp.max(masked, axis=-1, keepdims=True)
    expo_vals = jnp.exp(masked - top_score)
    total_weight = jnp.sum(expo_vals, axis=-1, keepdims=True)
    probs_low = (expo_vals / total_weight).astype(jnp.bfloat16)
    attended = (
        jnp.einsum("grtk,kgd->tgrd", probs_low, values_all, preferred_element_type=jnp.float32)
        .reshape(tok_count, width_q)
        .astype(jnp.bfloat16)
    )
    branch = jnp.dot(attended, full_out, preferred_element_type=jnp.float32)
    middle = tok_f + branch
    router_f = full_router.astype(jnp.float32)
    logits = jnp.dot(tok_f, router_f, precision=precise)
    onehot = (
        top_experts[:, :, None] == jnp.arange(experts, dtype=jnp.int32)[None, None, :]
    ).astype(jnp.float32)
    gate_vals = jax.nn.softmax(jnp.sum(onehot * logits[:, None, :], axis=-1), axis=-1)
    ffn_g = ffn_gain.astype(jnp.float32)
    normed_ffn = rms_scale(middle, ffn_g).astype(jnp.bfloat16)
    slot_hits = slot_table(top_experts, experts, capacity).astype(jnp.bfloat16)
    any_slot = jnp.sum(slot_hits, axis=1)
    dispatch = (
        jnp.dot(any_slot.T, normed_ffn, preferred_element_type=jnp.float32)
        .astype(jnp.bfloat16)
        .reshape(experts, capacity, D)
    )
    arrived = lax.all_to_all(dispatch, "expert", split_axis=0, concat_axis=0, tiled=True).reshape(
        experts * capacity, D
    )
    hidden = jnp.dot(arrived, gate_up[0], preferred_element_type=jnp.float32)

    def activate(hidden_in):
        return jax.nn.gelu(hidden_in[:, :FF], approximate=True) * hidden_in[:, FF:]

    mixed_hidden, act_pull = jax.vjp(activate, hidden)
    mixed_low = mixed_hidden.astype(jnp.bfloat16)
    expert_out = (
        jnp.dot(mixed_low, down_proj[0], preferred_element_type=jnp.float32)
        .astype(jnp.bfloat16)
        .reshape(experts, capacity, D)
    )
    returned = lax.all_to_all(
        expert_out, "expert", split_axis=0, concat_axis=0, tiled=True
    ).reshape(experts * capacity, D)
    picked = jnp.einsum("tkp,pd->tkd", slot_hits, returned, preferred_element_type=jnp.float32)
    combined = jnp.sum(gate_vals[:, :, None] * picked, axis=1)
    output = (middle + combined).astype(jnp.bfloat16)
    upstream = cotangent.astype(jnp.float32)
    gate_grad = jnp.sum(upstream[:, None, :] * picked, axis=-1)
    gate_mix = jnp.sum(gate_vals[:, :, None] * slot_hits.astype(jnp.float32), axis=1)
    row_grads = (
        jnp.dot(gate_mix.T, upstream, precision=precise)
        .astype(jnp.bfloat16)
        .reshape(experts, capacity, D)
    )
    arrived_grads = lax.all_to_all(
        row_grads, "expert", split_axis=0, concat_axis=0, tiled=True
    ).reshape(experts * capacity, D)
    grad_mixed = jnp.dot(arrived_grads, down_proj[0].T, preferred_element_type=jnp.float32)
    grad_down_local = jnp.dot(mixed_low.T, arrived_grads, preferred_element_type=jnp.float32)
    grad_hidden = act_pull(grad_mixed)[0].astype(jnp.bfloat16)
    grad_up_local = jnp.dot(arrived.T, grad_hidden, preferred_element_type=jnp.float32)
    grad_rows = (
        jnp.dot(grad_hidden, gate_up[0].T, preferred_element_type=jnp.float32)
        .astype(jnp.bfloat16)
        .reshape(experts, capacity, D)
    )
    back_rows = lax.all_to_all(
        grad_rows, "expert", split_axis=0, concat_axis=0, tiled=True
    ).reshape(experts * capacity, D)
    grad_normed_ffn = jnp.dot(any_slot, back_rows, preferred_element_type=jnp.float32)
    centered = gate_vals * (gate_grad - jnp.sum(gate_vals * gate_grad, axis=-1, keepdims=True))
    logit_grad = jnp.sum(centered[:, :, None] * onehot, axis=1)
    grad_router_local = jnp.dot(tok_f.T, logit_grad, precision=precise)
    grad_from_router = jnp.dot(logit_grad, router_f.T, precision=precise)
    ffn_value, ffn_pull = jax.vjp(rms_scale, middle, ffn_g)
    grad_mid_norm, grad_ffn_gain = ffn_pull(grad_normed_ffn)
    grad_middle = upstream + grad_mid_norm
    grad_branch = grad_middle.astype(jnp.bfloat16)
    back_qkv, back_out = (
        lax.all_gather(w_qkv, ("expert", "shard"), axis=0, tiled=True),
        lax.all_gather(w_out, ("expert", "shard"), axis=1, tiled=True),
    )
    grad_out_local = jnp.dot(attended.T, grad_branch, preferred_element_type=jnp.float32)
    grad_attended = (
        jnp.dot(grad_branch, back_out.T, preferred_element_type=jnp.float32)
        .astype(jnp.bfloat16)
        .reshape(tok_count, HEADS_KV, repeat, HEAD_DIM)
    )
    probs_again = jnp.exp(attn_scores() - top_score) / total_weight
    grad_probs = jnp.einsum(
        "tgrd,kgd->grtk", grad_attended, values_all, preferred_element_type=jnp.float32
    )
    grad_scores = (
        probs_again * (grad_probs - jnp.sum(probs_again * grad_probs, axis=-1, keepdims=True))
    ).astype(jnp.bfloat16)
    grad_queries = (
        jnp.einsum("grtk,kgd->tgrd", grad_scores, keys_all, preferred_element_type=jnp.float32)
        * scale
    )
    grad_keys = (
        jnp.einsum("grtk,tgrd->kgd", grad_scores, grouped, preferred_element_type=jnp.float32)
        * scale
    )
    grad_values = jnp.einsum(
        "grtk,tgrd->kgd", probs_low, grad_attended, preferred_element_type=jnp.float32
    )
    group_grads = jnp.concatenate(
        [grad_keys.reshape(group_rows, width_kv), grad_values.reshape(group_rows, width_kv)], axis=1
    )
    own_kv_grads = lax.psum_scatter(
        group_grads.astype(jnp.bfloat16), "shard", scatter_dimension=0, tiled=True
    ).astype(jnp.float32)
    grad_projected = jnp.concatenate(
        [
            unrotate(grad_queries.reshape(tok_count, HEADS_Q, HEAD_DIM), cosine, sine_tab).reshape(
                tok_count, width_q
            ),
            unrotate(
                own_kv_grads[:, :width_kv].reshape(tok_count, HEADS_KV, HEAD_DIM), cosine, sine_tab
            ).reshape(tok_count, width_kv),
            own_kv_grads[:, width_kv:],
        ],
        axis=1,
    ).astype(jnp.bfloat16)
    grad_qkv_local = jnp.dot(normed.T, grad_projected, preferred_element_type=jnp.float32)
    grad_normed = jnp.dot(grad_projected, back_qkv.T, preferred_element_type=jnp.float32)
    attn_value, attn_pull = jax.vjp(rms_scale, tok_f, attn_g)
    grad_tok_norm, grad_attn_gain = attn_pull(grad_normed)
    grad_tokens = (grad_middle + grad_tok_norm + grad_from_router).astype(jnp.bfloat16)
    summed = (
        lax.psum_scatter(grad_qkv_local, ("expert", "shard"), scatter_dimension=0, tiled=True),
        lax.psum_scatter(grad_out_local, ("expert", "shard"), scatter_dimension=1, tiled=True),
        lax.psum_scatter(grad_attn_gain, ("expert", "shard"), scatter_dimension=0, tiled=True),
        lax.psum_scatter(grad_ffn_gain, ("expert", "shard"), scatter_dimension=0, tiled=True),
        lax.psum_scatter(grad_router_local, ("expert", "shard"), scatter_dimension=0, tiled=True),
    )
    expert_sums = (
        lax.psum_scatter(
            grad_up_local[None].astype(jnp.bfloat16), "shard", scatter_dimension=1, tiled=True
        ).astype(jnp.float32),
        lax.psum_scatter(
            grad_down_local[None].astype(jnp.bfloat16), "shard", scatter_dimension=2, tiled=True
        ).astype(jnp.float32),
    )
    return (
        output,
        grad_tokens,
        summed[0],
        summed[1],
        summed[2],
        summed[3],
        summed[4],
        expert_sums[0],
        expert_sums[1],
    )


def solution(mesh):
    return jax.shard_map(
        body,
        mesh=mesh,
        in_specs=(
            P(("expert", "shard"), None),
            P("expert", None),
            P(("expert", "shard"), None),
            P(("expert", "shard"), None),
            P(None, ("expert", "shard")),
            P(("expert", "shard")),
            P(("expert", "shard")),
            P(("expert", "shard"), None),
            P("expert", None, None),
            P("expert", None, None),
            P(("expert", "shard"), None),
        ),
        out_specs=(
            P(("expert", "shard"), None),
            P(("expert", "shard"), None),
            P(("expert", "shard"), None),
            P(None, ("expert", "shard")),
            P(("expert", "shard")),
            P(("expert", "shard")),
            P(("expert", "shard"), None),
            P("expert", "shard", None),
            P("expert", None, "shard"),
        ),
        check_vma=False,
    )
```

profile of v0, /device:TPU:0, one launch (start us, length us, event | category | flops | bytes accessed | tf_op | source)
XLA Modules:
  0.0 1516.0 jit_solution(18202060495527208420)
XLA Ops:
  13.3 69.3 %all-reduce.12 = (bf16[1536]{0:T(1024)(128)(2,1)S(1)}, bf16[1536]{0:T(1024)(128)(2,1)}) all-reduce(bf16[1536]{0:T(1024)(128)(2,1)S(1)} %dynamic-update-slice, bf16[1536]{0:T(1024)(128)(2,1)S(1)} %dynamic-update-slice.1), channel_id=1, replica_groups=mesh['expert'=32,'shard'=4] {'expert','shard'}, use_global_device_ids=true, to_apply=%add.2 | all-reduce | flops 3072 | bytes 12288
  84.1 10.8 reshape.380
  94.9 4.7 fusion.69
  106.6 9.0 reduce-window.19
  119.8 33.2 %all-gather.11.cloned.1.call-done = bf16[128,12,1536]{2,1,0:T(8,128)(2,1)} async-done(((bf16[1,12,1536]{2,1,0:T(8,128)(2,1)}), bf16[128,12,1536]{2,1,0:T(8,128)(2,1)}) %all-gather.11.cloned.1.call-update) | async-done | bytes 4718608 | tf_op jit(solution)/shard_map/all_gather | solution.py:93
  152.9 8.2 reshape.382
  184.6 10.7 fusion.90
  195.3 5.9 fusion.46
  201.3 4.2 multiply_reduce_fusion.5
  207.6 63.4 %all_to_all.20 = bf16[32,48,1536]{2,1,0:T(8,128)(2,1)S(1)} all-to-all(bf16[32,48,1536]{2,1,0:T(8,128)(2,1)S(1)} %bitcast.162), channel_id=1, replica_groups=mesh['expert'=32,'shard'=4] {'expert'}, dimensions={0} | all-to-all | bytes 9437184 | tf_op jit(solution)/shard_map/all_to_all | solution.py:162
  271.0 7.5 fusion.22
  282.1 5.5 convolution_convert_fusion.1
  287.6 5.0 all-to-all-start.1
  292.7 109.5 %all-gather.2 = bf16[128,12,32]{2,1,0:T(8,128)(2,1)} all-gather(bf16[1,12,32]{2,1,0:T(8,128)(2,1)S(1)} %bitcast.205), channel_id=1, replica_groups=mesh['expert'=32,'shard'=4] {'expert','shard'}, dimensions={0}, use_global_device_ids=true | all-gather | bytes 99072 | tf_op jit(solution)/shard_map/all_gather | solution.py:96
  409.3 10.4 multiply_reduce_fusion
  419.8 4.1 convolution_convert_fusion
  423.9 63.6 %all_to_all.21 = bf16[32,48,1536]{2,1,0:T(8,128)(2,1)S(1)} all-to-all(bf16[32,48,1536]{2,1,0:T(8,128)(2,1)S(1)} %bitcast.163), channel_id=1, replica_groups=mesh['expert'=32,'shard'=4] {'expert'}, dimensions={0} | all-to-all | bytes 9437184 | tf_op jit(solution)/shard_map/all_to_all | solution.py:191
  487.6 8.8 fusion.37
  496.4 10.1 convolution_convert_fusion.4
  506.5 60.4 %all_to_all.22 = bf16[32,48,1536]{2,1,0:T(8,128)(2,1)S(1)} all-to-all(bf16[32,48,1536]{2,1,0:T(8,128)(2,1)S(1)} %bitcast.178), channel_id=1, replica_groups=mesh['expert'=32,'shard'=4] {'expert'}, dimensions={0} | all-to-all | bytes 9437184 | tf_op jit(solution)/shard_map/all_to_all | solution.py:203
  574.2 10.2 fusion.3
  584.4 7.1 fusion.53
  591.6 6.6 fusion.5
  607.0 8.4 fusion.30
  615.5 12.5 copy.147
  628.0 4.1 copy.163
  632.2 13.6 fusion.7
  646.8 3.9 convolution_multiply_fusion
  650.7 5.0 fusion.65
  666.0 7.5 fusion.63
  673.5 434.3 %fusion.86 = (f32[16,2048]{1,0:T(8,128)}, f32[1536,16]{0,1:T(8,128)}) fusion(f32[1536,2048]{1,0:T(8,128)} %fusion.63, f32[1536,1536]{0,1:T(8,128)} %fusion.65), kind=kCustom, calls=%all-reduce-scatter.2 | all-reduce-scatter fusion | flops 7340033 | bytes 22249472
  1121.3 9.0 collective-permute-start.40
  1130.4 7.1 collective-permute-start.41
  1143.0 11.9 collective-permute-start.45
  1158.4 8.8 collective-permute-start.47
  1176.6 6.2 collective-permute-start.53
  1198.6 3.8 collective-permute-start.60
  1205.9 6.7 collective-permute-start.62
  1223.1 6.8 collective-permute-start.13
  1235.1 4.9 collective-permute-start.15
  1251.0 4.5 copy.148
  1267.1 4.6 collective-permute-start.22
  1271.7 5.7 fusion.39
  1286.1 8.9 collective-permute-start.28
  1309.1 65.6 %all-reduce.11 = (f32[1536]{0:T(1024)S(1)}, f32[1536]{0:T(1024)S(1)}) all-reduce(f32[1536]{0:T(1024)S(1)} %copy-done.91, f32[1536]{0:T(1024)S(1)} %copy-done.90), channel_id=5, replica_groups=mesh['expert'=32,'shard'=4] {'expert','shard'}, use_global_device_ids=true, to_apply=%region_26.27.clone | all-reduce | flops 3072 | bytes 24576
  1375.9 53.5 %concatenate.42 = f32[1536,524]{0,1:T(8,128)} concatenate(f32[1536,12]{0,1:T(8,128)} %copy-done.48, f32[1536,16]{0,1:T(8,128)} %copy-done.76, f32[1536,16]{0,1:T(8,128)} %copy-done.75, f32[1536,16]{0,1:T(8,128)} %copy-done.74, f32[1536,16]{0,1:T(8,128)} %copy-done.73, f32[1536,16]{0,1:T(8,128)} %copy-done.72, f32[1536,16]{0,1:T(8,128)} %copy-done.71, f32[1536,16]{0,1:T(8,128)} %copy-done.70, ...), dimensions={1} | concatenate | bytes 6438912
  1441.3 6.4 collective-permute-start.9
  1449.8 54.5 %concatenate.41 = f32[524,2048]{1,0:T(8,128)} concatenate(f32[12,2048]{1,0:T(8,128)} %collective-permute-done.31, f32[16,2048]{1,0:T(8,128)} %collective-permute-done.30, f32[16,2048]{1,0:T(8,128)} %collective-permute-done.29, f32[16,2048]{1,0:T(8,128)} %collective-permute-done.28, f32[16,2048]{1,0:T(8,128)} %copy-done.42, f32[16,2048]{1,0:T(8,128)} %copy-done.41, ...), dimensions={0} | concatenate | bytes 8585216
  (449 shorter events, 213.0 us)
Async XLA Ops:
  7.2 76.9 %all-gather.9.cloned.1.call-start = ((), (), s32[]{:S(2)}) async-start(), calls=%async_computation.10 | async-start | bytes 8454144 | tf_op jit(solution)/shard_map/all_gather | solution.py:92
  7.9 145.0 %all-gather.11.cloned.1.call-start = ((), (), s32[]{:S(2)}) async-start(), calls=%async_computation.11 | async-start | bytes 6340608 | tf_op jit(solution)/shard_map/all_gather | solution.py:93
  8.7 167.5 %all-gather.7.cloned.1.call-start = ((), (), s32[]{:S(2)}) async-start(), calls=%async_computation.7 | async-start | bytes 1310720 | tf_op jit(solution)/shard_map/all_gather | solution.py:120
  287.6 121.7 %all-to-all-start.1 = ((bf16[32,48,1536]{2,1,0:T(8,128)(2,1)}), bf16[32,48,1536]{2,1,0:T(8,128)(2,1)}, u32[]{:S(2)}, u32[]{:S(2)}) async-start(bf16[32,48,1536]{2,1,0:T(8,128)(2,1)} %bitcast.176), calls=%async_computation.1 | async-start | bytes 9437184 | tf_op jit(solution)/shard_map/all_to_all | solution.py:177
  292.6 363.5 %reduce-scatter.11.cloned.1.call-start = ((), (), s32[]{:S(2)}) async-start(), calls=%async_computation.8 | async-start | bytes 1310720 | tf_op jit(solution)/shard_map/reduce_scatter | solution.py:246
  604.4 625.7 %all-reduce.16.cloned.1.call-start = ((), (), s32[]{:S(2)}) async-start(), calls=%async_computation.13 | async-start | bytes 393216
  607.0 641.4 %reduce-scatter.15.cloned.1.call-start = ((), (), s32[]{:S(2)}) async-start(), calls=%async_computation.12 | async-start | bytes 2949120
  632.1 873.9 %reduce-scatter.13.cloned.1.call-start = ((), (), s32[]{:S(2)}) async-start(), calls=%async_computation.9 | async-start | bytes 5898240 | tf_op jit(solution)/shard_map/reduce_scatter | solution.py:274
  1117.4 20.1 %collective-permute-start.37 = (f32[1536,16]{0,1:T(8,128)}, f32[1536,16]{0,1:T(8,128)S(1)}, u32[]{:S(2)}, u32[]{:S(2)}) collective-permute-start(f32[1536,16]{0,1:T(8,128)} %get-tuple-element.61), channel_id=1, source_target_pairs={{0,6},{1,7},{2,8},{3,9},{4,10},{5,11},{6,12},{7,13},{8,14},{9,15},... | collective-permute-start | bytes 294920
  1118.7 21.7 %collective-permute-start.38 = (f32[1536,16]{0,1:T(8,128)}, f32[1536,16]{0,1:T(8,128)S(1)}, u32[]{:S(2)}, u32[]{:S(2)}) collective-permute-start(f32[1536,16]{0,1:T(8,128)} %get-tuple-element.61), channel_id=1, source_target_pairs={{0,7},{1,8},{2,9},{3,10},{4,11},{5,12},{6,13},{7,14},{8,15},{9,16}... | collective-permute-start | bytes 294920
  1120.0 21.7 %collective-permute-start.39 = (f32[1536,16]{0,1:T(8,128)}, f32[1536,16]{0,1:T(8,128)S(1)}, u32[]{:S(2)}, u32[]{:S(2)}) collective-permute-start(f32[1536,16]{0,1:T(8,128)} %get-tuple-element.61), channel_id=1, source_target_pairs={{0,8},{1,9},{2,10},{3,11},{4,12},{5,13},{6,14},{7,15},{8,16},{9,17... | collective-permute-start | bytes 294920
  1121.3 21.7 %collective-permute-start.40 = (f32[1536,16]{0,1:T(8,128)}, f32[1536,16]{0,1:T(8,128)S(1)}, u32[]{:S(2)}, u32[]{:S(2)}) collective-permute-start(f32[1536,16]{0,1:T(8,128)} %get-tuple-element.61), channel_id=1, source_target_pairs={{0,9},{1,10},{2,11},{3,12},{4,13},{5,14},{6,15},{7,16},{8,17},{9,1... | collective-permute-start | bytes 294920
  1130.4 24.5 %collective-permute-start.41 = (f32[1536,16]{0,1:T(8,128)}, f32[1536,16]{0,1:T(8,128)S(1)}, u32[]{:S(2)}, u32[]{:S(2)}) collective-permute-start(f32[1536,16]{0,1:T(8,128)} %get-tuple-element.61), channel_id=1, source_target_pairs={{0,10},{1,11},{2,12},{3,13},{4,14},{5,15},{6,16},{7,17},{8,18},{9,... | collective-permute-start | bytes 294920
  1137.5 20.8 %collective-permute-start.42 = (f32[1536,16]{0,1:T(8,128)}, f32[1536,16]{0,1:T(8,128)S(1)}, u32[]{:S(2)}, u32[]{:S(2)}) collective-permute-start(f32[1536,16]{0,1:T(8,128)} %get-tuple-element.61), channel_id=1, source_target_pairs={{0,11},{1,12},{2,13},{3,14},{4,15},{5,16},{6,17},{7,18},{8,19},{9,... | collective-permute-start | bytes 294920
  1140.4 26.8 %collective-permute-start.43 = (f32[1536,16]{0,1:T(8,128)}, f32[1536,16]{0,1:T(8,128)S(1)}, u32[]{:S(2)}, u32[]{:S(2)}) collective-permute-start(f32[1536,16]{0,1:T(8,128)} %get-tuple-element.61), channel_id=1, source_target_pairs={{0,12},{1,13},{2,14},{3,15},{4,16},{5,17},{6,18},{7,19},{8,20},{9,... | collective-permute-start | bytes 294920
  1141.7 26.8 %collective-permute-start.44 = (f32[1536,16]{0,1:T(8,128)}, f32[1536,16]{0,1:T(8,128)S(1)}, u32[]{:S(2)}, u32[]{:S(2)}) collective-permute-start(f32[1536,16]{0,1:T(8,128)} %get-tuple-element.61), channel_id=1, source_target_pairs={{0,13},{1,14},{2,15},{3,16},{4,17},{5,18},{6,19},{7,20},{8,21},{9,... | collective-permute-start | bytes 294920
  1143.0 28.1 %collective-permute-start.45 = (f32[1536,16]{0,1:T(8,128)}, f32[1536,16]{0,1:T(8,128)S(1)}, u32[]{:S(2)}, u32[]{:S(2)}) collective-permute-start(f32[1536,16]{0,1:T(8,128)} %get-tuple-element.61), channel_id=1, source_target_pairs={{0,14},{1,15},{2,16},{3,17},{4,18},{5,19},{6,20},{7,21},{8,22},{9,... | collective-permute-start | bytes 294920
  1154.9 19.0 %collective-permute-start.46 = (f32[1536,16]{0,1:T(8,128)}, f32[1536,16]{0,1:T(8,128)S(1)}, u32[]{:S(2)}, u32[]{:S(2)}) collective-permute-start(f32[1536,16]{0,1:T(8,128)} %get-tuple-element.61), channel_id=1, source_target_pairs={{0,15},{1,16},{2,17},{3,18},{4,19},{5,20},{6,21},{7,22},{8,23},{9,... | collective-permute-start | bytes 294920
  1158.4 16.9 %collective-permute-start.47 = (f32[1536,16]{0,1:T(8,128)}, f32[1536,16]{0,1:T(8,128)S(1)}, u32[]{:S(2)}, u32[]{:S(2)}) collective-permute-start(f32[1536,16]{0,1:T(8,128)} %get-tuple-element.61), channel_id=1, source_target_pairs={{0,16},{1,17},{2,18},{3,19},{4,20},{5,21},{6,22},{7,23},{8,24},{9,... | collective-permute-start | bytes 294920
  1192.8 19.8 %collective-permute-start.59 = (f32[1536,16]{0,1:T(8,128)}, f32[1536,16]{0,1:T(8,128)S(1)}, u32[]{:S(2)}, u32[]{:S(2)}) collective-permute-start(f32[1536,16]{0,1:T(8,128)} %get-tuple-element.61), channel_id=1, source_target_pairs={{0,28},{1,29},{2,30},{3,31},{4,32},{5,33},{6,34},{7,35},{8,36},{9,... | collective-permute-start | bytes 294920
  1194.9 28.2 %collective-permute-start = (f32[16,2048]{1,0:T(8,128)}, f32[16,2048]{1,0:T(8,128)}, u32[]{:S(2)}, u32[]{:S(2)}) collective-permute-start(f32[16,2048]{1,0:T(8,128)} %get-tuple-element.60), channel_id=1, source_target_pairs={{0,1},{1,2},{2,3},{3,4},{4,5},{5,6},{6,7},{7,8},{8,9},{9,10},{10,1... | collective-permute-start | bytes 393224
  1198.6 15.9 %collective-permute-start.60 = (f32[1536,16]{0,1:T(8,128)}, f32[1536,16]{0,1:T(8,128)S(1)}, u32[]{:S(2)}, u32[]{:S(2)}) collective-permute-start(f32[1536,16]{0,1:T(8,128)} %get-tuple-element.61), channel_id=1, source_target_pairs={{0,29},{1,30},{2,31},{3,32},{4,33},{5,34},{6,35},{7,36},{8,37},{9,... | collective-permute-start | bytes 294920
  1214.6 18.3 %collective-permute-start.1 = (f32[16,2048]{1,0:T(8,128)}, f32[16,2048]{1,0:T(8,128)}, u32[]{:S(2)}, u32[]{:S(2)}) collective-permute-start(f32[16,2048]{1,0:T(8,128)} %get-tuple-element.60), channel_id=1, source_target_pairs={{0,2},{1,3},{2,4},{3,5},{4,6},{5,7},{6,8},{7,9},{8,10},{9,11},{10,... | collective-permute-start | bytes 393224
  1217.3 17.8 %collective-permute-start.10 = (f32[16,2048]{1,0:T(8,128)}, f32[16,2048]{1,0:T(8,128)}, u32[]{:S(2)}, u32[]{:S(2)}) collective-permute-start(f32[16,2048]{1,0:T(8,128)} %get-tuple-element.60), channel_id=1, source_target_pairs={{0,11},{1,12},{2,13},{3,14},{4,15},{5,16},{6,17},{7,18},{8,19},{9,... | collective-permute-start | bytes 393224
  1219.3 20.8 %collective-permute-start.11 = (f32[16,2048]{1,0:T(8,128)}, f32[16,2048]{1,0:T(8,128)}, u32[]{:S(2)}, u32[]{:S(2)}) collective-permute-start(f32[16,2048]{1,0:T(8,128)} %get-tuple-element.60), channel_id=1, source_target_pairs={{0,12},{1,13},{2,14},{3,15},{4,16},{5,17},{6,18},{7,19},{8,20},{9,... | collective-permute-start | bytes 393224
  1221.2 20.9 %collective-permute-start.12 = (f32[16,2048]{1,0:T(8,128)}, f32[16,2048]{1,0:T(8,128)}, u32[]{:S(2)}, u32[]{:S(2)}) collective-permute-start(f32[16,2048]{1,0:T(8,128)} %get-tuple-element.60), channel_id=1, source_target_pairs={{0,13},{1,14},{2,15},{3,16},{4,17},{5,18},{6,19},{7,20},{8,21},{9,... | collective-permute-start | bytes 393224
  1223.1 22.5 %collective-permute-start.13 = (f32[16,2048]{1,0:T(8,128)}, f32[16,2048]{1,0:T(8,128)}, u32[]{:S(2)}, u32[]{:S(2)}) collective-permute-start(f32[16,2048]{1,0:T(8,128)} %get-tuple-element.60), channel_id=1, source_target_pairs={{0,14},{1,15},{2,16},{3,17},{4,18},{5,19},{6,20},{7,21},{8,22},{9,... | collective-permute-start | bytes 393224
  1232.9 24.8 %collective-permute-start.14 = (f32[16,2048]{1,0:T(8,128)}, f32[16,2048]{1,0:T(8,128)}, u32[]{:S(2)}, u32[]{:S(2)}) collective-permute-start(f32[16,2048]{1,0:T(8,128)} %get-tuple-element.60), channel_id=1, source_target_pairs={{0,15},{1,16},{2,17},{3,18},{4,19},{5,20},{6,21},{7,22},{8,23},{9,... | collective-permute-start | bytes 393224
  1235.1 24.1 %collective-permute-start.15 = (f32[16,2048]{1,0:T(8,128)}, f32[16,2048]{1,0:T(8,128)}, u32[]{:S(2)}, u32[]{:S(2)}) collective-permute-start(f32[16,2048]{1,0:T(8,128)} %get-tuple-element.60), channel_id=1, source_target_pairs={{0,16},{1,17},{2,18},{3,19},{4,20},{5,21},{6,22},{7,23},{8,24},{9,... | collective-permute-start | bytes 393224
  1240.1 21.6 %collective-permute-start.16 = (f32[16,2048]{1,0:T(8,128)}, f32[16,2048]{1,0:T(8,128)}, u32[]{:S(2)}, u32[]{:S(2)}) collective-permute-start(f32[16,2048]{1,0:T(8,128)} %get-tuple-element.60), channel_id=1, source_target_pairs={{0,17},{1,18},{2,19},{3,20},{4,21},{5,22},{6,23},{7,24},{8,25},{9,... | collective-permute-start | bytes 393224
  1242.1 22.2 %collective-permute-start.17 = (f32[16,2048]{1,0:T(8,128)}, f32[16,2048]{1,0:T(8,128)}, u32[]{:S(2)}, u32[]{:S(2)}) collective-permute-start(f32[16,2048]{1,0:T(8,128)} %get-tuple-element.60), channel_id=1, source_target_pairs={{0,18},{1,19},{2,20},{3,21},{4,22},{5,23},{6,24},{7,25},{8,26},{9,... | collective-permute-start | bytes 393224
  1245.7 21.4 %collective-permute-start.18 = (f32[16,2048]{1,0:T(8,128)}, f32[16,2048]{1,0:T(8,128)}, u32[]{:S(2)}, u32[]{:S(2)}) collective-permute-start(f32[16,2048]{1,0:T(8,128)} %get-tuple-element.60), channel_id=1, source_target_pairs={{0,19},{1,20},{2,21},{3,22},{4,23},{5,24},{6,25},{7,26},{8,27},{9,... | collective-permute-start | bytes 393224
  1257.7 19.7 %collective-permute-start.19 = (f32[16,2048]{1,0:T(8,128)}, f32[16,2048]{1,0:T(8,128)S(1)}, u32[]{:S(2)}, u32[]{:S(2)}) collective-permute-start(f32[16,2048]{1,0:T(8,128)} %get-tuple-element.60), channel_id=1, source_target_pairs={{0,20},{1,21},{2,22},{3,23},{4,24},{5,25},{6,26},{7,27},{8,28},{9,... | collective-permute-start | bytes 393224
  1259.3 19.6 %collective-permute-start.2 = (f32[16,2048]{1,0:T(8,128)}, f32[16,2048]{1,0:T(8,128)S(1)}, u32[]{:S(2)}, u32[]{:S(2)}) collective-permute-start(f32[16,2048]{1,0:T(8,128)} %get-tuple-element.60), channel_id=1, source_target_pairs={{0,3},{1,4},{2,5},{3,6},{4,7},{5,8},{6,9},{7,10},{8,11},{9,12},{10... | collective-permute-start | bytes 393224
  1261.7 18.5 %collective-permute-start.20 = (f32[16,2048]{1,0:T(8,128)}, f32[16,2048]{1,0:T(8,128)S(1)}, u32[]{:S(2)}, u32[]{:S(2)}) collective-permute-start(f32[16,2048]{1,0:T(8,128)} %get-tuple-element.60), channel_id=1, source_target_pairs={{0,21},{1,22},{2,23},{3,24},{4,25},{5,26},{6,27},{7,28},{8,29},{9,... | collective-permute-start | bytes 393224
  1264.3 18.8 %collective-permute-start.21 = (f32[16,2048]{1,0:T(8,128)}, f32[16,2048]{1,0:T(8,128)S(1)}, u32[]{:S(2)}, u32[]{:S(2)}) collective-permute-start(f32[16,2048]{1,0:T(8,128)} %get-tuple-element.60), channel_id=1, source_target_pairs={{0,22},{1,23},{2,24},{3,25},{4,26},{5,27},{6,28},{7,29},{8,30},{9,... | collective-permute-start | bytes 393224
  1267.1 17.6 %collective-permute-start.22 = (f32[16,2048]{1,0:T(8,128)}, f32[16,2048]{1,0:T(8,128)S(1)}, u32[]{:S(2)}, u32[]{:S(2)}) collective-permute-start(f32[16,2048]{1,0:T(8,128)} %get-tuple-element.60), channel_id=1, source_target_pairs={{0,23},{1,24},{2,25},{3,26},{4,27},{5,28},{6,29},{7,30},{8,31},{9,... | collective-permute-start | bytes 393224
  1278.9 16.1 %collective-permute-start.24 = (f32[16,2048]{1,0:T(8,128)}, f32[16,2048]{1,0:T(8,128)S(1)}, u32[]{:S(2)}, u32[]{:S(2)}) collective-permute-start(f32[16,2048]{1,0:T(8,128)} %get-tuple-element.60), channel_id=1, source_target_pairs={{0,25},{1,26},{2,27},{3,28},{4,29},{5,30},{6,31},{7,32},{8,33},{9,... | collective-permute-start | bytes 393224
  1280.2 17.5 %collective-permute-start.25 = (f32[16,2048]{1,0:T(8,128)}, f32[16,2048]{1,0:T(8,128)S(1)}, u32[]{:S(2)}, u32[]{:S(2)}) collective-permute-start(f32[16,2048]{1,0:T(8,128)} %get-tuple-element.60), channel_id=1, source_target_pairs={{0,26},{1,27},{2,28},{3,29},{4,30},{5,31},{6,32},{7,33},{8,34},{9,... | collective-permute-start | bytes 393224
  1283.1 18.1 %collective-permute-start.26 = (f32[16,2048]{1,0:T(8,128)}, f32[16,2048]{1,0:T(8,128)S(1)}, u32[]{:S(2)}, u32[]{:S(2)}) collective-permute-start(f32[16,2048]{1,0:T(8,128)} %get-tuple-element.60), channel_id=1, source_target_pairs={{0,27},{1,28},{2,29},{3,30},{4,31},{5,32},{6,33},{7,34},{8,35},{9,... | collective-permute-start | bytes 393224
  1284.7 20.2 %collective-permute-start.27 = (f32[16,2048]{1,0:T(8,128)}, f32[16,2048]{1,0:T(8,128)S(1)}, u32[]{:S(2)}, u32[]{:S(2)}) collective-permute-start(f32[16,2048]{1,0:T(8,128)} %get-tuple-element.60), channel_id=1, source_target_pairs={{0,28},{1,29},{2,30},{3,31},{4,32},{5,33},{6,34},{7,35},{8,36},{9,... | collective-permute-start | bytes 393224
  1286.1 143.3 %collective-permute-start.28 = (f32[16,2048]{1,0:T(8,128)}, f32[16,2048]{1,0:T(8,128)}, u32[]{:S(2)}, u32[]{:S(2)}) collective-permute-start(f32[16,2048]{1,0:T(8,128)} %get-tuple-element.60), channel_id=1, source_target_pairs={{0,29},{1,30},{2,31},{3,32},{4,33},{5,34},{6,35},{7,36},{8,37},{9,... | collective-permute-start | bytes 393224
  1295.0 137.3 %collective-permute-start.29 = (f32[16,2048]{1,0:T(8,128)}, f32[16,2048]{1,0:T(8,128)}, u32[]{:S(2)}, u32[]{:S(2)}) collective-permute-start(f32[16,2048]{1,0:T(8,128)} %get-tuple-element.60), channel_id=1, source_target_pairs={{0,30},{1,31},{2,32},{3,33},{4,34},{5,35},{6,36},{7,37},{8,38},{9,... | collective-permute-start | bytes 393224
  1297.7 137.5 %collective-permute-start.3 = (f32[16,2048]{1,0:T(8,128)}, f32[16,2048]{1,0:T(8,128)}, u32[]{:S(2)}, u32[]{:S(2)}) collective-permute-start(f32[16,2048]{1,0:T(8,128)} %get-tuple-element.60), channel_id=1, source_target_pairs={{0,4},{1,5},{2,6},{3,7},{4,8},{5,9},{6,10},{7,11},{8,12},{9,13},{1... | collective-permute-start | bytes 393224
  1301.2 136.4 %collective-permute-start.30 = (f32[16,2048]{1,0:T(8,128)}, f32[16,2048]{1,0:T(8,128)}, u32[]{:S(2)}, u32[]{:S(2)}) collective-permute-start(f32[16,2048]{1,0:T(8,128)} %get-tuple-element.60), channel_id=1, source_target_pairs={{0,31},{1,32},{2,33},{3,34},{4,35},{5,36},{6,37},{7,38},{8,39},{9,... | collective-permute-start | bytes 393224
  1304.9 136.3 %collective-permute-start.4 = (f32[16,2048]{1,0:T(8,128)}, f32[16,2048]{1,0:T(8,128)}, u32[]{:S(2)}, u32[]{:S(2)}) collective-permute-start(f32[16,2048]{1,0:T(8,128)} %get-tuple-element.60), channel_id=1, source_target_pairs={{0,5},{1,6},{2,7},{3,8},{4,9},{5,10},{6,11},{7,12},{8,13},{9,14},{... | collective-permute-start | bytes 393224
  1429.4 20.0 %collective-permute-start.5 = (f32[16,2048]{1,0:T(8,128)}, f32[16,2048]{1,0:T(8,128)S(1)}, u32[]{:S(2)}, u32[]{:S(2)}) collective-permute-start(f32[16,2048]{1,0:T(8,128)} %get-tuple-element.60), channel_id=1, source_target_pairs={{0,6},{1,7},{2,8},{3,9},{4,10},{5,11},{6,12},{7,13},{8,14},{9,15},... | collective-permute-start | bytes 393224
  1432.3 17.1 %collective-permute-start.6 = (f32[16,2048]{1,0:T(8,128)}, f32[16,2048]{1,0:T(8,128)S(1)}, u32[]{:S(2)}, u32[]{:S(2)}) collective-permute-start(f32[16,2048]{1,0:T(8,128)} %get-tuple-element.60), channel_id=1, source_target_pairs={{0,7},{1,8},{2,9},{3,10},{4,11},{5,12},{6,13},{7,14},{8,15},{9,16}... | collective-permute-start | bytes 393224
  (131 other events, 4617.6 us)
Sparse Core Ops, SparseCore 0:
  11.2 72.4 all-gather.8
  86.7 66.1 all-gather.10
  154.6 21.5 all-gather.6
  604.5 20.1 reduce-scatter.10
  629.9 143.4 all-reduce.15
  776.2 48.5 reduce-scatter.14
  827.2 88.0 reduce-scatter.12
where the time goes:
time: 1530 us; the launch traced here: 1520 us
  blocking collectives  866 us (57%)
  local copies, waits for them, and re-layouts  201 us (13%)
  starting transfers between devices  200 us (13%)
  matrix products  145 us (9%)
  other arithmetic  46.7 us (3%)
  waiting for transfers between devices  39.8 us (3%)
  between operations  16.5 us (1%)
    unnamed x3, blocking collectives  569 us
    unnamed x66, starting transfers between devices  195 us
    unnamed x239, local copies, waits for them, and re-layouts  174 us
    all_gather x1, blocking collectives, body(): lax.all_gather(router, ('expert', 'shard'), axis=0, tiled=True)  109 us
    all_to_all x1, blocking collectives, body(): lax.all_to_all(row_grads, 'expert', split_axis=0, concat_axis=0, tiled=True)  63.6 us
    all_to_all x1, blocking collectives, body(): lax.all_to_all(dispatch, 'expert', split_axis=0, concat_axis=0, tiled=True)  63.4 us
    all_to_all x1, blocking collectives, body(): lax.all_to_all(grad_rows, 'expert', split_axis=0, concat_axis=0, tiled=True)  60.4 us
    all_gather x1, waiting for transfers between devices, body(): lax.all_gather(w_out, ('expert', 'shard'), axis=1, tiled=True)  33.2 us
  transfers between devices with their start and end apart: 72, of which 4 were waited for; matrix products, arithmetic and copies ran while one was open for 46% of the time, Pallas kernels for 0%

commit v1 on v0

v1 whole, which is shorter than its diff:
```python
import functools

import jax
import jax.numpy as jnp
from jax import lax
from jax.experimental import pallas as pl
from jax.experimental.pallas import tpu as pltpu
from jax.sharding import PartitionSpec as P

D = 1536
HEADS_Q = 12
HEADS_KV = 2
HEAD_DIM = 128
FF = 768
TOP = 4
EXPERTS = 32
CAP = 48
WIDTH_Q = HEADS_Q * HEAD_DIM
WIDTH_KV = HEADS_KV * HEAD_DIM
REPEAT = HEADS_Q // HEADS_KV

norm_eps = 1e-06
rope_base = 1000000.0
precise = lax.Precision.HIGHEST
MESH = pl.DeviceIdType.MESH
F32 = jnp.float32
BF16 = jnp.bfloat16

PIECE = 12
PADDED = 16
BLOCK = 48
WA = 2048
WB = 1664
SMALL = WB - D


def place():
    e = lax.axis_index("expert")
    return e // 8, (e // 2) % 4, e % 2, lax.axis_index("shard")


def device(y, z, c, x):
    return ((y * 4 + z) * 2 + c, x)


def greet(devices):
    barrier = pltpu.get_barrier_semaphore()
    for d in devices:
        pl.semaphore_signal(barrier, inc=1, device_id=d, device_id_type=MESH)
    pl.semaphore_wait(barrier, len(devices))


class Links:
    def __init__(self, send, recv):
        self.send, self.recv, self.made = send, recv, []

    def push(self, src, dst, where):
        i = len(self.made)
        copy = pltpu.make_async_remote_copy(
            src_ref=src,
            dst_ref=dst,
            send_sem=self.send.at[i],
            recv_sem=self.recv.at[i],
            device_id=where,
            device_id_type=MESH,
        )
        copy.start()
        self.made.append(copy)
        return copy

    def drain(self):
        for copy in self.made:
            copy.wait_send()


def neighbours(y, z, c, x):
    other = 1 - c
    return dict(
        x=[device(y, z, c, (x + d) % 4) for d in (1, 2, 3)],
        y=(device((y + 1) % 4, z, c, x), device((y + 3) % 4, z, c, x)),
        z=(device(y, (z + 1) % 4, c, x), device(y, (z + 3) % 4, c, x)),
        core=device(y, z, other, x),
    )


def everyone_near(near):
    return list(near["x"]) + list(near["y"]) + list(near["z"]) + [near["core"]]


def pick_rows(rows, columns, row_block, column_block):
    r = lax.broadcasted_iota(jnp.int32, (rows, columns), 0)
    q = lax.broadcasted_iota(jnp.int32, (rows, columns), 1)
    same = (r // row_block == q // column_block) & (r % row_block == q % column_block)
    return jnp.where(same, 1.0, 0.0).astype(BF16)


def gather_kernel(pack, full_a, full_b, xbuf, own_a, own_b, send, recv, local):
    y, z, c, x = place()
    near = neighbours(y, z, c, x)
    greet(everyone_near(near))
    link = Links(send, recv)
    first = [link.push(pack, xbuf.at[x], near["x"][d]) for d in range(3)]
    xbuf[pl.ds(x, 1)] = pack[...][None]
    for copy in first:
        copy.wait_recv()
    select = pick_rows(BLOCK, 4 * PADDED, PIECE, PADDED)
    pieces = xbuf[...].reshape(4 * PADDED, WA + WB)
    own_a[...] = jnp.dot(select, pieces[:, :WA], preferred_element_type=F32).astype(BF16)
    own_b[...] = jnp.dot(select, pieces[:, WA:], preferred_element_type=F32).astype(BF16)

    def at_a(far, close, columns=None):
        view = full_a.at[far, close, c]
        return view if columns is None else view.at[:, columns]

    def at_b(far, close, columns=None):
        view = full_b.at[close, far, c]
        return view if columns is None else view.at[:, columns]

    def line_a(far, part=slice(None)):
        return full_a.at[far, part, c]

    def line_b(far, part=slice(None)):
        return full_b.at[part, far, c]

    jobs = [
        dict(own=own_a, at=at_a, line=line_a, close="z", far="y", p=z, q=y, half=1024, i=0),
        dict(own=own_b, at=at_b, line=line_b, close="y", far="z", p=y, q=z, half=896, i=1),
    ]
    for j in jobs:
        here = j["at"](j["q"], j["p"])
        plus, minus = near[j["close"]]
        j["up"] = link.push(j["own"], here, plus)
        j["down"] = link.push(j["own"], here, minus)
        j["core"] = [link.push(j["own"], here, near["core"])]
        j["local"] = pltpu.make_async_copy(j["own"], here, local.at[j["i"]])
        j["local"].start()
    for j in jobs:
        plus, minus = near[j["close"]]
        left, right = (j["p"] + 3) % 4, (j["p"] + 1) % 4
        j["up"].wait_recv()
        part = j["at"](j["q"], left, pl.ds(0, j["half"]))
        j["up2"] = link.push(part, part, plus)
        j["down"].wait_recv()
        part = j["at"](j["q"], right, pl.ds(j["half"], j["own"].shape[1] - j["half"]))
        j["down2"] = link.push(part, part, minus)
        for side in (left, right):
            block = j["at"](j["q"], side)
            j["core"].append(link.push(block, block, near["core"]))
    for j in jobs:
        j["up2"].wait_recv()
        j["down2"].wait_recv()
        block = j["at"](j["q"], (j["p"] + 2) % 4)
        j["local"].wait()
        plus, minus = near[j["far"]]
        line = j["line"](j["q"])
        j["up"] = link.push(line, line, plus)
        j["down"] = link.push(line, line, minus)
        j["core"].append(link.push(block, block, near["core"]))
    for j in jobs:
        plus, minus = near[j["far"]]
        left, right = (j["q"] + 3) % 4, (j["q"] + 1) % 4
        j["up"].wait_recv()
        part = j["line"](left, pl.ds(0, 2))
        j["up2"] = link.push(part, part, plus)
        j["down"].wait_recv()
        part = j["line"](right, pl.ds(2, 2))
        j["down2"] = link.push(part, part, minus)
        for side in (left, right):
            block = j["line"](side)
            j["core"].append(link.push(block, block, near["core"]))
    for j in jobs:
        opposite = (j["q"] + 2) % 4
        j["up2"].wait_recv()
        part = j["line"](opposite, pl.ds(0, 2))
        j["core"].append(link.push(part, part, near["core"]))
        j["down2"].wait_recv()
        part = j["line"](opposite, pl.ds(2, 2))
        j["core"].append(link.push(part, part, near["core"]))
    for j in jobs:
        for copy in j["core"]:
            copy.wait_recv()
    link.drain()


def gather_weights(pack):
    copies = 3 + 2 * 16
    return pl.pallas_call(
        gather_kernel,
        name="gather_weights",
        out_shape=(
            jax.ShapeDtypeStruct((4, 4, 2, BLOCK, WA), BF16),
            jax.ShapeDtypeStruct((4, 4, 2, BLOCK, WB), BF16),
        ),
        in_specs=[pl.BlockSpec(memory_space=pltpu.VMEM)],
        out_specs=(pl.BlockSpec(memory_space=pl.ANY), pl.BlockSpec(memory_space=pl.ANY)),
        scratch_shapes=[
            pltpu.VMEM((4, PADDED, WA + WB), BF16),
            pltpu.VMEM((BLOCK, WA), BF16),
            pltpu.VMEM((BLOCK, WB), BF16),
            pltpu.SemaphoreType.DMA((copies,)),
            pltpu.SemaphoreType.DMA((copies,)),
            pltpu.SemaphoreType.DMA((2,)),
        ],
        compiler_params=pltpu.CompilerParams(
            collective_id=0, has_side_effects=True, vmem_limit_bytes=16 * 1024 * 1024
        ),
        cost_estimate=pl.CostEstimate(flops=0, bytes_accessed=24_000_000, transcendentals=0),
    )(pack)


def add_blocks(dst, far, start, count, sources):
    def step(i, carry):
        total = dst[far, start + i].astype(F32)
        for source in sources:
            total = total + source(i).astype(F32)
        dst[far, start + i] = total.astype(BF16)
        return carry

    lax.fori_loop(0, count, step, 0)


def scatter_kernel(
    ga, gb, gs, out_a, out_b,
    core_a, core_b, mine_a, mine_b, one_a, one_b, two_a, two_b,
    half_a0, half_a1, half_b0, half_b1, last_a, last_b, xout, xin,
    send, recv, local,
):
    y, z, c, x = place()
    near = neighbours(y, z, c, x)
    greet(everyone_near(near))
    link = Links(send, recv)
    other = 1 - c
    jobs = [
        dict(src=[(lambda f, s: ga.at[f, :, s], 0, WA)], core=core_a, mine=mine_a, one=one_a, two=two_a,
             halves=(half_a0, half_a1), last=last_a, far="y", close="z", q=y, p=z,
             width=WA, half=1024, lane=0, i=0),
        dict(src=[(lambda f, s: gb.at[:, f, s], 0, D), (lambda f, s: gs.at[:, f, s], D, SMALL)],
             core=core_b, mine=mine_b, one=one_b, two=two_b,
             halves=(half_b0, half_b1), last=last_b, far="z", close="y", q=z, p=y,
             width=WB, half=896, lane=WA, i=1),
    ]
    slots = 0
    for step in (2, 3, 1, 0):
        for j in jobs:
            f = (j["q"] + step) % 4
            j[step] = []
            for source, lane, width in j["src"]:
                lanes = pl.ds(lane, width)
                pushed = link.push(
                    source(f, other), j["core"].at[f, :, :, lanes], near["core"]
                )
                kept = pltpu.make_async_copy(
                    source(f, c), j["mine"].at[f, :, :, lanes], local.at[slots]
                )
                slots += 1
                kept.start()
                j[step].append((pushed, kept))

    def ready(j, step):
        for pushed, kept in j[step]:
            pushed.wait_recv()
            kept.wait()

    for j in jobs:
        f = (j["q"] + 2) % 4
        ready(j, 2)
        mine = j["mine"]
        add_blocks(j["core"], f, 0, 4, [lambda i, f=f, m=mine: m[f, i]])
        plus, minus = near[j["far"]]
        j["down"] = link.push(j["core"].at[f, pl.ds(0, 2)], j["one"].at[0], minus)
        j["up"] = link.push(j["core"].at[f, pl.ds(2, 2)], j["one"].at[1], plus)
    for j in jobs:
        plus, minus = near[j["far"]]
        mine, one = j["mine"], j["one"]
        f = (j["q"] + 3) % 4
        ready(j, 3)
        add_blocks(j["core"], f, 2, 2, [lambda i, f=f, m=mine: m[f, i + 2]])
        j["down"].wait_recv()
        add_blocks(
            j["core"], f, 0, 2, [lambda i, f=f, m=mine: m[f, i], lambda i, o=one: o[0, i]]
        )
        j["down2"] = link.push(j["core"].at[f], j["two"].at[0], minus)
        f = (j["q"] + 1) % 4
        ready(j, 1)
        add_blocks(j["core"], f, 0, 2, [lambda i, f=f, m=mine: m[f, i]])
        j["up"].wait_recv()
        add_blocks(
            j["core"], f, 2, 2, [lambda i, f=f, m=mine: m[f, i + 2], lambda i, o=one: o[1, i]]
        )
        j["up2"] = link.push(j["core"].at[f], j["two"].at[1], plus)
    for j in jobs:
        mine, two = j["mine"], j["two"]
        f = j["q"]
        ready(j, 0)
        j["down2"].wait_recv()
        j["up2"].wait_recv()
        add_blocks(
            j["core"], f, 0, 4,
            [lambda i, f=f, m=mine: m[f, i], lambda i, t=two: t[0, i], lambda i, t=two: t[1, i]],
        )
        plus, minus = near[j["close"]]
        g = (j["p"] + 2) % 4
        h, w = j["half"], j["width"]
        j["down"] = link.push(j["core"].at[f, g, :, pl.ds(0, h)], j["halves"][0], minus)
        j["up"] = link.push(j["core"].at[f, g, :, pl.ds(h, w - h)], j["halves"][1], plus)
    for j in jobs:
        plus, minus = near[j["close"]]
        f, h, w, core = j["q"], j["half"], j["width"], j["core"]
        g = (j["p"] + 3) % 4
        j["down"].wait_recv()
        core[f, g, :, 0:h] = (
            core[f, g, :, 0:h].astype(F32) + j["halves"][0][...].astype(F32)
        ).astype(BF16)
        j["down2"] = link.push(core.at[f, g], j["last"].at[0], minus)
        g = (j["p"] + 1) % 4
        j["up"].wait_recv()
        core[f, g, :, h:w] = (
            core[f, g, :, h:w].astype(F32) + j["halves"][1][...].astype(F32)
        ).astype(BF16)
        j["up2"] = link.push(core.at[f, g], j["last"].at[1], plus)
    select = pick_rows(4 * PADDED, BLOCK, PADDED, PIECE)
    for j in jobs:
        f, g = j["q"], j["p"]
        j["down2"].wait_recv()
        j["up2"].wait_recv()
        total = (
            j["core"][f, g].astype(F32)
            + j["last"][0].astype(F32)
            + j["last"][1].astype(F32)
        ).astype(BF16)
        spread = jnp.dot(select, total, preferred_element_type=F32).astype(BF16)
        xout[:, :, j["lane"] : j["lane"] + j["width"]] = spread.reshape(4, PADDED, j["width"])
    final = [
        link.push(xout.at[(x + d) % 4], xin.at[d - 1], near["x"][d - 1]) for d in (1, 2, 3)
    ]
    for copy in final:
        copy.wait_recv()
    mine = xout[x].astype(F32)
    for d in range(3):
        mine = mine + xin[d].astype(F32)
    out_a[...] = mine[:, :WA]
    out_b[...] = mine[:, WA:]
    link.drain()


def scatter_sums(ga, gb, gs):
    copies = 2 * (4 + 4 + 4) + 4 + 3
    vmem = pltpu.VMEM
    scratch = []
    for shape in ((4, 4), (4, 4), (2, 2), (2, 4)):
        scratch += [vmem((*shape, BLOCK, WA), BF16), vmem((*shape, BLOCK, WB), BF16)]
    scratch += [
        vmem((BLOCK, 1024), BF16),
        vmem((BLOCK, 1024), BF16),
        vmem((BLOCK, 896), BF16),
        vmem((BLOCK, WB - 896), BF16),
        vmem((2, BLOCK, WA), BF16),
        vmem((2, BLOCK, WB), BF16),
        vmem((4, PADDED, WA + WB), BF16),
        vmem((3, PADDED, WA + WB), BF16),
        pltpu.SemaphoreType.DMA((copies,)),
        pltpu.SemaphoreType.DMA((copies,)),
        pltpu.SemaphoreType.DMA((12,)),
    ]
    return pl.pallas_call(
        scatter_kernel,
        name="scatter_sums",
        out_shape=(
            jax.ShapeDtypeStruct((PADDED, WA), F32),
            jax.ShapeDtypeStruct((PADDED, WB), F32),
        ),
        in_specs=[pl.BlockSpec(memory_space=pl.ANY)] * 3,
        out_specs=(pl.BlockSpec(memory_space=pltpu.VMEM), pl.BlockSpec(memory_space=pltpu.VMEM)),
        scratch_shapes=scratch,
        compiler_params=pltpu.CompilerParams(
            collective_id=1, has_side_effects=True, vmem_limit_bytes=40 * 1024 * 1024
        ),
        cost_estimate=pl.CostEstimate(flops=0, bytes_accessed=24_000_000, transcendentals=0),
    )(ga, gb, gs)


def rms_scale(values, gain_vec):
    return (
        values * lax.rsqrt(jnp.mean(values * values, axis=-1, keepdims=True) + norm_eps) * gain_vec
    )


def rope_tables(position, half_dim):
    frequency = rope_base ** (-jnp.arange(half_dim, dtype=jnp.float32) / half_dim)
    angles = position.astype(jnp.float32)[:, None] * frequency[None, :]
    return (jnp.cos(angles)[:, None, :], jnp.sin(angles)[:, None, :])


def rotate(values, cosine, sine_tab):
    half_dim = values.shape[-1] // 2
    lower_half = values[..., :half_dim]
    upper_half = values[..., half_dim:]
    return jnp.concatenate(
        [lower_half * cosine - upper_half * sine_tab, lower_half * sine_tab + upper_half * cosine],
        axis=-1,
    )


def unrotate(grads_in, cosine, sine_tab):
    half_dim = grads_in.shape[-1] // 2
    lower_half = grads_in[..., :half_dim]
    upper_half = grads_in[..., half_dim:]
    return jnp.concatenate(
        [lower_half * cosine + upper_half * sine_tab, upper_half * cosine - lower_half * sine_tab],
        axis=-1,
    )


def seq_layout(seq_lens, row_ids):
    seq_ends = jnp.cumsum(seq_lens)
    segment = jnp.sum((row_ids[:, None] >= seq_ends[None, :]).astype(jnp.int32), axis=1)
    seq_start = jnp.sum(
        jnp.where(seq_ends[None, :] <= row_ids[:, None], seq_lens[None, :], 0), axis=1
    )
    return (segment, row_ids - seq_start)


def exchange(rows):
    return lax.all_to_all(
        rows.reshape(EXPERTS, CAP, D), "expert", split_axis=0, concat_axis=0, tiled=True
    ).reshape(EXPERTS * CAP, D)


def body(
    tokens, lengths, top_experts, w_qkv, w_out, gain_attn, gain_ffn, router, gate_up, down_proj, cotangent,
):
    count = tokens.shape[0]
    scale = HEAD_DIM ** (-0.5)
    pack = jnp.concatenate(
        [
            w_qkv,
            w_out.T,
            router,
            gain_attn[:, None],
            gain_ffn[:, None],
            jnp.zeros((PIECE, SMALL - EXPERTS - 2), BF16),
        ],
        axis=1,
    )
    pack = jnp.pad(pack, ((0, PADDED - PIECE), (0, 0)))
    full_a, full_b = gather_weights(pack)
    full_qkv = full_a.reshape(D, WA)
    full_b = full_b.reshape(D, WB)
    out_t = full_b[:, :D]
    full_router = full_b[:, D : D + EXPERTS]
    gains = full_b[:, D + EXPERTS : D + EXPERTS + 2].astype(F32).T
    attn_g, ffn_g = gains[0], gains[1]

    named = jnp.sum(
        (top_experts[:, :, None] == jnp.arange(EXPERTS, dtype=jnp.int32)).astype(F32), axis=1
    )
    row_ids = jnp.arange(count, dtype=jnp.int32)
    earlier = (row_ids[None, :] < row_ids[:, None]).astype(BF16)
    slot_of = jnp.dot(earlier, named.astype(BF16), preferred_element_type=F32)
    slot_of = jnp.where(named > 0, slot_of, -1.0)
    hits = slot_of[:, :, None] == jnp.arange(CAP, dtype=F32)
    any_slot = hits.reshape(count, EXPERTS * CAP).astype(BF16)
    logits = jnp.dot(tokens, full_router, preferred_element_type=F32)
    masked_logits = jnp.where(named > 0, logits, -jnp.inf)
    gates = jax.nn.softmax(masked_logits, axis=-1)
    slot_gates = jnp.sum(jnp.where(hits, gates[:, :, None], 0.0), axis=0).reshape(-1)
    row_grads = (
        jnp.dot(any_slot.T, cotangent, preferred_element_type=F32) * slot_gates[:, None]
    ).astype(BF16)
    arrived_grads = exchange(row_grads)

    tok_f = tokens.astype(F32)
    normed = rms_scale(tok_f, attn_g).astype(BF16)
    projected = jnp.dot(normed, full_qkv, preferred_element_type=F32)
    shard_pos = lax.axis_index("shard")
    group_rows = lax.axis_size("shard") * count
    all_ids = jnp.arange(group_rows, dtype=jnp.int32)
    key_segment, key_position = seq_layout(lengths[0], all_ids)
    own_ids = shard_pos * count + row_ids
    own_segment = lax.dynamic_slice_in_dim(key_segment, shard_pos * count, count)
    own_position = lax.dynamic_slice_in_dim(key_position, shard_pos * count, count)
    cosine, sine_tab = rope_tables(own_position, HEAD_DIM // 2)
    queries = rotate(
        projected[:, :WIDTH_Q].reshape(count, HEADS_Q, HEAD_DIM), cosine, sine_tab
    ).astype(BF16)
    keys_rot = rotate(
        projected[:, WIDTH_Q : WIDTH_Q + WIDTH_KV].reshape(count, HEADS_KV, HEAD_DIM),
        cosine,
        sine_tab,
    ).astype(BF16)
    values = projected[:, WIDTH_Q + WIDTH_KV :].astype(BF16)
    local_kv = jnp.concatenate([keys_rot.reshape(count, WIDTH_KV), values], axis=1)
    group_kv = lax.all_gather(local_kv, "shard", axis=0, tiled=True)
    keys_all = group_kv[:, :WIDTH_KV].reshape(group_rows, HEADS_KV, HEAD_DIM)
    values_all = group_kv[:, WIDTH_KV:].reshape(group_rows, HEADS_KV, HEAD_DIM)
    grouped = queries.reshape(count, HEADS_KV, REPEAT, HEAD_DIM)
    allowed = (own_segment[:, None] == key_segment[None, :]) & (
        all_ids[None, :] <= own_ids[:, None]
    )

    def attn_scores():
        raw_scores = (
            jnp.einsum("tgrd,kgd->grtk", grouped, keys_all, preferred_element_type=F32) * scale
        )
        return jnp.where(allowed, raw_scores, -1e30)

    masked = attn_scores()
    top_score = jnp.max(masked, axis=-1, keepdims=True)
    expo_vals = jnp.exp(masked - top_score)
    total_weight = jnp.sum(expo_vals, axis=-1, keepdims=True)
    probs_low = (expo_vals / total_weight).astype(BF16)
    attended = (
        jnp.einsum("grtk,kgd->tgrd", probs_low, values_all, preferred_element_type=F32)
        .reshape(count, WIDTH_Q)
        .astype(BF16)
    )
    branch = lax.dot_general(
        attended, out_t, (((1,), (1,)), ((), ())), preferred_element_type=F32
    )
    middle = tok_f + branch
    normed_ffn = rms_scale(middle, ffn_g).astype(BF16)
    dispatch = jnp.dot(any_slot.T, normed_ffn, preferred_element_type=F32).astype(BF16)
    dispatch, arrived_grads = lax.optimization_barrier((dispatch, arrived_grads))
    arrived = exchange(dispatch)
    hidden = jnp.dot(arrived, gate_up[0], preferred_element_type=F32)

    def activate(hidden_in):
        return jax.nn.gelu(hidden_in[:, :FF], approximate=True) * hidden_in[:, FF:]

    mixed_hidden, act_pull = jax.vjp(activate, hidden)
    mixed_low = mixed_hidden.astype(BF16)
    grad_mixed = jnp.dot(arrived_grads, down_proj[0].T, preferred_element_type=F32)
    grad_hidden = act_pull(grad_mixed)[0].astype(BF16)
    grad_rows = jnp.dot(grad_hidden, gate_up[0].T, preferred_element_type=F32).astype(BF16)
    back_rows = exchange(grad_rows)
    expert_out = jnp.dot(mixed_low, down_proj[0], preferred_element_type=F32).astype(BF16)
    expert_out, back_rows = lax.optimization_barrier((expert_out, back_rows))
    returned = exchange(expert_out)
    grad_down_local = jnp.dot(mixed_low.T, arrived_grads, preferred_element_type=F32)
    grad_up_local = jnp.dot(arrived.T, grad_hidden, preferred_element_type=F32)

    upstream = cotangent.astype(F32)
    grad_normed_ffn = jnp.dot(any_slot, back_rows, preferred_element_type=F32)
    ffn_value, ffn_pull = jax.vjp(rms_scale, middle, ffn_g)
    grad_mid_norm, grad_ffn_gain = ffn_pull(grad_normed_ffn)
    grad_middle = upstream + grad_mid_norm
    grad_branch = grad_middle.astype(BF16)
    grad_out_t = jnp.dot(grad_branch.T, attended, preferred_element_type=F32).astype(BF16)
    grad_attended = (
        jnp.dot(grad_branch, out_t, preferred_element_type=F32)
        .astype(BF16)
        .reshape(count, HEADS_KV, REPEAT, HEAD_DIM)
    )
    probs_again = jnp.exp(attn_scores() - top_score) / total_weight
    grad_probs = jnp.einsum(
        "tgrd,kgd->grtk", grad_attended, values_all, preferred_element_type=F32
    )
    grad_scores = (
        probs_again * (grad_probs - jnp.sum(probs_again * grad_probs, axis=-1, keepdims=True))
    ).astype(BF16)
    grad_queries = (
        jnp.einsum("grtk,kgd->tgrd", grad_scores, keys_all, preferred_element_type=F32) * scale
    )
    grad_keys = (
        jnp.einsum("grtk,tgrd->kgd", grad_scores, grouped, preferred_element_type=F32) * scale
    )
    grad_values = jnp.einsum(
        "grtk,tgrd->kgd", probs_low, grad_attended, preferred_element_type=F32
    )
    group_grads = jnp.concatenate(
        [grad_keys.reshape(group_rows, WIDTH_KV), grad_values.reshape(group_rows, WIDTH_KV)], axis=1
    )
    own_kv_grads = lax.psum_scatter(
        group_grads.astype(BF16), "shard", scatter_dimension=0, tiled=True
    ).astype(F32)
    grad_projected = jnp.concatenate(
        [
            unrotate(grad_queries.reshape(count, HEADS_Q, HEAD_DIM), cosine, sine_tab).reshape(
                count, WIDTH_Q
            ),
            unrotate(
                own_kv_grads[:, :WIDTH_KV].reshape(count, HEADS_KV, HEAD_DIM), cosine, sine_tab
            ).reshape(count, WIDTH_KV),
            own_kv_grads[:, WIDTH_KV:],
        ],
        axis=1,
    ).astype(BF16)
    grad_qkv_local = jnp.dot(normed.T, grad_projected, preferred_element_type=F32).astype(BF16)
    grad_normed = lax.dot_general(
        grad_projected, full_qkv, (((1,), (1,)), ((), ())), preferred_element_type=F32
    )
    attn_value, attn_pull = jax.vjp(rms_scale, tok_f, attn_g)
    grad_tok_norm, grad_attn_gain = attn_pull(grad_normed)

    mix = jnp.where(hits, gates[:, :, None], 0.0).reshape(count, EXPERTS * CAP)
    mix_high = mix.astype(BF16)
    mix_low = (mix - mix_high.astype(F32)).astype(BF16)
    combined = jnp.dot(mix_high, returned, preferred_element_type=F32) + jnp.dot(
        mix_low, returned, preferred_element_type=F32
    )
    output = (middle + combined).astype(BF16)
    products = lax.dot_general(
        cotangent, returned, (((1,), (1,)), ((), ())), preferred_element_type=F32
    ).reshape(count, EXPERTS, CAP)
    gate_grad = jnp.sum(jnp.where(hits, products, 0.0), axis=-1)
    logit_grad = gates * (gate_grad - jnp.sum(gates * gate_grad, axis=-1, keepdims=True))
    router_f = full_router.astype(F32)
    grad_router_local = jnp.dot(tok_f.T, logit_grad, precision=precise)
    grad_from_router = jnp.dot(logit_grad, router_f.T, precision=precise)
    grad_tokens = (grad_middle + grad_tok_norm + grad_from_router).astype(BF16)

    grad_small = jnp.concatenate(
        [
            grad_router_local,
            grad_attn_gain[:, None],
            grad_ffn_gain[:, None],
            jnp.zeros((D, SMALL - EXPERTS - 2), F32),
        ],
        axis=1,
    ).astype(BF16)
    sum_a, sum_b = scatter_sums(
        grad_qkv_local.reshape(4, 4, 2, BLOCK, WA),
        grad_out_t.reshape(4, 4, 2, BLOCK, D),
        grad_small.reshape(4, 4, 2, BLOCK, SMALL),
    )
    sum_b = sum_b[:PIECE]
    up_sum = lax.psum_scatter(
        grad_up_local[None].astype(BF16), "shard", scatter_dimension=1, tiled=True
    ).astype(F32)
    down_sum = lax.psum_scatter(
        grad_down_local[None].astype(BF16), "shard", scatter_dimension=2, tiled=True
    ).astype(F32)
    return (
        output,
        grad_tokens,
        sum_a[:PIECE],
        sum_b[:, :D].T,
        sum_b[:, D + EXPERTS],
        sum_b[:, D + EXPERTS + 1],
        sum_b[:, D : D + EXPERTS],
        up_sum,
        down_sum,
    )


def solution(mesh):
    return jax.shard_map(
        body,
        mesh=mesh,
        in_specs=(
            P(("expert", "shard"), None),
            P("expert", None),
            P(("expert", "shard"), None),
            P(("expert", "shard"), None),
            P(None, ("expert", "shard")),
            P(("expert", "shard")),
            P(("expert", "shard")),
            P(("expert", "shard"), None),
            P("expert", None, None),
            P("expert", None, None),
            P(("expert", "shard"), None),
        ),
        out_specs=(
            P(("expert", "shard"), None),
            P(("expert", "shard"), None),
            P(("expert", "shard"), None),
            P(None, ("expert", "shard")),
            P(("expert", "shard")),
            P(("expert", "shard")),
            P(("expert", "shard"), None),
            P("expert", "shard", None),
            P("expert", None, "shard"),
        ),
        check_vma=False,
    )
```

time: 1530 us -> 537 us (0.35)
  blocking collectives: 866 us -> 63.6 us
  starting transfers between devices: 200 us -> 18.6 us
  local copies, waits for them, and re-layouts: 201 us -> 70.1 us
  Pallas kernels: 0 us -> 110 us
  waiting for transfers between devices: 39.8 us -> 74 us
  other arithmetic: 46.7 us -> 24.5 us
    unnamed x3 -> x0, blocking collectives: 569 us -> none
    unnamed x66 -> x1, starting transfers between devices: 195 us -> 0.04 us
    unnamed x239 -> x147, local copies, waits for them, and re-layouts: 174 us -> 42.4 us
    all_to_all x3 -> x1, blocking collectives: 187 us -> 63.6 us  [exchange(): lax.all_to_all(rows.reshape(EXPERTS, CAP, D), 'expert', split_axis=0, con...]
    pallas_call x0 -> x2, Pallas kernels: none -> 110 us  [the longest x1 57.5 us: scatter_sums(): pl.pallas_call(scatter_kernel, name='scatter_sums', out_shape=(jax.ShapeD...]
    all_gather x1 -> x0, blocking collectives: 109 us -> none  [body(): lax.all_gather(router, ('expert', 'shard'), axis=0, tiled=True)]
    all_to_all x1 -> x3, waiting for transfers between devices: 0.01 us -> 73.7 us  [exchange(): lax.all_to_all(rows.reshape(EXPERTS, CAP, D), 'expert', split_axis=0, con...]
    all_gather x2 -> x0, waiting for transfers between devices: 33.2 us -> none  [the longest x1 33.2 us: body(): lax.all_gather(w_out, ('expert', 'shard'), axis=1, tiled=True)]
  transfers between devices with their start and end apart: 72 -> 7, of which waited for: 4 -> 4; matrix products, arithmetic and copies ran while one was open for 46% -> 32% of each run, Pallas kernels for 0% -> 11%
where the time goes in v1:
time: 537 us; the launch traced here: 530 us
  matrix products  154 us (29%)
  Pallas kernels  110 us (20%)
  waiting for transfers between devices  74 us (14%)
  local copies, waits for them, and re-layouts  70.1 us (13%)
  blocking collectives  63.6 us (12%)
  other arithmetic  24.5 us (5%)
  starting transfers between devices  18.6 us (3%)
  between operations  15.3 us (3%)
    all_to_all x3, waiting for transfers between devices, exchange(): lax.all_to_all(rows.reshape(EXPERTS, CAP, D), 'expert', split_axis=0, con...  73.7 us
    all_to_all x1, blocking collectives, exchange(): lax.all_to_all(rows.reshape(EXPERTS, CAP, D), 'expert', split_axis=0, con...  63.6 us
    pallas_call x1, Pallas kernels, scatter_sums(): pl.pallas_call(scatter_kernel, name='scatter_sums', out_shape=(jax.ShapeD...  57.5 us
    pallas_call x1, Pallas kernels, gather_weights(): pl.pallas_call(gather_kernel, name='gather_weights', out_shape=(jax.Shape...  52.5 us
    unnamed x147, local copies, waits for them, and re-layouts  42.4 us
    all_to_all x3, starting transfers between devices, exchange(): lax.all_to_all(rows.reshape(EXPERTS, CAP, D), 'expert', split_axis=0, con...  18.1 us
    dot_general x1, matrix products, body(): jnp.dot(arrived_grads, down_proj[0].T, preferred_element_type=F32)  14 us
    dot_general x1, matrix products, body(): grad_up_local = jnp.dot(arrived.T, grad_hidden, preferred_element_type=F32)  13.6 us
  transfers between devices with their start and end apart: 7, of which 4 were waited for; matrix products, arithmetic and copies ran while one was open for 32% of the time, Pallas kernels for 11%

profile of v1, /device:TPU:0, one launch (start us, length us, event | category | flops | bytes accessed | tf_op | source)
XLA Modules:
  0.0 530.0 jit_solution(4151425002264879303)
XLA Ops:
  9.9 52.5 %gather_weights.1 = (bf16[4,4,2,48,2048]{4,3,2,1,0:T(8,128)(2,1)S(1)}, bf16[4,4,2,48,1664]{4,3,2,1,0:T(8,128)(2,1)S(1)}) custom-call(bf16[16,3712]{1,0:T(8,128)(2,1)S(1)} %pad.10.pack), custom_call_target="tpu_custom_call" | custom-call | bytes 24000000 | tf_op jit(solution)/shard_map/gather_weights/pallas_call | solution.py:187
  62.4 2.7 copy-done.5
  65.1 2.3 copy-done.4
  69.3 4.9 fusion.84
  87.8 4.6 fusion.5
  92.5 5.6 %all-to-all-start = ((bf16[32,48,1536]{2,1,0:T(8,128)(2,1)}), bf16[32,48,1536]{2,1,0:T(8,128)(2,1)}, u32[]{:S(2)}, u32[]{:S(2)}) async-start(bf16[32,48,1536]{2,1,0:T(8,128)(2,1)} %bitcast.178), calls=%async_computation | async-start | bytes 9437184 | tf_op jit(solution)/shard_map/all_to_all | solution.py:424
  98.1 2.7 slice.124
  100.8 3.0 copy.98
  109.0 2.1 fusion.99
  114.3 10.8 %fusion.102 = (f32[2,6,256]{2,1,0:T(8,128)S(1)}, f32[2,6,256,1024]{2,3,1,0:T(8,128)}) fusion(pred[256,1024]{0,1:T(8,128)(4,1)} %fusion.65, bf16[1024,2,128,1]{0,2,3,1:T(8,128)(2,1)} %copy.123, bf16[256,2,6,64]{3,0,2,1:T(8,128)(2,1)} %bitcast.182, bf16[256,2,6,64]{3,0,2,1:T(8,128)(2,1)} %bitcast.180), kind=kOutput, calls=%fused_computation.179 | convolution fusion | flops 819463168 | bytes 14168064 | tf_op jit(solution)/shard_map/sub | solution.py:509
  125.1 6.0 %fusion.53 = bf16[2,128,6,256]{3,1,2,0:T(8,128)(2,1)S(1)} fusion(bf16[1024,2,128,1]{2,1,0,3:T(2,128)(2,1)} %bitcast.198, f32[2,6,256,1024]{2,3,1,0:T(8,128)} %get-tuple-element.55, f32[2,6,256]{2,1,0:T(8,128)S(1)} %get-tuple-element.54), kind=kOutput, calls=%fused_computation.89 | convolution fusion | flops 811991040 | bytes 13905920 | tf_op jit(solution)/shard_map/grtk,kgd->tgrd/dot_general | solution.py:513
  134.0 3.6 convolution_convert_fusion.3
  137.7 19.3 %all-to-all-done = bf16[32,48,1536]{2,1,0:T(8,128)(2,1)} async-done(((bf16[32,48,1536]{2,1,0:T(8,128)(2,1)}), bf16[32,48,1536]{2,1,0:T(8,128)(2,1)}, u32[]{:S(2)}, u32[]{:S(2)}) %all-to-all-start) | async-done | bytes 4718624 | tf_op jit(solution)/shard_map/all_to_all | solution.py:424
  157.0 63.6 %all_to_all.20 = bf16[32,48,1536]{2,1,0:T(8,128)(2,1)S(1)} all-to-all(bf16[32,48,1536]{2,1,0:T(8,128)(2,1)} %bitcast.168), channel_id=1, replica_groups=mesh['expert'=32,'shard'=4] {'expert'}, dimensions={0} | all-to-all | bytes 9437184 | tf_op jit(solution)/shard_map/all_to_all | solution.py:424
  220.6 2.1 copy-done.15
  222.7 12.1 %fusion.17 = f32[1536,1536]{1,0:T(8,128)} fusion(bf16[1536,1536]{1,0:T(8,128)(2,1)S(1)} %bitcast.176, bf16[1,1536,1536]{2,1,0:T(8,128)(2,1)} %param.19), kind=kOutput, calls=%fused_computation.32 | convolution fusion | flops 7247757312 | bytes 18874368 | tf_op jit(solution)/shard_map/dot_general | solution.py:525
  234.8 14.0 %fusion.43 = (f32[1536,768]{1,0:T(8,128)S(1)}, f32[1536,768]{1,0:T(8,128)S(1)}, bf16[1536,768]{1,0:T(8,128)(2,1)}) fusion(f32[1536,1536]{1,0:T(8,128)} %fusion.17, bf16[1536,1536]{1,0:T(8,128)(2,1)} %bitcast.20, bf16[1,768,1536]{2,1,0:T(8,128)(2,1)S(1)} %copy-done), kind=kOutput, calls=%fused_computation.72 | convolution fusion | flops 3652190208 | bytes 28311552 | tf_op jit(solution)/shard_map/dot_general | solution.py:532
  248.9 9.3 %convolution_convert_fusion.5 = bf16[1536,1536]{1,0:T(8,128)(2,1)} fusion(bf16[1,1536,1536]{2,1,0:T(8,128)(2,1)S(1)} %bitcast.210, f32[1536,768]{1,0:T(8,128)S(1)} %get-tuple-element.36, f32[1536,768]{1,0:T(8,128)S(1)} %get-tuple-element.35), kind=kOutput, calls=%fused_computation.17 | convolution fusion | flops 7254835200 | bytes 18874368 | tf_op jit(solution)/shard_map/dot_general | solution.py:534
  258.2 4.9 all-to-all-start.2
  263.2 8.3 %fusion.27 = bf16[1,768,1536]{2,1,0:T(8,128)(2,1)} fusion(bf16[1536,768]{1,0:T(8,128)(2,1)} %get-tuple-element.37, bf16[1536,1536]{1,0:T(8,128)(2,1)} %bitcast.20), kind=kOutput, calls=%fused_computation.50 | convolution fusion | flops 3625058304 | bytes 9437184 | tf_op jit(solution)/shard_map/dot_general | solution.py:539
  271.5 12.1 %copy.138 = bf16[1,768,1536]{1,0,2:T(2,128)(2,1)} copy(bf16[1,768,1536]{2,1,0:T(8,128)(2,1)} %fusion.27) | data formatting | bytes 4718592
  283.5 4.1 copy.154
  287.9 7.2 %convolution_convert_fusion.2 = bf16[1536,1536]{1,0:T(8,128)(2,1)} fusion(bf16[1536,768]{1,0:T(8,128)(2,1)} %get-tuple-element.37, bf16[1,768,1536]{2,1,0:T(8,128)(2,1)S(1)} %copy-done), kind=kOutput, calls=%fused_computation.14 | convolution fusion | flops 3626237952 | bytes 9437184 | tf_op jit(solution)/shard_map/dot_general | solution.py:536
  295.1 27.0 %all-to-all-done.2 = bf16[32,48,1536]{2,1,0:T(8,128)(2,1)} async-done(((bf16[32,48,1536]{2,1,0:T(8,128)(2,1)}), bf16[32,48,1536]{2,1,0:T(8,128)(2,1)}, u32[]{:S(2)}, u32[]{:S(2)}) %all-to-all-start.2) | async-done | bytes 4718624 | tf_op jit(solution)/shard_map/all_to_all | solution.py:424
  322.1 4.6 multiply_reduce_fusion
  329.0 10.3 %fusion.1 = (f32[2,6,256]{2,1,0:T(8,128)S(1)}, f32[2,1024,256,6]{2,1,3,0:T(8,128)}) fusion(f32[2,6,256,1024]{2,3,1,0:T(8,128)} %get-tuple-element.55, f32[2,6,256]{2,1,0:T(8,128)S(1)} %get-tuple-element.54, bf16[256,2,6,128]{0,3,2,1:T(8,128)(2,1)S(1)} %bitcast.191, bf16[1024,2,128,1]{2,1,0,3:T(2,128)(2,1)} %bitcast.199), kind=kOutput, calls=%fused_computation.3 | convolution fusion | flops 814740480 | bytes 26501120 | tf_op jit(solution)/shard_map/tgrd,kgd->grtk/dot_general | solution.py:555
  341.8 6.6 %fusion.3 = bf16[2,6,256,1024]{2,3,1,0:T(8,128)(2,1)S(1)} fusion(f32[2,1024,256,6]{2,1,3,0:T(8,128)} %get-tuple-element.62, f32[2,6,256]{2,1,0:T(8,128)S(1)} %get-tuple-element.61, f32[2,6,256,1024]{2,3,1,0:T(8,128)S(1)} %bitcast.171, f32[2,6,256]{2,1,0:T(8,128)S(1)} %get-tuple-element.54), kind=kLoop, calls=%fused_computation.5 | loop fusion | flops 12582912 | bytes 31481856 | tf_op jit(solution)/shard_map/convert_element_type | solution.py:560
  348.4 2.6 copy-done.6
  351.0 2.5 fusion.63
  353.5 2.2 fusion.60
  357.1 13.6 %fusion.6 = bf16[1,1536,1536]{2,1,0:T(8,128)(2,1)} fusion(bf16[1536,1536]{1,0:T(8,128)(2,1)} %bitcast.177, f32[1536,768]{1,0:T(8,128)} %copy-done.59, f32[1536,768]{1,0:T(8,128)} %copy-done.58), kind=kOutput, calls=%fused_computation.20 | convolution fusion | flops 7254835200 | bytes 18874368 | tf_op jit(solution)/shard_map/dot_general | solution.py:540
  370.7 7.6 %all-to-all-start.3 = ((bf16[32,48,1536]{2,1,0:T(8,128)(2,1)}), bf16[32,48,1536]{2,1,0:T(8,128)(2,1)}, u32[]{:S(2)}, u32[]{:S(2)}) async-start(bf16[32,48,1536]{2,1,0:T(8,128)(2,1)} %bitcast.175), calls=%async_computation.3 | async-start | bytes 9437184 | tf_op jit(solution)/shard_map/all_to_all | solution.py:424
  380.4 3.9 convolution_multiply_fusion.1
  384.7 3.5 convolution_convert_fusion.1
  388.3 1.8 reshape_bitcast_fusion
  390.1 3.2 copy.139
  393.3 2.3 convert_element_type.159
  397.8 6.0 %fusion.45 = (bf16[1536]{0:T(1024)(128)(2,1)S(1)}, f32[256]{0:T(256)S(1)}, f32[256,1536]{1,0:T(8,128)}) fusion(bf16[256,1536]{1,0:T(8,128)(2,1)S(1)} %copy-done.9, f32[256]{0:T(256)S(1)} %copy-done.50, f32[1536]{0:T(1024)S(1)} %copy-done.46, bf16[1536,2048]{1,0:T(8,128)(2,1)} %bitcast.167, bf16[256,256]{0,1:T(8,128)(2,1)S(1)} %get-tuple-element.49, ...), kind=kOutput, calls=%fused_computation.74 | convolution fusion | flops 1616509184 | bytes 9710592 | tf_op jit(solution)/shard_map/dot_general | solution.py:589
  404.6 5.6 %convolution_convert_fusion = bf16[1536,2048]{1,0:T(8,128)(2,1)} fusion(bf16[256,256]{0,1:T(8,128)(2,1)} %copy-done.36, bf16[256,256]{0,1:T(8,128)(2,1)S(1)} %bitcast.196, bf16[256,1536]{0,1:T(8,128)(2,1)S(1)} %bitcast.185, bf16[256,1536]{1,0:T(8,128)(2,1)S(1)} %copy-done.9, f32[1536]{0:T(1024)S(1)} %copy-done.46, f32[256]{0:T(256)S(1)} %copy-done.50), kind=kOutput, calls=%fused_computation.11 | convolution fusion | flops 1618477056 | bytes 8133632 | tf_op jit(solution)/shard_map/dot_general | solution.py:588
  410.1 27.3 %all-to-all-done.3 = bf16[32,48,1536]{2,1,0:T(8,128)(2,1)} async-done(((bf16[32,48,1536]{2,1,0:T(8,128)(2,1)}), bf16[32,48,1536]{2,1,0:T(8,128)(2,1)}, u32[]{:S(2)}, u32[]{:S(2)}) %all-to-all-start.3) | async-done | bytes 4718624 | tf_op jit(solution)/shard_map/all_to_all | solution.py:424
  437.5 3.8 fusion.104
  442.9 2.8 copy-done.2
  445.7 2.3 copy-done.3
  448.0 57.5 %scatter_sums.1 = (f32[16,2048]{1,0:T(8,128)S(1)}, f32[16,1664]{1,0:T(8,128)S(1)}) custom-call(bf16[4,4,2,48,2048]{4,3,2,1,0:T(8,128)(2,1)S(1)} %bitcast.154, bf16[4,4,2,48,1536]{4,3,2,1,0:T(8,128)(2,1)S(1)} %bitcast.155, bf16[4,4,2,48,128]{4,3,2,1,0:T(8,128)(2,1)S(1)} %maximum_maximum_fusion.gs), custom_call_target="tpu_custom_call" | custom-call | bytes 24000000 | tf_op jit(solution)/shard_map/scatter_sums/pallas_call | solution.py:365
  506.8 3.1 fusion.33
  510.6 3.9 convolution_bitcast_fusion
  514.5 4.8 fusion.32
  519.3 3.0 convert_element_type.156
  (222 shorter events, 44.7 us)
Async XLA Ops:
  7.2 227.6 %copy-start = (bf16[1,768,1536]{2,1,0:T(8,128)(2,1)S(1)}, bf16[1,768,1536]{2,1,0:T(8,128)(2,1)}, u32[]{:S(2)}) copy-start(bf16[1,768,1536]{2,1,0:T(8,128)(2,1)} %param.20) | copy-start | bytes 7077892
  7.2 101.8 %all-gather.2.cloned.1.call-start = ((), (), s32[]{:S(2)}) async-start(), calls=%async_computation.7 | async-start | bytes 1310720 | tf_op jit(solution)/shard_map/all_gather | solution.py:493
  67.8 6.4 %copy-start.45 = (f32[1536]{0:T(1024)}, f32[1536]{0:T(1024)S(1)}, u32[]{:S(2)}) copy-start(f32[1536]{0:T(1024)S(1)} %get-tuple-element.32) | copy-start | bytes 18436
  69.2 8.2 %copy-start.57 = (s32[1,4]{1,0:T(1,128)S(1)}, s32[1,4]{1,0:T(1,128)}, u32[]{:S(2)}) copy-start(s32[1,4]{1,0:T(1,128)} %param.12) | copy-start | bytes 52
  69.3 15.6 %copy-start.55 = (s32[256,4]{0,1:T(4,128)S(1)}, s32[256,4]{0,1:T(4,128)}, u32[]{:S(2)}) copy-start(s32[256,4]{0,1:T(4,128)} %param.13) | copy-start | bytes 12292
  69.3 15.6 %copy-start.7 = (bf16[256,1536]{1,0:T(8,128)(2,1)S(1)}, bf16[256,1536]{1,0:T(8,128)(2,1)}, u32[]{:S(2)}) copy-start(bf16[256,1536]{1,0:T(8,128)(2,1)} %param.11) | copy-start | bytes 2359300
  79.7 12.8 %copy-start.25 = (f32[256,64]{1,0:T(8,128)}, f32[256,64]{1,0:T(8,128)S(1)}, u32[]{:S(2)}) copy-start(f32[256,64]{1,0:T(8,128)S(1)} %copy.96) | copy-start | bytes 196612
  86.2 6.3 %copy-start.40 = (f32[256,32]{0,1:T(8,128)}, f32[256,32]{0,1:T(8,128)S(1)}, u32[]{:S(2)}) copy-start(f32[256,32]{0,1:T(8,128)S(1)} %get-tuple-element.59) | copy-start | bytes 98308
  86.2 6.3 %copy-start.47 = (f32[256]{0:T(256)}, f32[256]{0:T(256)S(1)}, u32[]{:S(2)}) copy-start(f32[256]{0:T(256)S(1)} %get-tuple-element.58) | copy-start | bytes 3076
  86.4 6.1 %copy-start.42 = (f32[256,32]{0,1:T(8,128)}, f32[256,32]{0,1:T(8,128)S(1)}, u32[]{:S(2)}) copy-start(f32[256,32]{0,1:T(8,128)S(1)} %convolution_select_fusion) | copy-start | bytes 98308
  86.8 5.7 %copy-start.20 = (pred[256,1536]{0,1:T(32,128)(4,1)}, pred[256,1536]{0,1:T(32,128)(4,1)S(1)}, u32[]{:S(2)}) copy-start(pred[256,1536]{0,1:T(32,128)(4,1)S(1)} %bitcast_compare_fusion) | copy-start | bytes 1179652
  92.5 64.5 %all-to-all-start = ((bf16[32,48,1536]{2,1,0:T(8,128)(2,1)}), bf16[32,48,1536]{2,1,0:T(8,128)(2,1)}, u32[]{:S(2)}, u32[]{:S(2)}) async-start(bf16[32,48,1536]{2,1,0:T(8,128)(2,1)} %bitcast.178), calls=%async_computation | async-start | bytes 9437184 | tf_op jit(solution)/shard_map/all_to_all | solution.py:424
  98.1 5.8 %copy-start.28 = (f32[256,64]{0,1:T(8,128)S(1)}, f32[256,64]{0,1:T(8,128)}, u32[]{:S(2)}) copy-start(f32[256,64]{0,1:T(8,128)} %get-tuple-element.52) | copy-start | bytes 196612
  98.1 5.8 %copy-start.30 = (f32[256,64]{0,1:T(8,128)S(1)}, f32[256,64]{0,1:T(8,128)}, u32[]{:S(2)}) copy-start(f32[256,64]{0,1:T(8,128)} %get-tuple-element.53) | copy-start | bytes 196612
  114.3 16.9 %slice-start = ((s8[5111808]{0:T(1024)(128)(4,1)}), s8[917504]{0:T(1024)(128)(4,1)S(1)}, s32[]{:S(2)}) async-start(s8[5111808]{0:T(1024)(128)(4,1)} %bitcast.159), calls=%async_computation.11 | async-start | bytes 1835008
  125.1 6.2 %slice-start.1 = ((s8[5111808]{0:T(1024)(128)(4,1)}), s8[4194304]{0:T(1024)(128)(4,1)S(1)}, s32[]{:S(2)}) async-start(s8[5111808]{0:T(1024)(128)(4,1)} %bitcast.159), calls=%async_computation.12 | async-start | bytes 8388608
  125.1 6.2 %copy-start.8 = (bf16[256,1536]{1,0:T(8,128)(2,1)S(1)}, bf16[256,1536]{1,0:T(8,128)(2,1)}, u32[]{:S(2)}) copy-start(bf16[256,1536]{1,0:T(8,128)(2,1)} %param.11) | copy-start | bytes 2359300
  222.7 26.1 %slice-start.7 = ((s8[4718592]{0:T(1024)(128)(4,1)}), s8[4194304]{0:T(1024)(128)(4,1)S(1)}, s32[]{:S(2)}) async-start(s8[4718592]{0:T(1024)(128)(4,1)} %bitcast.209), calls=%async_computation.18 | async-start | bytes 8388608
  234.8 14.0 %slice-start.8 = ((s8[4718592]{0:T(1024)(128)(4,1)}), s8[524288]{0:T(1024)(128)(4,1)S(1)}, s32[]{:S(2)}) async-start(s8[4718592]{0:T(1024)(128)(4,1)} %bitcast.209), calls=%async_computation.19 | async-start | bytes 1048576
  248.8 9.4 %copy-start.58 = (f32[1536,768]{1,0:T(8,128)}, f32[1536,768]{1,0:T(8,128)S(1)}, u32[]{:S(2)}) copy-start(f32[1536,768]{1,0:T(8,128)S(1)} %get-tuple-element.35) | copy-start | bytes 14155780
  248.8 9.4 %copy-start.59 = (f32[1536,768]{1,0:T(8,128)}, f32[1536,768]{1,0:T(8,128)S(1)}, u32[]{:S(2)}) copy-start(f32[1536,768]{1,0:T(8,128)S(1)} %get-tuple-element.36) | copy-start | bytes 14155780
  258.2 63.9 %all-to-all-start.2 = ((bf16[32,48,1536]{2,1,0:T(8,128)(2,1)}), bf16[32,48,1536]{2,1,0:T(8,128)(2,1)}, u32[]{:S(2)}, u32[]{:S(2)}) async-start(bf16[32,48,1536]{2,1,0:T(8,128)(2,1)} %bitcast.179), calls=%async_computation.2 | async-start | bytes 9437184 | tf_op jit(solution)/shard_map/all_to_all | solution.py:424
  263.1 125.2 %reduce-scatter.10.cloned.1.call-start = ((), (), s32[]{:S(2)}) async-start(), calls=%async_computation.10 | async-start | bytes 2949120
  287.7 34.5 %copy-start.22 = (pred[256,1536]{0,1:T(32,128)(4,1)S(1)}, pred[256,1536]{0,1:T(32,128)(4,1)}, u32[]{:S(2)}) copy-start(pred[256,1536]{0,1:T(32,128)(4,1)} %copy-done.20) | copy-start | bytes 1179652
  287.7 107.9 %reduce-scatter.6.cloned.1.call-start = ((), (), s32[]{:S(2)}) async-start(), calls=%async_computation.8 | async-start | bytes 1310720 | tf_op jit(solution)/shard_map/reduce_scatter | solution.py:573
  295.1 31.7 %copy-start.32 = (bf16[256,1536]{1,0:T(8,128)(2,1)S(1)}, bf16[256,1536]{1,0:T(8,128)(2,1)}, u32[]{:S(2)}) copy-start(bf16[256,1536]{1,0:T(8,128)(2,1)} %param.21) | copy-start | bytes 2359300
  327.3 57.4 %copy-start.10 = (f32[256,1536]{1,0:T(8,128)}, f32[256,1536]{1,0:T(8,128)S(1)}, u32[]{:S(2)}) copy-start(f32[256,1536]{1,0:T(8,128)S(1)} %fusion.46) | copy-start | bytes 4718596
  329.0 10.3 %slice-start.4 = ((s8[12582912]{0:T(1024)(128)(4,1)}), s8[4194304]{0:T(1024)(128)(4,1)S(1)}, s32[]{:S(2)}) async-start(s8[12582912]{0:T(1024)(128)(4,1)} %bitcast.170), calls=%async_computation.15 | async-start | bytes 8388608
  329.0 11.6 %slice-start.5 = ((s8[12582912]{0:T(1024)(128)(4,1)}), s8[4194304]{0:T(1024)(128)(4,1)S(1)}, s32[]{:S(2)}) async-start(s8[12582912]{0:T(1024)(128)(4,1)} %bitcast.170), calls=%async_computation.16 | async-start | bytes 8388608
  329.0 12.7 %slice-start.6 = ((s8[12582912]{0:T(1024)(128)(4,1)}), s8[4194304]{0:T(1024)(128)(4,1)S(1)}, s32[]{:S(2)}) async-start(s8[12582912]{0:T(1024)(128)(4,1)} %bitcast.170), calls=%async_computation.17 | async-start | bytes 8388608
  341.8 9.2 %copy-start.16 = (bf16[256,12,64]{2,0,1:T(8,128)(2,1)S(1)}, bf16[256,12,64]{2,0,1:T(8,128)(2,1)}, u32[]{:S(2)}) copy-start(bf16[256,12,64]{2,0,1:T(8,128)(2,1)} %copy.99) | copy-start | bytes 1179652
  341.8 9.2 %copy-start.17 = (bf16[256,12,64]{2,0,1:T(8,128)(2,1)S(1)}, bf16[256,12,64]{2,0,1:T(8,128)(2,1)}, u32[]{:S(2)}) copy-start(bf16[256,12,64]{2,0,1:T(8,128)(2,1)} %copy.100) | copy-start | bytes 1179652
  356.8 162.5 %reduce-scatter.8.cloned.1.call-start = ((), (), s32[]{:S(2)}) async-start(), calls=%async_computation.9 | async-start | bytes 5898240 | tf_op jit(solution)/shard_map/reduce_scatter | solution.py:627
  370.7 9.7 %copy-start.18 = (bf16[1024,2,128,1]{0,2,3,1:T(8,128)(2,1)S(1)}, bf16[1024,2,128,1]{0,2,3,1:T(8,128)(2,1)}, u32[]{:S(2)}) copy-start(bf16[1024,2,128,1]{0,2,3,1:T(8,128)(2,1)} %copy.123) | copy-start | bytes 1572868
  370.7 66.8 %all-to-all-start.3 = ((bf16[32,48,1536]{2,1,0:T(8,128)(2,1)}), bf16[32,48,1536]{2,1,0:T(8,128)(2,1)}, u32[]{:S(2)}, u32[]{:S(2)}) async-start(bf16[32,48,1536]{2,1,0:T(8,128)(2,1)} %bitcast.175), calls=%async_computation.3 | async-start | bytes 9437184 | tf_op jit(solution)/shard_map/all_to_all | solution.py:424
  378.3 6.0 %copy-start.29 = (f32[256,64]{0,1:T(8,128)S(1)}, f32[256,64]{0,1:T(8,128)}, u32[]{:S(2)}) copy-start(f32[256,64]{0,1:T(8,128)} %get-tuple-element.52) | copy-start | bytes 196612
  378.3 6.0 %copy-start.31 = (f32[256,64]{0,1:T(8,128)S(1)}, f32[256,64]{0,1:T(8,128)}, u32[]{:S(2)}) copy-start(f32[256,64]{0,1:T(8,128)} %get-tuple-element.53) | copy-start | bytes 196612
  388.3 8.7 %copy-start.26 = (f32[256,64]{1,0:T(8,128)S(1)}, f32[256,64]{1,0:T(8,128)}, u32[]{:S(2)}) copy-start(f32[256,64]{1,0:T(8,128)} %copy-done.25) | copy-start | bytes 196612
  388.3 8.7 %copy-start.27 = (f32[256,64]{1,0:T(8,128)S(1)}, f32[256,64]{1,0:T(8,128)}, u32[]{:S(2)}) copy-start(f32[256,64]{1,0:T(8,128)} %copy.97) | copy-start | bytes 196612
  388.3 9.5 %copy-start.9 = (bf16[256,1536]{1,0:T(8,128)(2,1)S(1)}, bf16[256,1536]{1,0:T(8,128)(2,1)}, u32[]{:S(2)}) copy-start(bf16[256,1536]{1,0:T(8,128)(2,1)} %param.11) | copy-start | bytes 2359300
  388.3 9.5 %copy-start.46 = (f32[1536]{0:T(1024)S(1)}, f32[1536]{0:T(1024)}, u32[]{:S(2)}) copy-start(f32[1536]{0:T(1024)} %copy-done.45) | copy-start | bytes 18436
  388.3 9.5 %copy-start.50 = (f32[256]{0:T(256)S(1)}, f32[256]{0:T(256)}, u32[]{:S(2)}) copy-start(f32[256]{0:T(256)} %copy-done.49) | copy-start | bytes 3076
  396.6 7.2 %copy-start.36 = (bf16[256,256]{0,1:T(8,128)(2,1)}, bf16[256,256]{0,1:T(8,128)(2,1)S(1)}, u32[]{:S(2)}) copy-start(bf16[256,256]{0,1:T(8,128)(2,1)S(1)} %get-tuple-element.49) | copy-start | bytes 393220
  397.8 6.8 %copy-start.54 = (f32[256]{0:T(256)S(1)}, f32[256]{0:T(256)}, u32[]{:S(2)}) copy-start(f32[256]{0:T(256)} %copy-done.53) | copy-start | bytes 3076
  404.6 32.9 %copy-start.33 = (bf16[256,1536]{1,0:T(8,128)(2,1)S(1)}, bf16[256,1536]{1,0:T(8,128)(2,1)}, u32[]{:S(2)}) copy-start(bf16[256,1536]{1,0:T(8,128)(2,1)} %param.21) | copy-start | bytes 2359300
  448.0 58.8 %copy-start.11 = (f32[256,1536]{1,0:T(8,128)S(1)}, f32[256,1536]{1,0:T(8,128)}, u32[]{:S(2)}) copy-start(f32[256,1536]{1,0:T(8,128)} %copy-done.10) | copy-start | bytes 4718596
  448.0 58.8 %copy-start.24 = (f32[256,1536]{1,0:T(8,128)S(1)}, f32[256,1536]{1,0:T(8,128)}, u32[]{:S(2)}) copy-start(f32[256,1536]{1,0:T(8,128)} %get-tuple-element.63) | copy-start | bytes 4718596
  514.5 8.4 %copy-start.1 = (bf16[1,768,1536]{2,1,0:T(8,128)(2,1)S(1)}, bf16[1,768,1536]{2,1,0:T(8,128)(2,1)}, u32[]{:S(2)}) copy-start(bf16[1,768,1536]{2,1,0:T(8,128)(2,1)} %param.20) | copy-start | bytes 7077892
  (28 other events, 99.2 us)
Sparse Core Ops, SparseCore 0:
  84.9 24.0 all-gather.1
  287.8 33.9 reduce-scatter.9
  356.9 25.7 reduce-scatter.5
  385.1 50.7 reduce-scatter.7

commit v2 on v1

--- a/solution.py
+++ b/solution.py
@@ -379,6 +379,205 @@
     )(ga, gb, gs)
 
 
+NEAREST = (
+    (0, 0), (0, 1), (1, 0), (0, 3),
+    (3, 0), (1, 1), (3, 3), (1, 3),
+    (3, 1), (0, 2), (2, 0), (1, 2),
+    (2, 1), (3, 2), (2, 3), (2, 2),
+)
+ROWS = EXPERTS * CAP
+CHUNKS = 4
+CHUNK = ROWS // CHUNKS
+TILE = 256
+
+
+def gelu_parts(g):
+    inner = 0.7978845608 * (g + 0.044715 * g * g * g)
+    th = jnp.tanh(inner)
+    half = 0.5 * (1.0 + th)
+    slope = half + 0.5 * g * (1.0 - th * th) * (0.7978845608 * (1.0 + 0.134145 * g * g))
+    return g * half, slope
+
+
+def experts_kernel(
+    sent, grads_in, gate_up, down, back, outs, up_grad, down_grad,
+    rows, grads, gu, dn, mixed, ghid, grow, eout,
+    send, recv, bsend, brecv, gsem, wsem, osem, own,
+):
+    y, z, c, x = place()
+    me = (y * 4 + z) * 2 + c
+    weights = [
+        pltpu.make_async_copy(gate_up.at[0], gu, wsem.at[0]),
+        pltpu.make_async_copy(down.at[0], dn, wsem.at[1]),
+    ]
+    slots = []
+    for s, (dy, dz) in enumerate(NEAREST):
+        for b in (0, 1):
+            core = c if b == 0 else 1 - c
+            source = device((y + dy) % 4, (z + dz) % 4, core, x)
+            target = device((y + 4 - dy) % 4, (z + 4 - dz) % 4, core, x)
+            slots.append((2 * s + b, source, target))
+    greet([source for _, source, _ in slots[1:]])
+    links, back_links = [], []
+    for i, source, target in slots:
+        here = rows.at[pl.ds(i * CAP, CAP)]
+        if i == 0:
+            copy = pltpu.make_async_copy(sent.at[me], here, own.at[0])
+        else:
+            copy = pltpu.make_async_remote_copy(
+                src_ref=sent.at[target[0]], dst_ref=here, send_sem=send.at[i],
+                recv_sem=recv.at[i], device_id=target, device_id_type=MESH,
+            )
+        copy.start()
+        links.append(copy)
+    incoming = []
+    for copy in weights:
+        copy.start()
+    for i, source, target in slots:
+        copy = pltpu.make_async_copy(
+            grads_in.at[source[0]], grads.at[pl.ds(i * CAP, CAP)], gsem.at[i]
+        )
+        copy.start()
+        incoming.append(copy)
+    for copy in weights:
+        copy.wait()
+    leaving = []
+    per = len(slots) // CHUNKS
+    for k in range(CHUNKS):
+        part = slots[k * per : (k + 1) * per]
+        for i, source, target in part:
+            incoming[i].wait()
+            if i == 0:
+                links[0].wait()
+            else:
+                links[i].wait_recv()
+        base = k * CHUNK
+        block = pl.ds(base, CHUNK)
+
+        def hidden_tile(j, carry, block=block):
+            lanes = pl.ds(pl.multiple_of(j * TILE, TILE), TILE)
+            upper = pl.ds(pl.multiple_of(FF + j * TILE, TILE), TILE)
+            g = jnp.dot(rows[block, :], gu[:, lanes], preferred_element_type=F32)
+            act, slope = gelu_parts(g)
+            u = jnp.dot(rows[block, :], gu[:, upper], preferred_element_type=F32)
+            mixed[block, lanes] = (act * u).astype(BF16)
+            m = lax.dot_general(
+                grads[block, :], dn[lanes, :], (((1,), (1,)), ((), ())),
+                preferred_element_type=F32,
+            )
+            ghid[block, lanes] = (m * u * slope).astype(BF16)
+            ghid[block, upper] = (m * act).astype(BF16)
+            return carry
+
+        lax.fori_loop(0, FF // TILE, hidden_tile, 0)
+
+        def rows_tile(j, carry, block=block):
+            lanes = pl.ds(pl.multiple_of(j * TILE, TILE), TILE)
+            grow[block, lanes] = lax.dot_general(
+                ghid[block, :], gu[lanes, :], (((1,), (1,)), ((), ())),
+                preferred_element_type=F32,
+            ).astype(BF16)
+            return carry
+
+        lax.fori_loop(0, D // TILE, rows_tile, 0)
+        for i, source, target in part:
+            here = grow.at[pl.ds(i * CAP, CAP)]
+            if i == 0:
+                copy = pltpu.make_async_copy(here, back.at[me], own.at[1])
+            else:
+                copy = pltpu.make_async_remote_copy(
+                    src_ref=here, dst_ref=back.at[me], send_sem=bsend.at[i],
+                    recv_sem=brecv.at[i], device_id=source, device_id_type=MESH,
+                )
+            copy.start()
+            back_links.append(copy)
+
+        def out_tile(j, carry, block=block):
+            lanes = pl.ds(pl.multiple_of(j * TILE, TILE), TILE)
+            eout[block, lanes] = jnp.dot(
+                mixed[block, :], dn[:, lanes], preferred_element_type=F32
+            ).astype(BF16)
+            return carry
+
+        lax.fori_loop(0, D // TILE, out_tile, 0)
+        for i, source, target in part:
+            copy = pltpu.make_async_copy(
+                eout.at[pl.ds(i * CAP, CAP)], outs.at[source[0]], osem.at[i]
+            )
+            copy.start()
+            leaving.append(copy)
+
+    def up_tile(j, carry):
+        lanes = pl.ds(pl.multiple_of(j * TILE, TILE), TILE)
+        up_grad[lanes, :] = lax.dot_general(
+            rows[:, lanes], ghid[...], (((0,), (0,)), ((), ())), preferred_element_type=F32
+        ).astype(BF16)
+        return carry
+
+    lax.fori_loop(0, D // TILE, up_tile, 0)
+
+    def down_tile(j, carry):
+        lanes = pl.ds(pl.multiple_of(j * TILE, TILE), TILE)
+        down_grad[lanes, :] = lax.dot_general(
+            mixed[:, lanes], grads[...], (((0,), (0,)), ((), ())), preferred_element_type=F32
+        ).astype(BF16)
+        return carry
+
+    lax.fori_loop(0, FF // TILE, down_tile, 0)
+    for copy in leaving:
+        copy.wait()
+    back_links[0].wait()
+    for copy in back_links[1:]:
+        copy.wait_recv()
+    for copy in links[1:]:
+        copy.wait_send()
+    for copy in back_links[1:]:
+        copy.wait_send()
+
+
+def run_experts(sent, grads_in, gate_up, down):
+    anywhere = pl.BlockSpec(memory_space=pl.ANY)
+    inside = pl.BlockSpec(memory_space=pltpu.VMEM)
+    blocks = jax.ShapeDtypeStruct((EXPERTS, CAP, D), BF16)
+    vmem, dma = pltpu.VMEM, pltpu.SemaphoreType.DMA
+    return pl.pallas_call(
+        experts_kernel,
+        name="experts",
+        out_shape=(
+            blocks,
+            blocks,
+            jax.ShapeDtypeStruct((D, 2 * FF), BF16),
+            jax.ShapeDtypeStruct((FF, D), BF16),
+        ),
+        in_specs=[anywhere] * 4,
+        out_specs=(anywhere, anywhere, inside, inside),
+        scratch_shapes=[
+            vmem((ROWS, D), BF16),
+            vmem((ROWS, D), BF16),
+            vmem((D, 2 * FF), BF16),
+            vmem((FF, D), BF16),
+            vmem((ROWS, FF), BF16),
+            vmem((ROWS, 2 * FF), BF16),
+            vmem((ROWS, D), BF16),
+            vmem((ROWS, D), BF16),
+            dma((EXPERTS,)),
+            dma((EXPERTS,)),
+            dma((EXPERTS,)),
+            dma((EXPERTS,)),
+            dma((EXPERTS,)),
+            dma((2,)),
+            dma((EXPERTS,)),
+            dma((2,)),
+        ],
+        compiler_params=pltpu.CompilerParams(
+            collective_id=2, has_side_effects=True, vmem_limit_bytes=58 * 1024 * 1024
+        ),
+        cost_estimate=pl.CostEstimate(
+            flops=33_000_000_000, bytes_accessed=60_000_000, transcendentals=1_200_000
+        ),
+    )(sent, grads_in, gate_up, down)
+
+
 def rms_scale(values, gain_vec):
     return (
         values * lax.rsqrt(jnp.mean(values * values, axis=-1, keepdims=True) + norm_eps) * gain_vec
@@ -520,24 +719,14 @@
     middle = tok_f + branch
     normed_ffn = rms_scale(middle, ffn_g).astype(BF16)
     dispatch = jnp.dot(any_slot.T, normed_ffn, preferred_element_type=F32).astype(BF16)
-    dispatch, arrived_grads = lax.optimization_barrier((dispatch, arrived_grads))
-    arrived = exchange(dispatch)
-    hidden = jnp.dot(arrived, gate_up[0], preferred_element_type=F32)
-
-    def activate(hidden_in):
-        return jax.nn.gelu(hidden_in[:, :FF], approximate=True) * hidden_in[:, FF:]
-
-    mixed_hidden, act_pull = jax.vjp(activate, hidden)
-    mixed_low = mixed_hidden.astype(BF16)
-    grad_mixed = jnp.dot(arrived_grads, down_proj[0].T, preferred_element_type=F32)
-    grad_hidden = act_pull(grad_mixed)[0].astype(BF16)
-    grad_rows = jnp.dot(grad_hidden, gate_up[0].T, preferred_element_type=F32).astype(BF16)
-    back_rows = exchange(grad_rows)
-    expert_out = jnp.dot(mixed_low, down_proj[0], preferred_element_type=F32).astype(BF16)
-    expert_out, back_rows = lax.optimization_barrier((expert_out, back_rows))
+    back_rows, expert_out, grad_up_local, grad_down_local = run_experts(
+        dispatch.reshape(EXPERTS, CAP, D),
+        arrived_grads.reshape(EXPERTS, CAP, D),
+        gate_up,
+        down_proj,
+    )
+    back_rows = back_rows.reshape(ROWS, D)
     returned = exchange(expert_out)
-    grad_down_local = jnp.dot(mixed_low.T, arrived_grads, preferred_element_type=F32)
-    grad_up_local = jnp.dot(arrived.T, grad_hidden, preferred_element_type=F32)
 
     upstream = cotangent.astype(F32)
     grad_normed_ffn = jnp.dot(any_slot, back_rows, preferred_element_type=F32)
@@ -625,10 +814,10 @@
     )
     sum_b = sum_b[:PIECE]
     up_sum = lax.psum_scatter(
-        grad_up_local[None].astype(BF16), "shard", scatter_dimension=1, tiled=True
+        grad_up_local[None], "shard", scatter_dimension=1, tiled=True
     ).astype(F32)
     down_sum = lax.psum_scatter(
-        grad_down_local[None].astype(BF16), "shard", scatter_dimension=2, tiled=True
+        grad_down_local[None], "shard", scatter_dimension=2, tiled=True
     ).astype(F32)
     return (
         output,

time: 537 us -> 528 us (0.983)
  Pallas kernels: 110 us -> 249 us
  blocking collectives: 63.6 us -> 0 us
  matrix products: 154 us -> 94.1 us
  waiting for transfers between devices: 74 us -> 46.1 us
  starting transfers between devices: 18.6 us -> 26.7 us
  local copies, waits for them, and re-layouts: 70.1 us -> 64.4 us
    pallas_call x0 -> x1, Pallas kernels: none -> 137 us  [run_experts(): pl.pallas_call(experts_kernel, name='experts', out_shape=(blocks, blocks,...]
    dot_general x6 -> x0, matrix products: 64.6 us -> none  [the longest x1 14 us: body(): jnp.dot(arrived_grads, down_proj[0].T, preferred_element_type=F32)]
    all_to_all x1 -> x0, blocking collectives: 63.6 us -> none  [exchange(): lax.all_to_all(rows.reshape(EXPERTS, CAP, D), 'expert', split_axis=0, con...]
    all_to_all x3 -> x2, waiting for transfers between devices: 73.7 us -> 39.4 us  [exchange(): lax.all_to_all(rows.reshape(EXPERTS, CAP, D), 'expert', split_axis=0, con...]
    all_to_all x3 -> x2, starting transfers between devices: 18.1 us -> 26.5 us  [exchange(): lax.all_to_all(rows.reshape(EXPERTS, CAP, D), 'expert', split_axis=0, con...]
    all_gather x1, waiting for transfers between devices: 0.16 us -> 6.12 us  [body(): group_kv = lax.all_gather(local_kv, 'shard', axis=0, tiled=True)]
    unnamed x147 -> x127, local copies, waits for them, and re-layouts: 42.4 us -> 38.8 us
  transfers between devices with their start and end apart: 7 -> 6, of which waited for: 4 -> 3; matrix products, arithmetic and copies ran while one was open for 32% -> 22% of each run, Pallas kernels for 11% -> 11%
where the time goes in v2:
time: 528 us; the launch traced here: 520 us
  Pallas kernels  249 us (47%)
  matrix products  94.1 us (18%)
  local copies, waits for them, and re-layouts  64.4 us (12%)
  waiting for transfers between devices  46.1 us (9%)
  starting transfers between devices  26.7 us (5%)
  other arithmetic  24.6 us (5%)
  between operations  14.9 us (3%)
    pallas_call x1, Pallas kernels, run_experts(): pl.pallas_call(experts_kernel, name='experts', out_shape=(blocks, blocks,...  137 us
    pallas_call x1, Pallas kernels, scatter_sums(): pl.pallas_call(scatter_kernel, name='scatter_sums', out_shape=(jax.ShapeD...  59.5 us
    pallas_call x1, Pallas kernels, gather_weights(): pl.pallas_call(gather_kernel, name='gather_weights', out_shape=(jax.Shape...  52.5 us
    all_to_all x2, waiting for transfers between devices, exchange(): lax.all_to_all(rows.reshape(EXPERTS, CAP, D), 'expert', split_axis=0, con...  39.4 us
    unnamed x127, local copies, waits for them, and re-layouts  38.8 us
    all_to_all x2, starting transfers between devices, exchange(): lax.all_to_all(rows.reshape(EXPERTS, CAP, D), 'expert', split_axis=0, con...  26.5 us
  transfers between devices with their start and end apart: 6, of which 3 were waited for; matrix products, arithmetic and copies ran while one was open for 22% of the time, Pallas kernels for 11%

profile of v2, /device:TPU:0, one launch (start us, length us, event | category | flops | bytes accessed | tf_op | source)
XLA Modules:
  0.0 519.9 jit_solution(18244930134021578676)
XLA Ops:
  7.3 1.4 fusion.34
  11.8 52.5 %gather_weights.1 = (bf16[4,4,2,48,2048]{4,3,2,1,0:T(8,128)(2,1)S(1)}, bf16[4,4,2,48,1664]{4,3,2,1,0:T(8,128)(2,1)S(1)}) custom-call(bf16[16,3712]{1,0:T(8,128)(2,1)S(1)} %pad.4.pack), custom_call_target="tpu_custom_call" | custom-call | bytes 24000000 | tf_op jit(solution)/shard_map/gather_weights/pallas_call | solution.py:187
  64.3 2.7 copy-done.3
  66.9 2.2 copy-done.2
  69.7 4.6 fusion.70
  80.8 3.6 fusion.5
  84.4 5.3 %all-to-all-start = ((bf16[32,48,1536]{2,1,0:T(8,128)(2,1)}), bf16[32,48,1536]{2,1,0:T(8,128)(2,1)}, u32[]{:S(2)}, u32[]{:S(2)}) async-start(bf16[32,48,1536]{2,1,0:T(8,128)(2,1)} %bitcast.152), calls=%async_computation | async-start | bytes 9437184 | tf_op jit(solution)/shard_map/all_to_all | solution.py:623
  89.8 1.5 slice.116
  91.4 1.6 copy.98
  93.0 1.6 subtract_convert_fusion.1
  96.5 6.1 %all-gather.2.cloned.1.call-done = bf16[1024,512]{1,0:T(8,128)(2,1)} async-done(((bf16[256,512]{1,0:T(8,128)(2,1)}), bf16[1024,512]{1,0:T(8,128)(2,1)}) %all-gather.2.cloned.1.call-update) | async-done | bytes 1048592 | tf_op jit(solution)/shard_map/all_gather | solution.py:692
  102.6 2.2 fusion.83
  107.3 2.0 reshape.258
  109.2 10.4 %fusion.86 = (f32[2,6,256]{2,1,0:T(8,128)S(1)}, f32[2,6,256,1024]{2,3,1,0:T(8,128)}) fusion(pred[256,1024]{0,1:T(8,128)(4,1)} %fusion.50, bf16[1024,2,128,1]{0,2,3,1:T(8,128)(2,1)} %copy.123, bf16[256,2,6,64]{3,0,2,1:T(8,128)(2,1)S(1)} %bitcast.155, bf16[256,2,6,64]{3,0,2,1:T(8,128)(2,1)S(1)} %bitcast.153), kind=kOutput, calls=%fused_computation.155 | convolution fusion | flops 819463168 | bytes 14168064 | tf_op jit(solution)/shard_map/sub | solution.py:708
  119.6 6.0 %fusion.38 = bf16[2,128,6,256]{3,1,2,0:T(8,128)(2,1)S(1)} fusion(bf16[1024,2,128,1]{2,1,0,3:T(2,128)(2,1)} %bitcast.172, f32[2,6,256,1024]{2,3,1,0:T(8,128)} %get-tuple-element.52, f32[2,6,256]{2,1,0:T(8,128)S(1)} %get-tuple-element.51), kind=kOutput, calls=%fused_computation.66 | convolution fusion | flops 811991040 | bytes 13905920 | tf_op jit(solution)/shard_map/grtk,kgd->tgrd/dot_general | solution.py:712
  125.7 1.6 multiply_reduce_fusion.2
  128.5 3.6 convolution_convert_fusion.2
  132.1 16.7 %all-to-all-done.grads_in = bf16[32,48,1536]{2,1,0:T(8,128)(2,1)} async-done(((bf16[32,48,1536]{2,1,0:T(8,128)(2,1)}), bf16[32,48,1536]{2,1,0:T(8,128)(2,1)}, u32[]{:S(2)}, u32[]{:S(2)}) %all-to-all-start) | async-done | bytes 4718624 | tf_op jit(solution)/shard_map/all_to_all | solution.py:623
  148.7 137.2 %experts.1 = (bf16[32,48,1536]{2,1,0:T(8,128)(2,1)}, bf16[32,48,1536]{2,1,0:T(8,128)(2,1)}, bf16[1536,1536]{1,0:T(8,128)(2,1)}, bf16[768,1536]{1,0:T(8,128)(2,1)}) custom-call(bf16[32,48,1536]{2,1,0:T(8,128)(2,1)} %bitcast.145, bf16[32,48,1536]{2,1,0:T(8,128)(2,1)} %all-to-all-done.grads_in, bf16[1,1536,1536]{2,1,0:T(8,128)(2,1)} %gate_up.1, ...), custom_call_target="tpu_custom_call" | custom-call | flops 32999999488 | bytes 60000000 | tf_op jit(solution)/shard_map/experts/pallas_call | solution.py:543
  286.0 5.2 %multiply_reduce_fusion = (bf16[1536]{0:T(1024)(128)(2,1)}, f32[256]{0:T(256)S(1)}, f32[256,1536]{1,0:T(8,128)S(1)}) fusion(f32[256,1536]{1,0:T(8,128)} %copy-done.8, f32[256]{0:T(256)S(1)} %fusion.76, f32[1536]{0:T(1024)S(1)} %get-tuple-element.31, bf16[32,48,1536]{2,1,0:T(8,128)(2,1)} %get-tuple-element.20, f32[256,32]{0,1:T(8,128)S(1)} %convolution_select_fusion), kind=kOutput, calls=%fused_computation.58 | convolution fusion | flops 1210710272 | bytes 7908352 | tf_op jit(solution)/shard_map/dot_general | solution.py:732
  292.9 2.3 fusion.23
  296.6 6.9 %fusion.45 = bf16[2,128,1024]{2,1,0:T(8,128)(2,1)S(1)} fusion(bf16[256,2,6,128]{0,3,2,1:T(8,128)(2,1)S(1)} %bitcast.165, f32[2,6,256,1024]{2,3,1,0:T(8,128)} %get-tuple-element.52, f32[2,6,256]{2,1,0:T(8,128)S(1)} %get-tuple-element.51), kind=kOutput, calls=%fused_computation.70 | convolution fusion | flops 811859968 | bytes 13905920 | tf_op jit(solution)/shard_map/grtk,tgrd->kgd/dot_general | solution.py:756
  303.5 8.9 %fusion.1 = (f32[2,6,256]{2,1,0:T(8,128)S(1)}, f32[2,1024,256,6]{2,1,3,0:T(8,128)}) fusion(f32[2,6,256,1024]{2,3,1,0:T(8,128)} %get-tuple-element.52, f32[2,6,256]{2,1,0:T(8,128)S(1)} %get-tuple-element.51, bf16[256,2,6,128]{0,3,2,1:T(8,128)(2,1)S(1)} %bitcast.166, bf16[1024,2,128,1]{2,1,0,3:T(2,128)(2,1)S(1)} %bitcast.173), kind=kOutput, calls=%fused_computation.3 | convolution fusion | flops 814740480 | bytes 26501120 | tf_op jit(solution)/shard_map/tgrd,kgd->grtk/dot_general | solution.py:744
  312.5 6.6 %fusion.3 = bf16[2,6,256,1024]{2,3,1,0:T(8,128)(2,1)S(1)} fusion(f32[2,1024,256,6]{2,1,3,0:T(8,128)} %get-tuple-element.59, f32[2,6,256]{2,1,0:T(8,128)S(1)} %get-tuple-element.58, f32[2,6,256,1024]{2,3,1,0:T(8,128)S(1)} %bitcast.147, f32[2,6,256]{2,1,0:T(8,128)S(1)} %get-tuple-element.51), kind=kLoop, calls=%fused_computation.5 | loop fusion | flops 12582912 | bytes 31481856 | tf_op jit(solution)/shard_map/convert_element_type | solution.py:749
  319.1 2.5 fusion.48
  323.8 8.4 %copy.138 = bf16[1,768,1536]{1,0,2:T(2,128)(2,1)} copy(bf16[1,768,1536]{2,1,0:T(8,128)(2,1)S(1)} %bitcast.159) | data formatting | bytes 4718592
  332.3 4.1 copy.154
  337.0 21.2 %all-to-all-start.1 = ((bf16[32,48,1536]{2,1,0:T(8,128)(2,1)}), bf16[32,48,1536]{2,1,0:T(8,128)(2,1)}, u32[]{:S(2)}, u32[]{:S(2)}) async-start(bf16[32,48,1536]{2,1,0:T(8,128)(2,1)} %get-tuple-element.19), calls=%async_computation.1 | async-start | bytes 9437184 | tf_op jit(solution)/shard_map/all_to_all | solution.py:623
  359.6 3.9 convolution_multiply_fusion.1
  365.1 3.6 convolution_convert_fusion.1
  368.7 1.6 fusion.84
  371.1 1.7 copy.143
  372.8 1.8 copy.142
  377.0 1.7 copy.114
  378.6 6.8 %fusion.30 = (bf16[1536]{0:T(1024)(128)(2,1)}, f32[256]{0:T(256)}, f32[256,1536]{1,0:T(8,128)}) fusion(bf16[256,1536]{1,0:T(8,128)(2,1)S(1)} %copy-done.5, f32[256]{0:T(256)S(1)} %fusion.75, f32[1536]{0:T(1024)S(1)} %get-tuple-element.32, bf16[1536,2048]{1,0:T(8,128)(2,1)} %bitcast.143, bf16[256,256]{0,1:T(8,128)(2,1)} %get-tuple-element.46, ...), kind=kOutput, calls=%fused_computation.51 | convolution fusion | flops 1616509184 | bytes 9710592 | tf_op jit(solution)/shard_map/dot_general | solution.py:778
  385.4 2.1 concatenate.60
  388.8 5.6 %convolution_convert_fusion = bf16[1536,2048]{1,0:T(8,128)(2,1)} fusion(bf16[256,256]{0,1:T(8,128)(2,1)} %get-tuple-element.46, bf16[256,256]{0,1:T(8,128)(2,1)} %bitcast.170, bf16[256,1536]{0,1:T(8,128)(2,1)S(1)} %bitcast.158, bf16[256,1536]{1,0:T(8,128)(2,1)S(1)} %copy-done.5, f32[1536]{0:T(1024)S(1)} %get-tuple-element.32, f32[256]{0:T(256)S(1)} %fusion.75), kind=kOutput, calls=%fused_computation.10 | convolution fusion | flops 1618477056 | bytes 8133632 | tf_op jit(solution)/shard_map/dot_general | solution.py:777
  394.4 22.7 %all-to-all-done.1 = bf16[32,48,1536]{2,1,0:T(8,128)(2,1)} async-done(((bf16[32,48,1536]{2,1,0:T(8,128)(2,1)}), bf16[32,48,1536]{2,1,0:T(8,128)(2,1)}, u32[]{:S(2)}, u32[]{:S(2)}) %all-to-all-start.1) | async-done | bytes 4718624 | tf_op jit(solution)/shard_map/all_to_all | solution.py:623
  417.1 4.1 fusion.88
  426.5 2.9 copy-done
  429.4 2.4 copy-done.1
  431.8 59.5 %scatter_sums.1 = (f32[16,2048]{1,0:T(8,128)S(1)}, f32[16,1664]{1,0:T(8,128)S(1)}) custom-call(bf16[4,4,2,48,2048]{4,3,2,1,0:T(8,128)(2,1)S(1)} %bitcast.130, bf16[4,4,2,48,1536]{4,3,2,1,0:T(8,128)(2,1)S(1)} %bitcast.131, bf16[4,4,2,48,128]{4,3,2,1,0:T(8,128)(2,1)S(1)} %maximum_maximum_fusion.gs), custom_call_target="tpu_custom_call" | custom-call | bytes 24000000 | tf_op jit(solution)/shard_map/scatter_sums/pallas_call | solution.py:365
  492.6 3.2 fusion.22
  496.5 3.9 convolution_bitcast_fusion.1
  500.3 4.7 fusion.21
  505.0 1.7 reshape_bitcast_fusion
  506.7 1.7 copy.139
  509.5 3.0 convert_element_type.126
  (193 shorter events, 37.4 us)
Async XLA Ops:
  7.2 95.4 %all-gather.2.cloned.1.call-start = ((), (), s32[]{:S(2)}) async-start(), calls=%async_computation.5 | async-start | bytes 1310720 | tf_op jit(solution)/shard_map/all_gather | solution.py:692
  7.2 62.4 %copy-start.5 = (bf16[256,1536]{1,0:T(8,128)(2,1)S(1)}, bf16[256,1536]{1,0:T(8,128)(2,1)}, u32[]{:S(2)}) copy-start(bf16[256,1536]{1,0:T(8,128)(2,1)} %param.11) | copy-start | bytes 2359300
  64.2 2.7 copy-start.3
  69.7 6.0 %copy-start.51 = (s32[1,4]{1,0:T(1,128)S(1)}, s32[1,4]{1,0:T(1,128)}, u32[]{:S(2)}) copy-start(s32[1,4]{1,0:T(1,128)} %param.12) | copy-start | bytes 52
  76.4 16.7 %copy-start.24 = (f32[256,64]{0,1:T(8,128)}, f32[256,64]{0,1:T(8,128)S(1)}, u32[]{:S(2)}) copy-start(f32[256,64]{0,1:T(8,128)S(1)} %get-tuple-element.49) | copy-start | bytes 196612
  76.4 16.7 %copy-start.26 = (f32[256,64]{0,1:T(8,128)}, f32[256,64]{0,1:T(8,128)S(1)}, u32[]{:S(2)}) copy-start(f32[256,64]{0,1:T(8,128)S(1)} %get-tuple-element.50) | copy-start | bytes 196612
  76.6 3.2 copy-start.23
  77.6 3.2 copy-start.28
  79.8 4.6 copy-start.37
  80.0 206.0 %copy-start.40 = (f32[256,32]{0,1:T(8,128)}, f32[256,32]{0,1:T(8,128)S(1)}, u32[]{:S(2)}) copy-start(f32[256,32]{0,1:T(8,128)S(1)} %convolution_select_fusion) | copy-start | bytes 98308
  80.4 4.0 copy-start.18
  80.4 4.0 copy-start.43
  80.4 4.0 copy-start.34
  84.4 64.3 %all-to-all-start = ((bf16[32,48,1536]{2,1,0:T(8,128)(2,1)}), bf16[32,48,1536]{2,1,0:T(8,128)(2,1)}, u32[]{:S(2)}, u32[]{:S(2)}) async-start(bf16[32,48,1536]{2,1,0:T(8,128)(2,1)} %bitcast.152), calls=%async_computation | async-start | bytes 9437184 | tf_op jit(solution)/shard_map/all_to_all | solution.py:623
  89.8 278.9 %reduce-scatter.6.cloned.1.call-start = ((), (), s32[]{:S(2)}) async-start(), calls=%async_computation.6 | async-start | bytes 1310720 | tf_op jit(solution)/shard_map/reduce_scatter | solution.py:762
  95.0 14.2 %copy-start.11 = (bf16[256,12,64]{2,0,1:T(8,128)(2,1)}, bf16[256,12,64]{2,0,1:T(8,128)(2,1)S(1)}, u32[]{:S(2)}) copy-start(bf16[256,12,64]{2,0,1:T(8,128)(2,1)S(1)} %copy.99) | copy-start | bytes 1179652
  95.4 13.8 %copy-start.13 = (bf16[256,12,64]{2,0,1:T(8,128)(2,1)}, bf16[256,12,64]{2,0,1:T(8,128)(2,1)S(1)}, u32[]{:S(2)}) copy-start(bf16[256,12,64]{2,0,1:T(8,128)(2,1)S(1)} %copy.100) | copy-start | bytes 1179652
  109.2 16.4 %slice-start = ((s8[5111808]{0:T(1024)(128)(4,1)}), s8[917504]{0:T(1024)(128)(4,1)S(1)}, s32[]{:S(2)}) async-start(s8[5111808]{0:T(1024)(128)(4,1)} %bitcast.135), calls=%async_computation.9 | async-start | bytes 1835008
  119.6 6.1 %slice-start.1 = ((s8[5111808]{0:T(1024)(128)(4,1)}), s8[4194304]{0:T(1024)(128)(4,1)S(1)}, s32[]{:S(2)}) async-start(s8[5111808]{0:T(1024)(128)(4,1)} %bitcast.135), calls=%async_computation.10 | async-start | bytes 8388608
  125.7 2.8 copy-start.19
  128.5 164.4 %slice-start.2 = ((s8[5111808]{0:T(1024)(128)(4,1)}), s8[917504]{0:T(1024)(128)(4,1)S(1)}, s32[]{:S(2)}) async-start(s8[5111808]{0:T(1024)(128)(4,1)} %bitcast.138), calls=%async_computation.11 | async-start | bytes 1835008
  148.7 144.2 %slice-start.3 = ((s8[5111808]{0:T(1024)(128)(4,1)}), s8[4194304]{0:T(1024)(128)(4,1)S(1)}, s32[]{:S(2)}) async-start(s8[5111808]{0:T(1024)(128)(4,1)} %bitcast.138), calls=%async_computation.12 | async-start | bytes 8388608
  286.0 5.3 %copy-start.9 = (f32[256,1536]{1,0:T(8,128)S(1)}, f32[256,1536]{1,0:T(8,128)}, u32[]{:S(2)}) copy-start(f32[256,1536]{1,0:T(8,128)} %copy-done.8) | copy-start | bytes 4718596
  286.0 5.3 %copy-start.29 = (bf16[256,1536]{1,0:T(8,128)(2,1)S(1)}, bf16[256,1536]{1,0:T(8,128)(2,1)}, u32[]{:S(2)}) copy-start(bf16[256,1536]{1,0:T(8,128)(2,1)} %param.21) | copy-start | bytes 2359300
  296.6 6.9 %copy-start.39 = (bf16[1024,2,128]{2,1,0:T(2,128)(2,1)S(1)}, bf16[1024,2,128]{2,1,0:T(2,128)(2,1)}, u32[]{:S(2)}) copy-start(bf16[1024,2,128]{2,1,0:T(2,128)(2,1)} %reshape.258) | copy-start | bytes 1572868
  296.6 15.9 %slice-start.4 = ((s8[12582912]{0:T(1024)(128)(4,1)}), s8[4194304]{0:T(1024)(128)(4,1)S(1)}, s32[]{:S(2)}) async-start(s8[12582912]{0:T(1024)(128)(4,1)} %bitcast.146), calls=%async_computation.13 | async-start | bytes 8388608
  296.6 15.9 %slice-start.5 = ((s8[12582912]{0:T(1024)(128)(4,1)}), s8[4194304]{0:T(1024)(128)(4,1)S(1)}, s32[]{:S(2)}) async-start(s8[12582912]{0:T(1024)(128)(4,1)} %bitcast.146), calls=%async_computation.14 | async-start | bytes 8388608
  303.5 9.0 %slice-start.6 = ((s8[12582912]{0:T(1024)(128)(4,1)}), s8[4194304]{0:T(1024)(128)(4,1)S(1)}, s32[]{:S(2)}) async-start(s8[12582912]{0:T(1024)(128)(4,1)} %bitcast.146), calls=%async_computation.15 | async-start | bytes 8388608
  312.5 6.6 %copy-start.12 = (bf16[256,12,64]{2,0,1:T(8,128)(2,1)S(1)}, bf16[256,12,64]{2,0,1:T(8,128)(2,1)}, u32[]{:S(2)}) copy-start(bf16[256,12,64]{2,0,1:T(8,128)(2,1)} %copy-done.11) | copy-start | bytes 1179652
  312.5 6.6 %copy-start.14 = (bf16[256,12,64]{2,0,1:T(8,128)(2,1)S(1)}, bf16[256,12,64]{2,0,1:T(8,128)(2,1)}, u32[]{:S(2)}) copy-start(bf16[256,12,64]{2,0,1:T(8,128)(2,1)} %copy-done.13) | copy-start | bytes 1179652
  319.1 2.6 copy-start.4
  322.8 182.2 %reduce-scatter.10.cloned.1.call-start = ((), (), s32[]{:S(2)}) async-start(), calls=%async_computation.8 | async-start | bytes 2949120
  336.4 173.1 %reduce-scatter.8.cloned.1.call-start = ((), (), s32[]{:S(2)}) async-start(), calls=%async_computation.7 | async-start | bytes 5898240 | tf_op jit(solution)/shard_map/reduce_scatter | solution.py:816
  337.0 21.8 %copy-start.48 = (bf16[1536]{0:T(1024)(128)(2,1)S(1)}, bf16[1536]{0:T(1024)(128)(2,1)}, u32[]{:S(2)}) copy-start(bf16[1536]{0:T(1024)(128)(2,1)} %get-tuple-element.25) | copy-start | bytes 9220
  337.0 22.5 %copy-start.16 = (bf16[1024,2,128,1]{0,2,3,1:T(8,128)(2,1)S(1)}, bf16[1024,2,128,1]{0,2,3,1:T(8,128)(2,1)}, u32[]{:S(2)}) copy-start(bf16[1024,2,128,1]{0,2,3,1:T(8,128)(2,1)} %copy.123) | copy-start | bytes 1572868
  337.0 80.1 %all-to-all-start.1 = ((bf16[32,48,1536]{2,1,0:T(8,128)(2,1)}), bf16[32,48,1536]{2,1,0:T(8,128)(2,1)}, u32[]{:S(2)}, u32[]{:S(2)}) async-start(bf16[32,48,1536]{2,1,0:T(8,128)(2,1)} %get-tuple-element.19), calls=%async_computation.1 | async-start | bytes 9437184 | tf_op jit(solution)/shard_map/all_to_all | solution.py:623
  359.5 3.9 copy-start.25
  359.6 3.9 copy-start.27
  417.1 4.2 copy-start.41
  421.3 4.2 copy-start.20
  426.5 2.9 copy-start
  431.8 60.8 %copy-start.21 = (f32[256,1536]{1,0:T(8,128)S(1)}, f32[256,1536]{1,0:T(8,128)}, u32[]{:S(2)}) copy-start(f32[256,1536]{1,0:T(8,128)} %get-tuple-element.60) | copy-start | bytes 4718596
  431.8 60.8 %copy-start.33 = (f32[256,32]{0,1:T(8,128)S(1)}, f32[256,32]{0,1:T(8,128)}, u32[]{:S(2)}) copy-start(f32[256,32]{0,1:T(8,128)} %copy-done.32) | copy-start | bytes 98308
  431.8 60.8 %copy-start.36 = (f32[256,32]{0,1:T(8,128)S(1)}, f32[256,32]{0,1:T(8,128)}, u32[]{:S(2)}) copy-start(f32[256,32]{0,1:T(8,128)} %copy-done.34) | copy-start | bytes 98308
  431.8 60.8 %copy-start.47 = (f32[256]{0:T(256)S(1)}, f32[256]{0:T(256)}, u32[]{:S(2)}) copy-start(f32[256]{0:T(256)} %copy-done.46) | copy-start | bytes 3076
  431.8 60.8 %copy-start.50 = (f32[256]{0:T(256)S(1)}, f32[256]{0:T(256)}, u32[]{:S(2)}) copy-start(f32[256]{0:T(256)} %multiply_multiply_fusion) | copy-start | bytes 3076
  492.6 3.8 copy-start.42
  496.5 3.9 copy-start.10
  (17 other events, 24.0 us)
Sparse Core Ops, SparseCore 0:
  78.5 24.0 all-gather.1
  323.0 39.0 reduce-scatter.5
  365.2 31.5 reduce-scatter.9
  399.2 50.7 reduce-scatter.7

commit v3 on v2

--- a/solution.py
+++ b/solution.py
@@ -94,7 +94,23 @@
     return jnp.where(same, 1.0, 0.0).astype(BF16)
 
 
-def gather_kernel(pack, full_a, full_b, xbuf, own_a, own_b, send, recv, local):
+def route(top_experts, named, any_slot):
+    lanes = iota((COUNT, 128), 1)
+    for k in range(TOP):
+        hit = jnp.where(top_experts[:, k : k + 1] == lanes, 1.0, 0.0)
+        named[...] = hit if k == 0 else named[...] + hit
+    earlier = hot(iota((COUNT, COUNT), 1) < iota((COUNT, COUNT), 0))
+    slot_of = mul(earlier, named[...].astype(BF16))
+    slot_of = jnp.where(named[...] > 0, slot_of, -1.0).astype(BF16)
+    expand = hot(iota((128, ROWS), 0) == iota((128, ROWS), 1) // CAP)
+    place_of = (iota((1, ROWS), 1) % CAP).astype(F32)
+    any_slot[...] = hot(mul(slot_of, expand) == place_of)
+
+
+def gather_kernel(
+    pack, top_experts, cotangent, full_a, full_b, named, any_slot, dy_rows,
+    xbuf, own_a, own_b, send, recv, local,
+):
     y, z, c, x = place()
     near = neighbours(y, z, c, x)
     greet(everyone_near(near))
@@ -134,6 +150,7 @@
         j["core"] = [link.push(j["own"], here, near["core"])]
         j["local"] = pltpu.make_async_copy(j["own"], here, local.at[j["i"]])
         j["local"].start()
+    route(top_experts, named, any_slot)
     for j in jobs:
         plus, minus = near[j["close"]]
         left, right = (j["p"] + 3) % 4, (j["p"] + 1) % 4
@@ -156,6 +173,13 @@
         j["up"] = link.push(line, line, plus)
         j["down"] = link.push(line, line, minus)
         j["core"].append(link.push(block, block, near["core"]))
+
+    def dy_tile(j, carry):
+        lanes = pl.ds(pl.multiple_of(j * TILE, TILE), TILE)
+        dy_rows[lanes, :] = mul(any_slot[:, lanes], cotangent[...], TN).astype(BF16)
+        return carry
+
+    lax.fori_loop(0, ROWS // TILE, dy_tile, 0)
     for j in jobs:
         plus, minus = near[j["far"]]
         left, right = (j["q"] + 3) % 4, (j["q"] + 1) % 4
@@ -182,7 +206,9 @@
     link.drain()
 
 
-def gather_weights(pack):
+def gather_weights(pack, top_experts, cotangent):
+    inside = pl.BlockSpec(memory_space=pltpu.VMEM)
+    anywhere = pl.BlockSpec(memory_space=pl.ANY)
     copies = 3 + 2 * 16
     return pl.pallas_call(
         gather_kernel,
@@ -190,9 +216,12 @@
         out_shape=(
             jax.ShapeDtypeStruct((4, 4, 2, BLOCK, WA), BF16),
             jax.ShapeDtypeStruct((4, 4, 2, BLOCK, WB), BF16),
-        ),
-        in_specs=[pl.BlockSpec(memory_space=pltpu.VMEM)],
-        out_specs=(pl.BlockSpec(memory_space=pl.ANY), pl.BlockSpec(memory_space=pl.ANY)),
+            jax.ShapeDtypeStruct((COUNT, 128), F32),
+            jax.ShapeDtypeStruct((COUNT, ROWS), BF16),
+            jax.ShapeDtypeStruct((ROWS, D), BF16),
+        ),
+        in_specs=[inside] * 3,
+        out_specs=(anywhere, anywhere, inside, inside, inside),
         scratch_shapes=[
             pltpu.VMEM((4, PADDED, WA + WB), BF16),
             pltpu.VMEM((BLOCK, WA), BF16),
@@ -202,10 +231,10 @@
             pltpu.SemaphoreType.DMA((2,)),
         ],
         compiler_params=pltpu.CompilerParams(
-            collective_id=0, has_side_effects=True, vmem_limit_bytes=16 * 1024 * 1024
+            collective_id=0, has_side_effects=True, vmem_limit_bytes=24 * 1024 * 1024
         ),
         cost_estimate=pl.CostEstimate(flops=0, bytes_accessed=24_000_000, transcendentals=0),
-    )(pack)
+    )(pack, top_experts, cotangent)
 
 
 def add_blocks(dst, far, start, count, sources):
@@ -220,9 +249,10 @@
 
 
 def scatter_kernel(
-    ga, gb, gs, out_a, out_b,
+    ga, gb, gs, up_in, down_in, up_far, down_far, out_a, out_b, up_out, down_out,
     core_a, core_b, mine_a, mine_b, one_a, one_b, two_a, two_b,
     half_a0, half_a1, half_b0, half_b1, last_a, last_b, xout, xin,
+    ups, downs, up_got, down_got, up_land, down_land,
     send, recv, local,
 ):
     y, z, c, x = place()
@@ -255,6 +285,33 @@
                 slots += 1
                 kept.start()
                 j[step].append((pushed, kept))
+
+    fetches = []
+    for i, d in enumerate((3, 1, 0)):
+        part = (x + d) % 4
+        up_rows = pl.ds(pl.multiple_of(part * UP_PART, UP_PART), UP_PART)
+        lanes = pl.ds(pl.multiple_of(part * DOWN_PART, 128), DOWN_PART)
+        fetches.append(pltpu.make_async_copy(up_in.at[up_rows], ups.at[i], local.at[slots]))
+        fetches.append(
+            pltpu.make_async_copy(down_in.at[:, lanes], downs.at[i], local.at[slots + 1])
+        )
+        slots += 2
+    fetches.append(pltpu.make_async_copy(up_far, up_got, local.at[slots]))
+    fetches.append(pltpu.make_async_copy(down_far, down_got, local.at[slots + 1]))
+    for fetch in fetches:
+        fetch.start()
+    for fetch in fetches:
+        fetch.wait()
+    sides = []
+    for i, peer in enumerate((near["x"][2], near["x"][0])):
+        up_rows = slice(i * UP_HALF, (i + 1) * UP_HALF)
+        down_rows = slice(i * DOWN_HALF, (i + 1) * DOWN_HALF)
+        ups[i, up_rows, :] = (ups[i, up_rows, :].astype(F32) + up_got[i].astype(F32)).astype(BF16)
+        downs[i, down_rows, :] = (
+            downs[i, down_rows, :].astype(F32) + down_got[i].astype(F32)
+        ).astype(BF16)
+        sides.append(link.push(ups.at[i], up_land.at[i], peer))
+        sides.append(link.push(downs.at[i], down_land.at[i], peer))
 
     def ready(j, step):
         for pushed, kept in j[step]:
@@ -340,11 +397,15 @@
         mine = mine + xin[d].astype(F32)
     out_a[...] = mine[:, :WA]
     out_b[...] = mine[:, WA:]
+    for push in sides:
+        push.wait_recv()
+    up_out[...] = ups[2].astype(F32) + up_land[0].astype(F32) + up_land[1].astype(F32)
+    down_out[...] = downs[2].astype(F32) + down_land[0].astype(F32) + down_land[1].astype(F32)
     link.drain()
 
 
-def scatter_sums(ga, gb, gs):
-    copies = 2 * (4 + 4 + 4) + 4 + 3
+def scatter_sums(*operands):
+    copies = 2 * (4 + 4 + 4) + 4 + 3 + 4
     vmem = pltpu.VMEM
     scratch = []
     for shape in ((4, 4), (4, 4), (2, 2), (2, 4)):
@@ -358,9 +419,15 @@
         vmem((2, BLOCK, WB), BF16),
         vmem((4, PADDED, WA + WB), BF16),
         vmem((3, PADDED, WA + WB), BF16),
+        vmem((3, UP_PART, 2 * FF), BF16),
+        vmem((3, FF, DOWN_PART), BF16),
+        vmem((2, UP_HALF, 2 * FF), BF16),
+        vmem((2, DOWN_HALF, DOWN_PART), BF16),
+        vmem((2, UP_PART, 2 * FF), BF16),
+        vmem((2, FF, DOWN_PART), BF16),
         pltpu.SemaphoreType.DMA((copies,)),
         pltpu.SemaphoreType.DMA((copies,)),
-        pltpu.SemaphoreType.DMA((12,)),
+        pltpu.SemaphoreType.DMA((20,)),
     ]
     return pl.pallas_call(
         scatter_kernel,
@@ -368,15 +435,17 @@
         out_shape=(
             jax.ShapeDtypeStruct((PADDED, WA), F32),
             jax.ShapeDtypeStruct((PADDED, WB), F32),
-        ),
-        in_specs=[pl.BlockSpec(memory_space=pl.ANY)] * 3,
-        out_specs=(pl.BlockSpec(memory_space=pltpu.VMEM), pl.BlockSpec(memory_space=pltpu.VMEM)),
+            jax.ShapeDtypeStruct((UP_PART, 2 * FF), F32),
+            jax.ShapeDtypeStruct((FF, DOWN_PART), F32),
+        ),
+        in_specs=[pl.BlockSpec(memory_space=pl.ANY)] * 7,
+        out_specs=(pl.BlockSpec(memory_space=pltpu.VMEM),) * 4,
         scratch_shapes=scratch,
         compiler_params=pltpu.CompilerParams(
             collective_id=1, has_side_effects=True, vmem_limit_bytes=40 * 1024 * 1024
         ),
         cost_estimate=pl.CostEstimate(flops=0, bytes_accessed=24_000_000, transcendentals=0),
-    )(ga, gb, gs)
+    )(*operands)
 
 
 NEAREST = (
@@ -400,9 +469,9 @@
 
 
 def experts_kernel(
-    sent, grads_in, gate_up, down, back, outs, up_grad, down_grad,
-    rows, grads, gu, dn, mixed, ghid, grow, eout,
-    send, recv, bsend, brecv, gsem, wsem, osem, own,
+    sent, gates_in, dy_in, gate_up, down, back, gate_back, outs, up_grad, down_grad,
+    rows, gates, dys, grads, gu, dn, mixed, ghid, grow, eout, dots,
+    send, recv, tsend, trecv, bsend, brecv, dsend, drecv, gsem, wsem, osem, own,
 ):
     y, z, c, x = place()
     me = (y * 4 + z) * 2 + c
@@ -418,24 +487,32 @@
             target = device((y + 4 - dy) % 4, (z + 4 - dz) % 4, core, x)
             slots.append((2 * s + b, source, target))
     greet([source for _, source, _ in slots[1:]])
-    links, back_links = [], []
-    for i, source, target in slots:
-        here = rows.at[pl.ds(i * CAP, CAP)]
+    links, tile_links, back_links, dot_links = [], [], [], []
+
+    def move(src, dst, where, i, sends, recvs, k):
         if i == 0:
-            copy = pltpu.make_async_copy(sent.at[me], here, own.at[0])
+            copy = pltpu.make_async_copy(src, dst, own.at[k])
         else:
             copy = pltpu.make_async_remote_copy(
-                src_ref=sent.at[target[0]], dst_ref=here, send_sem=send.at[i],
-                recv_sem=recv.at[i], device_id=target, device_id_type=MESH,
+                src_ref=src, dst_ref=dst, send_sem=sends.at[i],
+                recv_sem=recvs.at[i], device_id=where, device_id_type=MESH,
             )
         copy.start()
-        links.append(copy)
+        return copy
+
+    for i, source, target in slots:
+        tile_links.append(
+            move(gates_in.at[target[0]], gates.at[i], target, i, tsend, trecv, 0)
+        )
+        links.append(
+            move(sent.at[target[0]], rows.at[pl.ds(i * CAP, CAP)], target, i, send, recv, 1)
+        )
     incoming = []
     for copy in weights:
         copy.start()
     for i, source, target in slots:
         copy = pltpu.make_async_copy(
-            grads_in.at[source[0]], grads.at[pl.ds(i * CAP, CAP)], gsem.at[i]
+            dy_in.at[source[0]], dys.at[pl.ds(i * CAP, CAP)], gsem.at[i]
         )
         copy.start()
         incoming.append(copy)
@@ -443,16 +520,29 @@
         copy.wait()
     leaving = []
     per = len(slots) // CHUNKS
+    diagonal = lax.broadcasted_iota(jnp.int32, (CAP, 128), 0) == lax.broadcasted_iota(
+        jnp.int32, (CAP, 128), 1
+    )
     for k in range(CHUNKS):
         part = slots[k * per : (k + 1) * per]
         for i, source, target in part:
             incoming[i].wait()
             if i == 0:
+                tile_links[0].wait()
                 links[0].wait()
             else:
+                tile_links[i].wait_recv()
                 links[i].wait_recv()
         base = k * CHUNK
         block = pl.ds(base, CHUNK)
+
+        def scale_block(i, carry):
+            at = pl.ds(pl.multiple_of(i * CAP, CAP), CAP)
+            column = jnp.sum(jnp.where(diagonal, gates[i, 0:1, :], 0.0), axis=1, keepdims=True)
+            grads[at, :] = (dys[at, :].astype(F32) * column).astype(BF16)
+            return carry
+
+        lax.fori_loop(k * per, (k + 1) * per, scale_block, 0)
 
         def hidden_tile(j, carry, block=block):
             lanes = pl.ds(pl.multiple_of(j * TILE, TILE), TILE)
@@ -481,16 +571,9 @@
 
         lax.fori_loop(0, D // TILE, rows_tile, 0)
         for i, source, target in part:
-            here = grow.at[pl.ds(i * CAP, CAP)]
-            if i == 0:
-                copy = pltpu.make_async_copy(here, back.at[me], own.at[1])
-            else:
-                copy = pltpu.make_async_remote_copy(
-                    src_ref=here, dst_ref=back.at[me], send_sem=bsend.at[i],
-                    recv_sem=brecv.at[i], device_id=source, device_id_type=MESH,
-                )
-            copy.start()
-            back_links.append(copy)
+            back_links.append(
+                move(grow.at[pl.ds(i * CAP, CAP)], back.at[me], source, i, bsend, brecv, 2)
+            )
 
         def out_tile(j, carry, block=block):
             lanes = pl.ds(pl.multiple_of(j * TILE, TILE), TILE)
@@ -507,6 +590,21 @@
             copy.start()
             leaving.append(copy)
 
+        def dot_block(i, carry):
+            at = pl.ds(pl.multiple_of(i * CAP, CAP), CAP)
+            column = jnp.sum(
+                eout[at, :].astype(F32) * dys[at, :].astype(F32), axis=1, keepdims=True
+            )
+            row = jnp.sum(jnp.where(diagonal, column, 0.0), axis=0, keepdims=True)
+            dots[i] = jnp.broadcast_to(row, (8, 128))
+            return carry
+
+        lax.fori_loop(k * per, (k + 1) * per, dot_block, 0)
+        for i, source, target in part:
+            dot_links.append(
+                move(dots.at[i], gate_back.at[me], source, i, dsend, drecv, 3)
+            )
+
     def up_tile(j, carry):
         lanes = pl.ds(pl.multiple_of(j * TILE, TILE), TILE)
         up_grad[lanes, :] = lax.dot_general(
@@ -527,15 +625,14 @@
     for copy in leaving:
         copy.wait()
     back_links[0].wait()
-    for copy in back_links[1:]:
+    dot_links[0].wait()
+    for copy in back_links[1:] + dot_links[1:]:
         copy.wait_recv()
-    for copy in links[1:]:
+    for copy in tile_links[1:] + links[1:] + back_links[1:] + dot_links[1:]:
         copy.wait_send()
-    for copy in back_links[1:]:
-        copy.wait_send()
-
-
-def run_experts(sent, grads_in, gate_up, down):
+
+
+def run_experts(sent, gates_in, dy_in, gate_up, down):
     anywhere = pl.BlockSpec(memory_space=pl.ANY)
     inside = pl.BlockSpec(memory_space=pltpu.VMEM)
     blocks = jax.ShapeDtypeStruct((EXPERTS, CAP, D), BF16)
@@ -545,13 +642,16 @@
         name="experts",
         out_shape=(
             blocks,
+            jax.ShapeDtypeStruct((EXPERTS, 8, 128), F32),
             blocks,
             jax.ShapeDtypeStruct((D, 2 * FF), BF16),
             jax.ShapeDtypeStruct((FF, D), BF16),
         ),
-        in_specs=[anywhere] * 4,
-        out_specs=(anywhere, anywhere, inside, inside),
+        in_specs=[anywhere] * 5,
+        out_specs=(anywhere, anywhere, anywhere, inside, inside),
         scratch_shapes=[
+            vmem((ROWS, D), BF16),
+            vmem((EXPERTS, 8, 128), F32),
             vmem((ROWS, D), BF16),
             vmem((ROWS, D), BF16),
             vmem((D, 2 * FF), BF16),
@@ -560,54 +660,411 @@
             vmem((ROWS, 2 * FF), BF16),
             vmem((ROWS, D), BF16),
             vmem((ROWS, D), BF16),
-            dma((EXPERTS,)),
-            dma((EXPERTS,)),
-            dma((EXPERTS,)),
-            dma((EXPERTS,)),
-            dma((EXPERTS,)),
-            dma((2,)),
-            dma((EXPERTS,)),
-            dma((2,)),
+            vmem((EXPERTS, 8, 128), F32),
+        ]
+        + [dma((EXPERTS,))] * 8
+        + [dma((EXPERTS,)), dma((2,)), dma((EXPERTS,)), dma((4,))],
+        compiler_params=pltpu.CompilerParams(
+            collective_id=2, has_side_effects=True, vmem_limit_bytes=58 * 1024 * 1024
+        ),
+        cost_estimate=pl.CostEstimate(
+            flops=33_000_000_000, bytes_accessed=60_000_000, transcendentals=1_200_000
+        ),
+    )(sent, gates_in, dy_in, gate_up, down)
+
+
+UP_PART = D // 4
+UP_HALF = UP_PART // 2
+DOWN_PART = D // 4
+DOWN_HALF = FF // 2
+SCALE = HEAD_DIM ** (-0.5)
+GROUP_ROWS = 1024
+COUNT = 256
+NT = (((1,), (1,)), ((), ()))
+TN = (((0,), (0,)), ((), ()))
+
+
+def mul(a, b, dims=None):
+    if dims is None:
+        return jnp.dot(a, b, preferred_element_type=F32)
+    return lax.dot_general(a, b, dims, preferred_element_type=F32)
+
+
+def thirds(v):
+    high = v.astype(BF16)
+    rest = v - high.astype(F32)
+    middle = rest.astype(BF16)
+    return high, middle, (rest - middle.astype(F32)).astype(BF16)
+
+
+def exact(v, one_hot, dims=None):
+    return sum(mul(part, one_hot, dims) for part in thirds(v))
+
+
+def iota(shape, axis):
+    return lax.broadcasted_iota(jnp.int32, shape, axis)
+
+
+def hot(same):
+    return jnp.where(same, 1.0, 0.0).astype(BF16)
+
+
+def read_gains(small):
+    select = hot(iota((8, SMALL), 1) == iota((8, SMALL), 0) + EXPERTS)
+    select = jnp.where(iota((8, SMALL), 0) < 2, select, jnp.zeros_like(select))
+    return mul(select, small, NT), select
+
+
+def fill_bias(lengths, bias, x):
+    first = lengths[0, 0]
+    second = first + lengths[0, 1]
+    third = second + lengths[0, 2]
+    own = x * COUNT + iota((1, COUNT), 1)
+    own_seg = sum(jnp.where(own >= end, 1, 0) for end in (first, second, third))
+
+    def step(i, carry):
+        base = pl.multiple_of(i * COUNT, COUNT)
+        key = base + iota((COUNT, 1), 0)
+        key_seg = sum(jnp.where(key >= end, 1, 0) for end in (first, second, third))
+        allowed = (key_seg == own_seg) & (key <= own)
+        bias[pl.ds(base, COUNT), :] = jnp.where(allowed, 0.0, -1e30)
+        return carry
+
+    lax.fori_loop(0, GROUP_ROWS // COUNT, step, 0)
+
+
+def turn(v, cosd, sind):
+    return v * cosd + pltpu.roll(v, HEAD_DIM // 2, 1) * sind
+
+
+def forward_kernel(
+    lengths, tokens, wq_in, wb_in, any_slot, named, cosd, sind,
+    q_out, kv_out, attended, middle, normed, tops, totals, gates_out, tiles, dispatch,
+    wq, wb, kv, own_kv, bias, vt, nf, send, recv, local,
+):
+    y, z, c, x = place()
+    peers = [device(y, z, c, (x + d) % 4) for d in (1, 2, 3)]
+    loads = [
+        pltpu.make_async_copy(wq_in.at[:, pl.ds(D, 512)], wq.at[:, pl.ds(D, 512)], local.at[0]),
+        pltpu.make_async_copy(wq_in.at[:, pl.ds(0, D)], wq.at[:, pl.ds(0, D)], local.at[1]),
+        pltpu.make_async_copy(wb_in, wb, local.at[2]),
+    ]
+    for load in loads:
+        load.start()
+    greet(peers)
+    loads[2].wait()
+    small = wb[:, D:]
+    gains, _ = read_gains(small)
+    xf = tokens[...].astype(F32)
+    inverse = lax.rsqrt(jnp.mean(xf * xf, axis=1, keepdims=True) + norm_eps)
+    normed[...] = (xf * inverse * gains[0:1, :]).astype(BF16)
+    loads[0].wait()
+    for j in range(2):
+        part = mul(normed[...], wq[:, D + j * 256 : D + (j + 1) * 256])
+        if j == 0:
+            for h in range(2):
+                lanes = slice(h * HEAD_DIM, (h + 1) * HEAD_DIM)
+                own_kv[:, lanes] = turn(part[:, lanes], cosd[...], sind[...]).astype(BF16)
+        else:
+            own_kv[:, 256:512] = part.astype(BF16)
+    rows = pl.ds(pl.multiple_of(x * COUNT, COUNT), COUNT)
+    link = Links(send, recv)
+    pushes = [link.push(own_kv, kv.at[rows], peer) for peer in peers]
+    kv[rows, :] = own_kv[...]
+    fill_bias(lengths, bias, x)
+    loads[1].wait()
+
+    def query_tile(j, carry):
+        lanes = pl.ds(pl.multiple_of(j * 256, 256), 256)
+        part = mul(normed[...], wq[:, lanes])
+        q_out[:, lanes] = jnp.concatenate(
+            [turn(part[:, h * 128 : (h + 1) * 128], cosd[...], sind[...]) for h in range(2)],
+            axis=1,
+        ).astype(BF16)
+        return carry
+
+    lax.fori_loop(0, D // 256, query_tile, 0)
+
+    logits = jnp.where(named[...] > 0, mul(tokens[...], small), -jnp.inf)
+    weight = jnp.exp(logits - jnp.max(logits, axis=1, keepdims=True))
+    gates = weight / jnp.sum(weight, axis=1, keepdims=True)
+    gates_out[...] = gates
+    expand = hot(iota((128, ROWS), 0) == iota((128, ROWS), 1) // CAP)
+    spread = exact(gates, expand)
+    slot_gates = jnp.sum(any_slot[...].astype(F32) * spread, axis=0, keepdims=True)
+    expert_of = iota((EXPERTS, ROWS), 1) // CAP == iota((EXPERTS, ROWS), 0)
+    fold = hot(iota((128, ROWS), 1) % CAP == iota((128, ROWS), 0))
+    tile = exact(jnp.where(expert_of, slot_gates, 0.0), fold, NT)
+    tiles[...] = jnp.broadcast_to(tile[:, None, :], (EXPERTS, 8, 128))
+
+    for push in pushes:
+        push.wait_recv()
+    kv_out[...] = kv[...]
+    for g in range(HEADS_KV):
+        vt[g] = kv[:, 256 + g * 128 : 384 + g * 128].T
+    for g in range(HEADS_KV):
+
+        def head(i, carry, g=g):
+            h = g * REPEAT + i
+            lanes = pl.ds(pl.multiple_of(h * HEAD_DIM, HEAD_DIM), HEAD_DIM)
+            s = mul(kv[:, g * 128 : (g + 1) * 128], q_out[:, lanes], NT) * SCALE + bias[...]
+            top = jnp.max(s, axis=0, keepdims=True)
+            p = jnp.exp(s - top)
+            total = jnp.sum(p, axis=0, keepdims=True)
+            tops[pl.ds(h, 1), :] = top
+            totals[pl.ds(h, 1), :] = total
+            low = (p * (1.0 / total)).astype(BF16)
+            attended[:, lanes] = mul(vt[g], low).T.astype(BF16)
+            return carry
+
+        lax.fori_loop(0, REPEAT, head, 0)
+
+    def out_tile(j, carry):
+        lanes = pl.ds(pl.multiple_of(j * 256, 256), 256)
+        middle[:, lanes] = tokens[:, lanes].astype(F32) + mul(attended[...], wb[lanes, 0:D], NT)
+        return carry
+
+    lax.fori_loop(0, D // 256, out_tile, 0)
+    m = middle[...]
+    inverse = lax.rsqrt(jnp.mean(m * m, axis=1, keepdims=True) + norm_eps)
+    nf[...] = (m * inverse * gains[1:2, :]).astype(BF16)
+
+    def dispatch_tile(j, carry):
+        lanes = pl.ds(pl.multiple_of(j * 256, 256), 256)
+        dispatch[lanes, :] = mul(any_slot[:, lanes], nf[...], TN).astype(BF16)
+        return carry
+
+    lax.fori_loop(0, ROWS // 256, dispatch_tile, 0)
+    link.drain()
+
+
+def run_forward(lengths, tokens, wq, wb, any_slot, named, cosd, sind):
+    anywhere = pl.BlockSpec(memory_space=pl.ANY)
+    inside = pl.BlockSpec(memory_space=pltpu.VMEM)
+    vmem, dma = pltpu.VMEM, pltpu.SemaphoreType.DMA
+    shape = jax.ShapeDtypeStruct
+    return pl.pallas_call(
+        forward_kernel,
+        name="forward",
+        out_shape=(
+            shape((COUNT, D), BF16),
+            shape((GROUP_ROWS, 512), BF16),
+            shape((COUNT, D), BF16),
+            shape((COUNT, D), F32),
+            shape((COUNT, D), BF16),
+            shape((16, COUNT), F32),
+            shape((16, COUNT), F32),
+            shape((COUNT, 128), F32),
+            shape((EXPERTS, 8, 128), F32),
+            shape((ROWS, D), BF16),
+        ),
+        in_specs=[pl.BlockSpec(memory_space=pltpu.SMEM), inside, anywhere, anywhere] + [inside] * 4,
+        out_specs=(inside,) * 10,
+        scratch_shapes=[
+            vmem((D, WA), BF16),
+            vmem((D, WB), BF16),
+            vmem((GROUP_ROWS, 512), BF16),
+            vmem((COUNT, 512), BF16),
+            vmem((GROUP_ROWS, COUNT), F32),
+            vmem((HEADS_KV, HEAD_DIM, GROUP_ROWS), BF16),
+            vmem((COUNT, D), BF16),
+            dma((3,)),
+            dma((3,)),
+            dma((3,)),
         ],
         compiler_params=pltpu.CompilerParams(
-            collective_id=2, has_side_effects=True, vmem_limit_bytes=58 * 1024 * 1024
+            collective_id=3, has_side_effects=True, vmem_limit_bytes=48 * 1024 * 1024
         ),
         cost_estimate=pl.CostEstimate(
-            flops=33_000_000_000, bytes_accessed=60_000_000, transcendentals=1_200_000
-        ),
-    )(sent, grads_in, gate_up, down)
-
-
-def rms_scale(values, gain_vec):
-    return (
-        values * lax.rsqrt(jnp.mean(values * values, axis=-1, keepdims=True) + norm_eps) * gain_vec
+            flops=6_000_000_000, bytes_accessed=30_000_000, transcendentals=3_200_000
+        ),
+    )(lengths, tokens, wq, wb, any_slot, named, cosd, sind)
+
+
+def norm_grad(values, gain, grad):
+    inverse = lax.rsqrt(jnp.mean(values * values, axis=1, keepdims=True) + norm_eps)
+    unit = values * inverse
+    scaled = grad * gain
+    drop = jnp.mean(scaled * unit, axis=1, keepdims=True)
+    return inverse * (scaled - unit * drop), jnp.sum(grad * unit, axis=0, keepdims=True)
+
+
+def backward_kernel(
+    lengths, tokens, cotangent, any_slot, gates, gate_back, queries, kv_in, attended, middle,
+    normed, tops, totals, cosd, sind, wq_in, wb_in, back_in, up_in, down_in,
+    grad_tokens, grad_qkv, grad_out, grad_small, up_far, down_far,
+    wq, wb, back, bias, kt, gn, gmid, gb, gatt, gp, dk, dv, leave, land, send, recv, local,
+):
+    y, z, c, x = place()
+    peers = [device(y, z, c, (x + d) % 4) for d in (1, 2, 3)]
+    loads = [
+        pltpu.make_async_copy(back_in, back, local.at[0]),
+        pltpu.make_async_copy(wb_in, wb, local.at[1]),
+        pltpu.make_async_copy(wq_in, wq, local.at[2]),
+    ]
+    for load in loads:
+        load.start()
+    greet(peers)
+    link = Links(send, recv)
+    facing = (x + 2) % 4
+    pushes = []
+    for half, peer in ((0, peers[2]), (1, peers[0])):
+        up_rows = pl.ds(pl.multiple_of(facing * UP_PART + half * UP_HALF, UP_HALF), UP_HALF)
+        pushes.append(link.push(up_in.at[up_rows], up_far.at[half], peer))
+        lanes = pl.ds(pl.multiple_of(facing * DOWN_PART, 128), DOWN_PART)
+        down_rows = pl.ds(half * DOWN_HALF, DOWN_HALF)
+        pushes.append(link.push(down_in.at[down_rows, lanes], down_far.at[half], peer))
+    fill_bias(lengths, bias, x)
+    for g in range(HEADS_KV):
+        kt[g] = kv_in[:, g * 128 : (g + 1) * 128].T
+    loads[0].wait()
+
+    def ffn_tile(j, carry):
+        lanes = pl.ds(pl.multiple_of(j * 256, 256), 256)
+        gn[:, lanes] = mul(any_slot[...], back[:, lanes])
+        return carry
+
+    lax.fori_loop(0, D // 256, ffn_tile, 0)
+    loads[1].wait()
+    gains, select = read_gains(wb[:, D:])
+    moved, ffn_gain = norm_grad(middle[...], gains[1:2, :], gn[...])
+    gm = cotangent[...].astype(F32) + moved
+    gmid[...] = gm
+    gb[...] = gm.astype(BF16)
+
+    def att_tile(j, carry):
+        lanes = pl.ds(pl.multiple_of(j * 256, 256), 256)
+        gatt[:, lanes] = mul(gb[...], wb[:, lanes]).astype(BF16)
+        return carry
+
+    lax.fori_loop(0, D // 256, att_tile, 0)
+    kv_pushes = []
+    for g in range(HEADS_KV):
+        dk[...] = jnp.zeros_like(dk)
+        dv[...] = jnp.zeros_like(dv)
+
+        def head(i, carry, g=g):
+            h = g * REPEAT + i
+            lanes = pl.ds(pl.multiple_of(h * HEAD_DIM, HEAD_DIM), HEAD_DIM)
+            s = mul(kv_in[:, g * 128 : (g + 1) * 128], queries[:, lanes], NT) * SCALE + bias[...]
+            p = jnp.exp(s - tops[pl.ds(h, 1), :]) * (1.0 / totals[pl.ds(h, 1), :])
+            dv[...] += mul(p.astype(BF16), gatt[:, lanes])
+            t = p * mul(kv_in[:, 256 + g * 128 : 384 + g * 128], gatt[:, lanes], NT)
+            ds = (t - p * jnp.sum(t, axis=0, keepdims=True)).astype(BF16)
+            dk[...] += mul(ds, queries[:, lanes])
+            dq = mul(kt[g], ds).T * SCALE
+            gp[:, lanes] = turn(dq, cosd[...], -sind[...]).astype(BF16)
+            return carry
+
+        lax.fori_loop(0, REPEAT, head, 0)
+        leave[g, :, 0:128] = (dk[...] * SCALE).astype(BF16)
+        leave[g, :, 128:256] = dv[...].astype(BF16)
+        for d in (1, 2, 3):
+            away = pl.ds(pl.multiple_of(((x + d) % 4) * COUNT, COUNT), COUNT)
+            kv_pushes.append(link.push(leave.at[g, away], land.at[g, d - 1], peers[d - 1]))
+
+    def out_tile(j, carry):
+        lanes = pl.ds(pl.multiple_of(j * 256, 256), 256)
+        grad_out[lanes, :] = mul(gb[:, lanes], attended[...], TN).astype(BF16)
+        return carry
+
+    lax.fori_loop(0, D // 256, out_tile, 0)
+
+    expert_of = iota((EXPERTS, ROWS), 1) // CAP == iota((EXPERTS, ROWS), 0)
+    fold = hot(iota((128, ROWS), 1) % CAP == iota((128, ROWS), 0))
+    wide = exact(gate_back[:, 0, :], fold)
+    slot_grads = jnp.sum(jnp.where(expert_of, wide, 0.0), axis=0, keepdims=True)
+    expand = hot(iota((128, ROWS), 0) == iota((128, ROWS), 1) // CAP)
+    gate_grad = exact(any_slot[...].astype(F32) * slot_grads, expand, NT)
+    weighted = gates[...] * gate_grad
+    logit_grad = weighted - gates[...] * jnp.sum(weighted, axis=1, keepdims=True)
+    parts = thirds(logit_grad)
+    router_grad = sum(mul(tokens[...], part, TN) for part in parts)
+    small = wb[:, D:]
+
+    for push in kv_pushes:
+        push.wait_recv()
+    mine = pl.ds(pl.multiple_of(x * COUNT, COUNT), COUNT)
+    for g in range(HEADS_KV):
+        total = leave[g, mine, :].astype(F32)
+        for d in range(3):
+            total = total + land[g, d].astype(F32)
+        gp[:, D + g * 128 : D + (g + 1) * 128] = turn(
+            total[:, 0:128], cosd[...], -sind[...]
+        ).astype(BF16)
+        gp[:, D + 256 + g * 128 : D + 384 + g * 128] = total[:, 128:256].astype(BF16)
+    loads[2].wait()
+
+    def qkv_tile(j, carry):
+        lanes = pl.ds(pl.multiple_of(j * 256, 256), 256)
+        grad_qkv[lanes, :] = mul(normed[:, lanes], gp[...], TN).astype(BF16)
+        gn[:, lanes] = mul(gp[...], wq[lanes, :], NT)
+        return carry
+
+    lax.fori_loop(0, D // 256, qkv_tile, 0)
+    moved, attn_gain = norm_grad(tokens[...].astype(F32), gains[0:1, :], gn[...])
+    from_router = sum(mul(part, small, NT) for part in parts)
+    grad_tokens[...] = (gmid[...] + moved + from_router).astype(BF16)
+    both = jnp.where(
+        iota((8, D), 0) == 0, attn_gain, jnp.where(iota((8, D), 0) == 1, ffn_gain, 0.0)
     )
+    gain_columns = sum(mul(part, select, TN) for part in thirds(both))
+    grad_small[...] = (router_grad + gain_columns).astype(BF16)
+    for push in pushes:
+        push.wait_recv()
+    link.drain()
+
+
+def run_backward(*operands):
+    anywhere = pl.BlockSpec(memory_space=pl.ANY)
+    inside = pl.BlockSpec(memory_space=pltpu.VMEM)
+    vmem, dma = pltpu.VMEM, pltpu.SemaphoreType.DMA
+    shape = jax.ShapeDtypeStruct
+    return pl.pallas_call(
+        backward_kernel,
+        name="backward",
+        out_shape=(
+            shape((COUNT, D), BF16),
+            shape((D, WA), BF16),
+            shape((D, D), BF16),
+            shape((D, SMALL), BF16),
+            shape((2, UP_HALF, 2 * FF), BF16),
+            shape((2, DOWN_HALF, DOWN_PART), BF16),
+        ),
+        in_specs=[pl.BlockSpec(memory_space=pltpu.SMEM)] + [inside] * 14 + [anywhere] * 5,
+        out_specs=(inside,) * 4 + (anywhere,) * 2,
+        scratch_shapes=[
+            vmem((D, WA), BF16),
+            vmem((D, WB), BF16),
+            vmem((ROWS, D), BF16),
+            vmem((GROUP_ROWS, COUNT), F32),
+            vmem((HEADS_KV, HEAD_DIM, GROUP_ROWS), BF16),
+            vmem((COUNT, D), F32),
+            vmem((COUNT, D), F32),
+            vmem((COUNT, D), BF16),
+            vmem((COUNT, D), BF16),
+            vmem((COUNT, WA), BF16),
+            vmem((GROUP_ROWS, HEAD_DIM), F32),
+            vmem((GROUP_ROWS, HEAD_DIM), F32),
+            vmem((HEADS_KV, GROUP_ROWS, 256), BF16),
+            vmem((HEADS_KV, 3, COUNT, 256), BF16),
+            dma((10,)),
+            dma((10,)),
+            dma((3,)),
+        ],
+        compiler_params=pltpu.CompilerParams(
+            collective_id=4, has_side_effects=True, vmem_limit_bytes=58 * 1024 * 1024
+        ),
+        cost_estimate=pl.CostEstimate(
+            flops=13_000_000_000, bytes_accessed=50_000_000, transcendentals=3_200_000
+        ),
+    )(*operands)
 
 
 def rope_tables(position, half_dim):
     frequency = rope_base ** (-jnp.arange(half_dim, dtype=jnp.float32) / half_dim)
     angles = position.astype(jnp.float32)[:, None] * frequency[None, :]
-    return (jnp.cos(angles)[:, None, :], jnp.sin(angles)[:, None, :])
-
-
-def rotate(values, cosine, sine_tab):
-    half_dim = values.shape[-1] // 2
-    lower_half = values[..., :half_dim]
-    upper_half = values[..., half_dim:]
-    return jnp.concatenate(
-        [lower_half * cosine - upper_half * sine_tab, lower_half * sine_tab + upper_half * cosine],
-        axis=-1,
-    )
-
-
-def unrotate(grads_in, cosine, sine_tab):
-    half_dim = grads_in.shape[-1] // 2
-    lower_half = grads_in[..., :half_dim]
-    upper_half = grads_in[..., half_dim:]
-    return jnp.concatenate(
-        [lower_half * cosine + upper_half * sine_tab, upper_half * cosine - lower_half * sine_tab],
-        axis=-1,
-    )
+    return jnp.cos(angles), jnp.sin(angles)
 
 
 def seq_layout(seq_lens, row_ids):
@@ -628,8 +1085,6 @@
 def body(
     tokens, lengths, top_experts, w_qkv, w_out, gain_attn, gain_ffn, router, gate_up, down_proj, cotangent,
 ):
-    count = tokens.shape[0]
-    scale = HEAD_DIM ** (-0.5)
     pack = jnp.concatenate(
         [
             w_qkv,
@@ -642,183 +1097,49 @@
         axis=1,
     )
     pack = jnp.pad(pack, ((0, PADDED - PIECE), (0, 0)))
-    full_a, full_b = gather_weights(pack)
-    full_qkv = full_a.reshape(D, WA)
-    full_b = full_b.reshape(D, WB)
-    out_t = full_b[:, :D]
-    full_router = full_b[:, D : D + EXPERTS]
-    gains = full_b[:, D + EXPERTS : D + EXPERTS + 2].astype(F32).T
-    attn_g, ffn_g = gains[0], gains[1]
-
-    named = jnp.sum(
-        (top_experts[:, :, None] == jnp.arange(EXPERTS, dtype=jnp.int32)).astype(F32), axis=1
+
+    row_ids = jnp.arange(COUNT, dtype=jnp.int32)
+    own_ids = lax.axis_index("shard") * COUNT + row_ids
+    _, own_position = seq_layout(lengths[0], own_ids)
+    cosine, sine = rope_tables(own_position, HEAD_DIM // 2)
+    cosd = jnp.concatenate([cosine, cosine], axis=1)
+    sind = jnp.concatenate([-sine, sine], axis=1)
+
+    full_a, full_b, named, any_slot, dy_rows = gather_weights(pack, top_experts, cotangent)
+    dy_rows = exchange(dy_rows)
+    wq = full_a.reshape(D, WA)
+    wb = full_b.reshape(D, WB)
+    queries, kv, attended, middle, normed, tops, totals, gates, tiles, dispatch = run_forward(
+        lengths, tokens, wq, wb, any_slot, named, cosd, sind
     )
-    row_ids = jnp.arange(count, dtype=jnp.int32)
-    earlier = (row_ids[None, :] < row_ids[:, None]).astype(BF16)
-    slot_of = jnp.dot(earlier, named.astype(BF16), preferred_element_type=F32)
-    slot_of = jnp.where(named > 0, slot_of, -1.0)
-    hits = slot_of[:, :, None] == jnp.arange(CAP, dtype=F32)
-    any_slot = hits.reshape(count, EXPERTS * CAP).astype(BF16)
-    logits = jnp.dot(tokens, full_router, preferred_element_type=F32)
-    masked_logits = jnp.where(named > 0, logits, -jnp.inf)
-    gates = jax.nn.softmax(masked_logits, axis=-1)
-    slot_gates = jnp.sum(jnp.where(hits, gates[:, :, None], 0.0), axis=0).reshape(-1)
-    row_grads = (
-        jnp.dot(any_slot.T, cotangent, preferred_element_type=F32) * slot_gates[:, None]
-    ).astype(BF16)
-    arrived_grads = exchange(row_grads)
-
-    tok_f = tokens.astype(F32)
-    normed = rms_scale(tok_f, attn_g).astype(BF16)
-    projected = jnp.dot(normed, full_qkv, preferred_element_type=F32)
-    shard_pos = lax.axis_index("shard")
-    group_rows = lax.axis_size("shard") * count
-    all_ids = jnp.arange(group_rows, dtype=jnp.int32)
-    key_segment, key_position = seq_layout(lengths[0], all_ids)
-    own_ids = shard_pos * count + row_ids
-    own_segment = lax.dynamic_slice_in_dim(key_segment, shard_pos * count, count)
-    own_position = lax.dynamic_slice_in_dim(key_position, shard_pos * count, count)
-    cosine, sine_tab = rope_tables(own_position, HEAD_DIM // 2)
-    queries = rotate(
-        projected[:, :WIDTH_Q].reshape(count, HEADS_Q, HEAD_DIM), cosine, sine_tab
-    ).astype(BF16)
-    keys_rot = rotate(
-        projected[:, WIDTH_Q : WIDTH_Q + WIDTH_KV].reshape(count, HEADS_KV, HEAD_DIM),
-        cosine,
-        sine_tab,
-    ).astype(BF16)
-    values = projected[:, WIDTH_Q + WIDTH_KV :].astype(BF16)
-    local_kv = jnp.concatenate([keys_rot.reshape(count, WIDTH_KV), values], axis=1)
-    group_kv = lax.all_gather(local_kv, "shard", axis=0, tiled=True)
-    keys_all = group_kv[:, :WIDTH_KV].reshape(group_rows, HEADS_KV, HEAD_DIM)
-    values_all = group_kv[:, WIDTH_KV:].reshape(group_rows, HEADS_KV, HEAD_DIM)
-    grouped = queries.reshape(count, HEADS_KV, REPEAT, HEAD_DIM)
-    allowed = (own_segment[:, None] == key_segment[None, :]) & (
-        all_ids[None, :] <= own_ids[:, None]
-    )
-
-    def attn_scores():
-        raw_scores = (
-            jnp.einsum("tgrd,kgd->grtk", grouped, keys_all, preferred_element_type=F32) * scale
-        )
-        return jnp.where(allowed, raw_scores, -1e30)
-
-    masked = attn_scores()
-    top_score = jnp.max(masked, axis=-1, keepdims=True)
-    expo_vals = jnp.exp(masked - top_score)
-    total_weight = jnp.sum(expo_vals, axis=-1, keepdims=True)
-    probs_low = (expo_vals / total_weight).astype(BF16)
-    attended = (
-        jnp.einsum("grtk,kgd->tgrd", probs_low, values_all, preferred_element_type=F32)
-        .reshape(count, WIDTH_Q)
-        .astype(BF16)
-    )
-    branch = lax.dot_general(
-        attended, out_t, (((1,), (1,)), ((), ())), preferred_element_type=F32
-    )
-    middle = tok_f + branch
-    normed_ffn = rms_scale(middle, ffn_g).astype(BF16)
-    dispatch = jnp.dot(any_slot.T, normed_ffn, preferred_element_type=F32).astype(BF16)
-    back_rows, expert_out, grad_up_local, grad_down_local = run_experts(
+    back, gate_back, expert_out, up_local, down_local = run_experts(
         dispatch.reshape(EXPERTS, CAP, D),
-        arrived_grads.reshape(EXPERTS, CAP, D),
+        tiles,
+        dy_rows.reshape(EXPERTS, CAP, D),
         gate_up,
         down_proj,
     )
-    back_rows = back_rows.reshape(ROWS, D)
     returned = exchange(expert_out)
-
-    upstream = cotangent.astype(F32)
-    grad_normed_ffn = jnp.dot(any_slot, back_rows, preferred_element_type=F32)
-    ffn_value, ffn_pull = jax.vjp(rms_scale, middle, ffn_g)
-    grad_mid_norm, grad_ffn_gain = ffn_pull(grad_normed_ffn)
-    grad_middle = upstream + grad_mid_norm
-    grad_branch = grad_middle.astype(BF16)
-    grad_out_t = jnp.dot(grad_branch.T, attended, preferred_element_type=F32).astype(BF16)
-    grad_attended = (
-        jnp.dot(grad_branch, out_t, preferred_element_type=F32)
-        .astype(BF16)
-        .reshape(count, HEADS_KV, REPEAT, HEAD_DIM)
+    grad_tokens, grad_qkv, grad_out, grad_small, up_far, down_far = run_backward(
+        lengths, tokens, cotangent, any_slot, gates, gate_back, queries, kv, attended, middle,
+        normed, tops, totals, cosd, sind, wq, wb, back.reshape(ROWS, D), up_local, down_local,
     )
-    probs_again = jnp.exp(attn_scores() - top_score) / total_weight
-    grad_probs = jnp.einsum(
-        "tgrd,kgd->grtk", grad_attended, values_all, preferred_element_type=F32
-    )
-    grad_scores = (
-        probs_again * (grad_probs - jnp.sum(probs_again * grad_probs, axis=-1, keepdims=True))
-    ).astype(BF16)
-    grad_queries = (
-        jnp.einsum("grtk,kgd->tgrd", grad_scores, keys_all, preferred_element_type=F32) * scale
-    )
-    grad_keys = (
-        jnp.einsum("grtk,tgrd->kgd", grad_scores, grouped, preferred_element_type=F32) * scale
-    )
-    grad_values = jnp.einsum(
-        "grtk,tgrd->kgd", probs_low, grad_attended, preferred_element_type=F32
-    )
-    group_grads = jnp.concatenate(
-        [grad_keys.reshape(group_rows, WIDTH_KV), grad_values.reshape(group_rows, WIDTH_KV)], axis=1
-    )
-    own_kv_grads = lax.psum_scatter(
-        group_grads.astype(BF16), "shard", scatter_dimension=0, tiled=True
-    ).astype(F32)
-    grad_projected = jnp.concatenate(
-        [
-            unrotate(grad_queries.reshape(count, HEADS_Q, HEAD_DIM), cosine, sine_tab).reshape(
-                count, WIDTH_Q
-            ),
-            unrotate(
-                own_kv_grads[:, :WIDTH_KV].reshape(count, HEADS_KV, HEAD_DIM), cosine, sine_tab
-            ).reshape(count, WIDTH_KV),
-            own_kv_grads[:, WIDTH_KV:],
-        ],
-        axis=1,
-    ).astype(BF16)
-    grad_qkv_local = jnp.dot(normed.T, grad_projected, preferred_element_type=F32).astype(BF16)
-    grad_normed = lax.dot_general(
-        grad_projected, full_qkv, (((1,), (1,)), ((), ())), preferred_element_type=F32
-    )
-    attn_value, attn_pull = jax.vjp(rms_scale, tok_f, attn_g)
-    grad_tok_norm, grad_attn_gain = attn_pull(grad_normed)
-
-    mix = jnp.where(hits, gates[:, :, None], 0.0).reshape(count, EXPERTS * CAP)
-    mix_high = mix.astype(BF16)
-    mix_low = (mix - mix_high.astype(F32)).astype(BF16)
-    combined = jnp.dot(mix_high, returned, preferred_element_type=F32) + jnp.dot(
-        mix_low, returned, preferred_element_type=F32
-    )
-    output = (middle + combined).astype(BF16)
-    products = lax.dot_general(
-        cotangent, returned, (((1,), (1,)), ((), ())), preferred_element_type=F32
-    ).reshape(count, EXPERTS, CAP)
-    gate_grad = jnp.sum(jnp.where(hits, products, 0.0), axis=-1)
-    logit_grad = gates * (gate_grad - jnp.sum(gates * gate_grad, axis=-1, keepdims=True))
-    router_f = full_router.astype(F32)
-    grad_router_local = jnp.dot(tok_f.T, logit_grad, precision=precise)
-    grad_from_router = jnp.dot(logit_grad, router_f.T, precision=precise)
-    grad_tokens = (grad_middle + grad_tok_norm + grad_from_router).astype(BF16)
-
-    grad_small = jnp.concatenate(
-        [
-            grad_router_local,
-            grad_attn_gain[:, None],
-            grad_ffn_gain[:, None],
-            jnp.zeros((D, SMALL - EXPERTS - 2), F32),
-        ],
-        axis=1,
-    ).astype(BF16)
-    sum_a, sum_b = scatter_sums(
-        grad_qkv_local.reshape(4, 4, 2, BLOCK, WA),
-        grad_out_t.reshape(4, 4, 2, BLOCK, D),
+    sum_a, sum_b, up_sum, down_sum = scatter_sums(
+        grad_qkv.reshape(4, 4, 2, BLOCK, WA),
+        grad_out.reshape(4, 4, 2, BLOCK, D),
         grad_small.reshape(4, 4, 2, BLOCK, SMALL),
+        up_local,
+        down_local,
+        up_far,
+        down_far,
     )
     sum_b = sum_b[:PIECE]
-    up_sum = lax.psum_scatter(
-        grad_up_local[None], "shard", scatter_dimension=1, tiled=True
-    ).astype(F32)
-    down_sum = lax.psum_scatter(
-        grad_down_local[None], "shard", scatter_dimension=2, tiled=True
-    ).astype(F32)
+
+    expand = jnp.arange(ROWS) // CAP == jnp.arange(128)[:, None]
+    mix = jnp.dot(gates.astype(BF16), expand.astype(BF16), preferred_element_type=F32)
+    mix = (mix * any_slot.astype(F32)).astype(BF16)
+    combined = jnp.dot(mix, returned, preferred_element_type=F32)
+    output = (middle + combined).astype(BF16)
     return (
         output,
         grad_tokens,
@@ -827,8 +1148,8 @@
         sum_b[:, D + EXPERTS],
         sum_b[:, D + EXPERTS + 1],
         sum_b[:, D : D + EXPERTS],
-        up_sum,
-        down_sum,
+        up_sum[None],
+        down_sum[None],
     )
 
 

time: 528 us -> 420 us (0.80); the launches traced: 520 us -> 420 us
  Pallas kernels: 249 us -> 344 us
  matrix products: 94.1 us -> 5.57 us
  waiting for transfers between devices: 46.1 us -> 10.1 us
  local copies, waits for them, and re-layouts: 64.4 us -> 31.9 us
  other arithmetic: 24.6 us -> 0.97 us
  between operations: 14.9 us -> 0.87 us
    pallas_call x1 -> x3, Pallas kernels: 137 us -> 236 us  [the longest x1 144 us: run_experts(): pl.pallas_call(experts_kernel, name='experts', out_shape=(blocks, jax.Sha...]
    dot_general x21 -> x1, matrix products: 83.7 us -> 5.57 us  [body(): combined = jnp.dot(mix, returned, preferred_element_type=F32)]
    all_to_all x2, waiting for transfers between devices: 39.4 us -> 10.1 us  [exchange(): lax.all_to_all(rows.reshape(EXPERTS, CAP, D), 'expert', split_axis=0, con...]
    unnamed x127 -> x51, local copies, waits for them, and re-layouts: 38.8 us -> 27.5 us
    convert_element_type x3 -> x0, other arithmetic: 10.6 us -> none  [the longest x1 6.58 us: body(): grad_scores = (probs_again * (grad_probs - jnp.sum(probs_again * grad_pro...]
    sub x1 -> x0, matrix products: 10.4 us -> none  [body(): expo_vals = jnp.exp(masked - top_score)]
    slice x8 -> x0, local copies, waits for them, and re-layouts: 7.79 us -> none  [the longest x2 3.13 us: body(): projected[:, :WIDTH_Q].reshape(count, HEADS_Q, HEAD_DIM)]
    all_gather x1 -> x0, waiting for transfers between devices: 6.12 us -> none  [body(): group_kv = lax.all_gather(local_kv, 'shard', axis=0, tiled=True)]
  transfers between devices with their start and end apart: 6 -> 2, of which waited for: 3 -> 1; matrix products, arithmetic and copies ran while one was open for 22% -> 1% of each run, Pallas kernels for 11% -> 35%
where the time goes in v3:
time: 420 us
  Pallas kernels  344 us (82%)
  local copies, waits for them, and re-layouts  31.9 us (8%)
  starting transfers between devices  26.2 us (6%)
  waiting for transfers between devices  10.1 us (2%)
  matrix products  5.57 us (1%)
    pallas_call x1, Pallas kernels, run_experts(): pl.pallas_call(experts_kernel, name='experts', out_shape=(blocks, jax.Sha...  144 us
    pallas_call x1, Pallas kernels, scatter_sums(): pl.pallas_call(scatter_kernel, name='scatter_sums', out_shape=(jax.ShapeD...  55.3 us
    pallas_call x1, Pallas kernels, gather_weights(): pl.pallas_call(gather_kernel, name='gather_weights', out_shape=(jax.Shape...  52.3 us
    pallas_call x1, Pallas kernels, run_backward(): pl.pallas_call(backward_kernel, name='backward', out_shape=(shape((COUNT,...  50.6 us
    pallas_call x1, Pallas kernels, run_forward(): pl.pallas_call(forward_kernel, name='forward', out_shape=(shape((COUNT, D...  41.5 us
    unnamed x51, local copies, waits for them, and re-layouts  27.5 us
    all_to_all x2, starting transfers between devices, exchange(): lax.all_to_all(rows.reshape(EXPERTS, CAP, D), 'expert', split_axis=0, con...  26.2 us
    all_to_all x2, waiting for transfers between devices, exchange(): lax.all_to_all(rows.reshape(EXPERTS, CAP, D), 'expert', split_axis=0, con...  10.1 us
  transfers between devices with their start and end apart: 2, of which 1 were waited for; matrix products, arithmetic and copies ran while one was open for 1% of the time, Pallas kernels for 35%

profile of v3, /device:TPU:0, one launch (start us, length us, event | category | flops | bytes accessed | tf_op | source)
XLA Modules:
  0.0 419.8 jit_solution(8184163776389328243)
XLA Ops:
  0.6 0.7 copy.26
  1.4 0.8 copy.27
  2.1 1.0 concatenate.9
  3.1 0.8 copy.28.top_experts
  4.0 0.0 copy-start.4
  4.0 1.1 copy-done.4
  5.1 52.3 %gather_weights.1 = (bf16[4,4,2,48,2048]{4,3,2,1,0:T(8,128)(2,1)S(1)}, bf16[4,4,2,48,1664]{4,3,2,1,0:T(8,128)(2,1)S(1)}, f32[256,128]{1,0:T(8,128)S(1)}, bf16[25...) custom-call(bf16[16,3712]{1,0:T(8,128)(2,1)S(1)} %pad.4.pack, s32[256,4]{1,0:T(8,128)S(1)} %copy.28.top_experts, ...), custom_call_target="tpu_custom_call" | custom-call | bytes 24000000 | tf_op jit(solution)/shard_map/gather_weights/pallas_call | solution.py:213
  57.5 0.0 copy-start.1
  57.5 2.2 copy-done.1
  59.6 2.6 copy-done.11
  62.3 2.2 copy-done.12
  64.5 5.7 %all-to-all-start = ((bf16[32,48,1536]{2,1,0:T(8,128)(2,1)}), bf16[32,48,1536]{2,1,0:T(8,128)(2,1)}, u32[]{:S(2)}, u32[]{:S(2)}) async-start(bf16[32,48,1536]{2,1,0:T(8,128)(2,1)} %bitcast.22), calls=%async_computation | async-start | bytes 9437184 | tf_op jit(solution)/shard_map/all_to_all | solution.py:1080
  70.3 0.0 copy-done.10
  70.3 0.2 reduce-window.8
  70.5 0.1 select_reduce_fusion
  70.6 0.5 fusion.6
  71.1 0.1 pad_maximum_fusion
  71.2 0.0 copy-start.7
  71.3 41.5 %forward.1 = (bf16[256,1536]{1,0:T(8,128)(2,1)S(1)}, bf16[1024,512]{1,0:T(8,128)(2,1)S(1)}, bf16[256,1536]{1,0:T(8,128)(2,1)S(1)}, f32[256,1536]{1,0:T(8,128)}, ...) custom-call(s32[1,4]{1,0:T(1,128)S(1)} %copy-done.10, ...), custom_call_target="tpu_custom_call" | custom-call | flops 6000000000 | bytes 30000000 | tf_op jit(solution)/shard_map/forward/pallas_call | solution.py:846
  112.8 0.6 copy-done.15
  113.4 1.0 copy-done.16
  114.4 0.9 copy-done.17
  115.3 0.9 copy-done.18
  116.2 0.9 copy-done.19
  117.1 0.7 copy-done.20
  117.7 0.6 copy-done.21
  118.3 0.6 copy-done.22
  118.9 10.1 %all-to-all-done.dy_in = bf16[32,48,1536]{2,1,0:T(8,128)(2,1)} async-done(((bf16[32,48,1536]{2,1,0:T(8,128)(2,1)}), bf16[32,48,1536]{2,1,0:T(8,128)(2,1)}, u32[]{:S(2)}, u32[]{:S(2)}) %all-to-all-start) | async-done | bytes 4718624 | tf_op jit(solution)/shard_map/all_to_all | solution.py:1080
  129.0 144.4 %experts.1 = (bf16[32,48,1536]{2,1,0:T(8,128)(2,1)}, f32[32,8,128]{2,1,0:T(8,128)}, bf16[32,48,1536]{2,1,0:T(8,128)(2,1)}, bf16[1536,1536]{1,0:T(8,128)(2,1)}, bf16[768,1536]{1,0:T(8,128)(2,1)}) custom-call(bf16[32,48,1536]{2,1,0:T(8,128)(2,1)} %bitcast.39, f32[32,8,128]{2,1,0:T(8,128)} %copy-done.20, bf16[32,48,1536]{2,1,0:T(8,128)(2,1)} %all-to-all-done.dy_in, ...), custom_call_target="tpu_custom_call" | custom-call | flops 32999999488 | bytes 60000000 | tf_op jit(solution)/shard_map/experts/pallas_call | solution.py:640
  273.4 20.5 %all-to-all-start.1 = ((bf16[32,48,1536]{2,1,0:T(8,128)(2,1)}), bf16[32,48,1536]{2,1,0:T(8,128)(2,1)}, u32[]{:S(2)}, u32[]{:S(2)}) async-start(bf16[32,48,1536]{2,1,0:T(8,128)(2,1)} %get-tuple-element.48), calls=%async_computation.1 | async-start | bytes 9437184 | tf_op jit(solution)/shard_map/all_to_all | solution.py:1080
  293.9 0.0 copy-start.2
  294.0 50.6 %backward.1 = (bf16[256,1536]{1,0:T(8,128)(2,1)}, bf16[1536,2048]{1,0:T(8,128)(2,1)}, bf16[1536,1536]{1,0:T(8,128)(2,1)}, bf16[1536,128]{1,0:T(8,128)(2,1)}, bf1...) custom-call(s32[1,4]{1,0:T(1,128)} %lengths.3, bf16[256,1536]{1,0:T(8,128)(2,1)} %tokens.3, ...), custom_call_target="tpu_custom_call" | custom-call | flops 12999999488 | bytes 50000000 | tf_op jit(solution)/shard_map/backward/pallas_call | solution.py:1023
  344.6 2.3 copy-done
  346.9 1.3 copy-done.3
  348.2 1.1 copy-done.5
  349.3 1.0 copy-done.6
  350.3 55.3 %scatter_sums.1 = (f32[16,2048]{1,0:T(8,128)S(1)}, f32[16,1664]{1,0:T(8,128)S(1)}, f32[384,1536]{1,0:T(8,128)S(1)}, f32[768,384]{1,0:T(8,128)S(1)}) custom-call(bf16[4,4,2,48,2048]{4,3,2,1,0:T(8,128)(2,1)} %bitcast.33, bf16[4,4,2,48,1536]{4,3,2,1,0:T(8,128)(2,1)S(1)} %bitcast.21, bf16[4,4,2,48,128]{4,3,2,1,0:T(8,128)(2,1)S(1)} %bitcast.25, ...), custom_call_target="tpu_custom_call" | custom-call | bytes 24000000 | tf_op jit(solution)/shard_map/scatter_sums/pallas_call | solution.py:432
  405.6 0.0 copy-start.9
  405.6 0.6 copy-done.9
  406.2 0.6 slice.24
  406.8 0.7 slice_reduce_fusion
  407.5 0.6 slice_bitcast_fusion
  408.2 0.0 all-to-all-done.1
  408.2 5.6 %fusion = bf16[256,1536]{1,0:T(8,128)(2,1)} fusion(f32[256,1536]{1,0:T(8,128)} %get-tuple-element.43.middle, bf16[1536,1536]{1,0:T(8,128)(2,1)} %bitcast.10, bf16[256,1536]{1,0:T(8,128)(2,1)} %copy-done.14, s32[1536]{0:T(1024)S(1)} %add_select_fusion, f32[256,128]{1,0:T(8,128)} %copy-done.15), kind=kOutput, calls=%fused_computation.2 | convolution fusion | flops 1310818304 | bytes 8001536 | tf_op jit(solution)/shard_map/dot_general | solution.py:1141
  413.7 2.1 copy.33
  415.8 1.6 copy.34
  417.4 1.4 copy.35
  418.8 1.0 copy.36
  (29 shorter events, 0.1 us)
Async XLA Ops:
  4.0 1.1 copy-start.4
  57.5 2.2 copy-start.1
  59.6 2.7 copy-start.11
  62.3 2.2 copy-start.12
  64.5 6.7 %copy-start.14 = (bf16[256,1536]{1,0:T(8,128)(2,1)}, bf16[256,1536]{1,0:T(8,128)(2,1)S(1)}, u32[]{:S(2)}) copy-start(bf16[256,1536]{1,0:T(8,128)(2,1)S(1)} %get-tuple-element.41.any_slot) | copy-start | bytes 2359300
  64.5 5.7 %copy-start.10 = (s32[1,4]{1,0:T(1,128)S(1)}, s32[1,4]{1,0:T(1,128)}, u32[]{:S(2)}) copy-start(s32[1,4]{1,0:T(1,128)} %lengths.3) | copy-start | bytes 52
  64.5 6.7 %copy-start.13 = (bf16[256,1536]{1,0:T(8,128)(2,1)S(1)}, bf16[256,1536]{1,0:T(8,128)(2,1)}, u32[]{:S(2)}) copy-start(bf16[256,1536]{1,0:T(8,128)(2,1)} %tokens.3) | copy-start | bytes 2359300
  64.5 64.4 %all-to-all-start = ((bf16[32,48,1536]{2,1,0:T(8,128)(2,1)}), bf16[32,48,1536]{2,1,0:T(8,128)(2,1)}, u32[]{:S(2)}, u32[]{:S(2)}) async-start(bf16[32,48,1536]{2,1,0:T(8,128)(2,1)} %bitcast.22), calls=%async_computation | async-start | bytes 9437184 | tf_op jit(solution)/shard_map/all_to_all | solution.py:1080
  71.2 41.5 %copy-start.7 = (f32[256,128]{1,0:T(8,128)}, f32[256,128]{1,0:T(8,128)S(1)}, u32[]{:S(2)}) copy-start(f32[256,128]{1,0:T(8,128)S(1)} %get-tuple-element.74.cosd) | copy-start | bytes 393220
  71.3 41.5 %copy-start.8 = (f32[256,128]{1,0:T(8,128)}, f32[256,128]{1,0:T(8,128)S(1)}, u32[]{:S(2)}) copy-start(f32[256,128]{1,0:T(8,128)S(1)} %get-tuple-element.75.sind) | copy-start | bytes 393220
  112.8 0.6 copy-start.15
  113.4 1.0 copy-start.16
  114.4 0.9 copy-start.17
  115.3 0.9 copy-start.18
  116.2 0.9 copy-start.19
  117.1 0.7 copy-start.20
  117.7 0.6 copy-start.21
  118.3 0.6 copy-start.22
  273.4 134.8 %all-to-all-start.1 = ((bf16[32,48,1536]{2,1,0:T(8,128)(2,1)}), bf16[32,48,1536]{2,1,0:T(8,128)(2,1)}, u32[]{:S(2)}, u32[]{:S(2)}) async-start(bf16[32,48,1536]{2,1,0:T(8,128)(2,1)} %get-tuple-element.48), calls=%async_computation.1 | async-start | bytes 9437184 | tf_op jit(solution)/shard_map/all_to_all | solution.py:1080
  293.9 50.7 %copy-start.2 = (bf16[768,1536]{1,0:T(8,128)(2,1)S(1)}, bf16[768,1536]{1,0:T(8,128)(2,1)}, u32[]{:S(2)}) copy-start(bf16[768,1536]{1,0:T(8,128)(2,1)} %get-tuple-element.58.down_in) | copy-start | bytes 7077892
  344.6 2.3 copy-start
  346.9 1.3 copy-start.3
  348.2 1.1 copy-start.5
  349.3 1.0 copy-start.6
  405.6 0.7 copy-start.9

commit v4 on v3

--- a/solution.py
+++ b/solution.py
@@ -68,9 +68,10 @@
         self.made.append(copy)
         return copy
 
-    def drain(self):
+    def drain(self, skip=()):
         for copy in self.made:
-            copy.wait_send()
+            if not any(copy is done for done in skip):
+                copy.wait_send()
 
 
 def neighbours(y, z, c, x):
@@ -94,26 +95,60 @@
     return jnp.where(same, 1.0, 0.0).astype(BF16)
 
 
-def route(top_experts, named, any_slot):
+def faces(y, z, c, x):
+    along_z, along_y = [], []
+    for d in range(4):
+        for k in range(2):
+            core = c if k == 0 else 1 - c
+            along_z.append((device(y, (z + d) % 4, core, x), (z + d) % 4, core))
+            along_y.append((device((y + d) % 4, z, core, x), (y + d) % 4, core))
+    return along_z, along_y
+
+
+def cross(y, z, c, x):
+    along_z, along_y = faces(y, z, c, x)
+    return [f[0] for f in along_z[1:] + along_y[2:]]
+
+
+def lines(y, z, c, x):
+    return (
+        [device((y + d) % 4, z, c, x) for d in (1, 2, 3)],
+        [device(y, (z + d) % 4, c, x) for d in (1, 2, 3)],
+    )
+
+
+def route(top_experts, named, own_slot):
     lanes = iota((COUNT, 128), 1)
     for k in range(TOP):
         hit = jnp.where(top_experts[:, k : k + 1] == lanes, 1.0, 0.0)
         named[...] = hit if k == 0 else named[...] + hit
     earlier = hot(iota((COUNT, COUNT), 1) < iota((COUNT, COUNT), 0))
     slot_of = mul(earlier, named[...].astype(BF16))
-    slot_of = jnp.where(named[...] > 0, slot_of, -1.0).astype(BF16)
-    expand = hot(iota((128, ROWS), 0) == iota((128, ROWS), 1) // CAP)
-    place_of = (iota((1, ROWS), 1) % CAP).astype(F32)
-    any_slot[...] = hot(mul(slot_of, expand) == place_of)
+    own_slot[...] = jnp.where(named[...] > 0, slot_of, -1.0).astype(BF16)
+
+
+def slot_hits(slot_of, hits, experts):
+    p = iota((1, SLOTS), 1)
+    q = p - 8 * FIRST
+    wanted = jnp.where(p < 8 * FIRST, p % FIRST, FIRST + q % SECOND).astype(F32)
+    local = jnp.where(p < 8 * FIRST, p // FIRST, q // SECOND)
+    expand = hot(iota((128, SLOTS), 0) == experts(local))
+
+    def step(s, carry):
+        hits[s] = hot(mul(slot_of[s], expand) == wanted)
+        return carry
+
+    lax.fori_loop(0, 4, step, 0)
 
 
 def gather_kernel(
-    pack, top_experts, cotangent, full_a, full_b, named, any_slot, dy_rows,
-    xbuf, own_a, own_b, send, recv, local,
+    pack, top_experts, cotangent, full_a, full_b, named, hot_a, hot_b, dy_a, dy_b,
+    xbuf, own_a, own_b, own_slot, slot_y, slot_z, send, recv, local,
 ):
     y, z, c, x = place()
     near = neighbours(y, z, c, x)
-    greet(everyone_near(near))
+    line_y, line_z = lines(y, z, c, x)
+    greet(everyone_near(near) + [line_y[1], line_z[1]])
     link = Links(send, recv)
     first = [link.push(pack, xbuf.at[x], near["x"][d]) for d in range(3)]
     xbuf[pl.ds(x, 1)] = pack[...][None]
@@ -150,7 +185,11 @@
         j["core"] = [link.push(j["own"], here, near["core"])]
         j["local"] = pltpu.make_async_copy(j["own"], here, local.at[j["i"]])
         j["local"].start()
-    route(top_experts, named, any_slot)
+    route(top_experts, named, own_slot)
+    slot_y[pl.ds(y, 1)] = own_slot[...][None]
+    slot_z[pl.ds(z, 1)] = own_slot[...][None]
+    slots = [link.push(own_slot, slot_y.at[y], peer) for peer in line_y]
+    slots += [link.push(own_slot, slot_z.at[z], peer) for peer in line_z]
     for j in jobs:
         plus, minus = near[j["close"]]
         left, right = (j["p"] + 3) % 4, (j["p"] + 1) % 4
@@ -173,13 +212,19 @@
         j["up"] = link.push(line, line, plus)
         j["down"] = link.push(line, line, minus)
         j["core"].append(link.push(block, block, near["core"]))
-
-    def dy_tile(j, carry):
-        lanes = pl.ds(pl.multiple_of(j * TILE, TILE), TILE)
-        dy_rows[lanes, :] = mul(any_slot[:, lanes], cotangent[...], TN).astype(BF16)
-        return carry
-
-    lax.fori_loop(0, ROWS // TILE, dy_tile, 0)
+    half_a, half_b = cotangent.at[:, pl.ds(0, HALF)], cotangent.at[:, pl.ds(HALF, HALF)]
+    kept = [
+        pltpu.make_async_copy(half_a, dy_a.at[y], local.at[2]),
+        pltpu.make_async_copy(half_b, dy_b.at[z], local.at[3]),
+    ]
+    for copy in kept:
+        copy.start()
+    dys = [link.push(half_a, dy_a.at[y], peer) for peer in line_y]
+    dys += [link.push(half_b, dy_b.at[z], peer) for peer in line_z]
+    for copy in slots:
+        copy.wait_recv()
+    slot_hits(slot_y, hot_a, lambda e: y * 8 + e)
+    slot_hits(slot_z, hot_b, lambda e: (e // 2) * 8 + z * 2 + e % 2)
     for j in jobs:
         plus, minus = near[j["far"]]
         left, right = (j["q"] + 3) % 4, (j["q"] + 1) % 4
@@ -203,13 +248,17 @@
     for j in jobs:
         for copy in j["core"]:
             copy.wait_recv()
+    for copy in dys:
+        copy.wait_recv()
+    for copy in kept:
+        copy.wait()
     link.drain()
 
 
 def gather_weights(pack, top_experts, cotangent):
     inside = pl.BlockSpec(memory_space=pltpu.VMEM)
     anywhere = pl.BlockSpec(memory_space=pl.ANY)
-    copies = 3 + 2 * 16
+    copies = 3 + 2 * 16 + 12
     return pl.pallas_call(
         gather_kernel,
         name="gather_weights",
@@ -217,18 +266,23 @@
             jax.ShapeDtypeStruct((4, 4, 2, BLOCK, WA), BF16),
             jax.ShapeDtypeStruct((4, 4, 2, BLOCK, WB), BF16),
             jax.ShapeDtypeStruct((COUNT, 128), F32),
-            jax.ShapeDtypeStruct((COUNT, ROWS), BF16),
-            jax.ShapeDtypeStruct((ROWS, D), BF16),
+            jax.ShapeDtypeStruct((4, COUNT, SLOTS), BF16),
+            jax.ShapeDtypeStruct((4, COUNT, SLOTS), BF16),
+            jax.ShapeDtypeStruct((4, COUNT, HALF), BF16),
+            jax.ShapeDtypeStruct((4, COUNT, HALF), BF16),
         ),
-        in_specs=[inside] * 3,
-        out_specs=(anywhere, anywhere, inside, inside, inside),
+        in_specs=[inside, inside, anywhere],
+        out_specs=(anywhere, anywhere, inside, inside, inside, anywhere, anywhere),
         scratch_shapes=[
             pltpu.VMEM((4, PADDED, WA + WB), BF16),
             pltpu.VMEM((BLOCK, WA), BF16),
             pltpu.VMEM((BLOCK, WB), BF16),
+            pltpu.VMEM((COUNT, 128), BF16),
+            pltpu.VMEM((4, COUNT, 128), BF16),
+            pltpu.VMEM((4, COUNT, 128), BF16),
             pltpu.SemaphoreType.DMA((copies,)),
             pltpu.SemaphoreType.DMA((copies,)),
-            pltpu.SemaphoreType.DMA((2,)),
+            pltpu.SemaphoreType.DMA((4,)),
         ],
         compiler_params=pltpu.CompilerParams(
             collective_id=0, has_side_effects=True, vmem_limit_bytes=24 * 1024 * 1024
@@ -448,16 +502,121 @@
     )(*operands)
 
 
-NEAREST = (
-    (0, 0), (0, 1), (1, 0), (0, 3),
-    (3, 0), (1, 1), (3, 3), (1, 3),
-    (3, 1), (0, 2), (2, 0), (1, 2),
-    (2, 1), (3, 2), (2, 3), (2, 2),
-)
 ROWS = EXPERTS * CAP
-CHUNKS = 4
-CHUNK = ROWS // CHUNKS
 TILE = 256
+FIRST = 32
+SECOND = 16
+PIECES = (FIRST, SECOND)
+SLOTS = 8 * CAP
+HALF = D // 2
+LANES = 128
+WIDE = D + LANES
+WIDE_A = HALF
+WIDE_B = WIDE - HALF
+SCALE = HEAD_DIM ** (-0.5)
+GROUP_ROWS = 1024
+COUNT = 256
+NT = (((1,), (1,)), ((), ()))
+TN = (((0,), (0,)), ((), ()))
+
+
+def mul(a, b, dims=None):
+    if dims is None:
+        return jnp.dot(a, b, preferred_element_type=F32)
+    return lax.dot_general(a, b, dims, preferred_element_type=F32)
+
+
+def thirds(v):
+    high = v.astype(BF16)
+    rest = v - high.astype(F32)
+    middle = rest.astype(BF16)
+    return high, middle, (rest - middle.astype(F32)).astype(BF16)
+
+
+def iota(shape, axis):
+    return lax.broadcasted_iota(jnp.int32, shape, axis)
+
+
+def hot(same):
+    return jnp.where(same, 1.0, 0.0).astype(BF16)
+
+
+class Moves(Links):
+    def __init__(self, send, recv, local):
+        super().__init__(send, recv)
+        self.local, self.kept = local, 0
+
+    def keep(self, src, dst):
+        copy = pltpu.make_async_copy(src, dst, self.local.at[self.kept])
+        self.kept += 1
+        copy.start()
+        return copy
+
+    def send_or_keep(self, i, src, dst, where):
+        if i == 0:
+            return self.keep(src, dst).wait
+        return self.push(src, dst, where).wait_recv
+
+
+def to_slots(hits, rows, stage, piece):
+    n = PIECES[piece]
+    columns = slice(0, 8 * FIRST) if piece == 0 else slice(8 * FIRST, SLOTS)
+    for s in range(4):
+        taken = mul(hits[s, :, columns], rows[s], TN).astype(BF16)
+        stage[:, s] = taken.reshape(8, n, taken.shape[1])
+
+
+def deliver(moves, at, stage_a, stage_b, rows, split):
+    y, z, c, x = at
+    along_z, along_y = faces(y, z, c, x)
+    width = rows.shape[3]
+    waits = []
+    for i, (where, zt, ct) in enumerate(along_z):
+        dst = rows.at[z, pl.ds(c * 4, 4), :, pl.ds(0, split)]
+        waits.append(moves.send_or_keep(i, stage_a.at[zt * 2 + ct], dst, where))
+    for i, (where, yt, ct) in enumerate(along_y):
+        dst = rows.at[:, c * 4 + y, :, pl.ds(split, width - split)]
+        waits.append(moves.send_or_keep(i, stage_b.at[yt * 2 + ct], dst, where))
+    return waits
+
+
+def give_back_a(moves, at, rows, back_a, split):
+    y, z, c, x = at
+    along_z, _ = faces(y, z, c, x)
+    return [
+        moves.send_or_keep(
+            i, rows.at[zt, pl.ds(ct * 4, 4), :, pl.ds(0, split)], back_a.at[z * 2 + c], where
+        )
+        for i, (where, zt, ct) in enumerate(along_z)
+    ]
+
+
+def give_back_b(moves, at, rows, back_b, split):
+    y, z, c, x = at
+    _, along_y = faces(y, z, c, x)
+    width = rows.shape[3]
+    return [
+        moves.send_or_keep(
+            i, rows.at[:, ct * 4 + yt, :, pl.ds(split, width - split)], back_b.at[y * 2 + c], where
+        )
+        for i, (where, yt, ct) in enumerate(along_y)
+    ]
+
+
+def add_up(hits, back_1, back_2, parts, land, me, line, moves):
+    waits = []
+    for d in (1, 2, 3, 0):
+        s = (me + d) % 4
+        first, second = back_1[:, s], back_2[:, s]
+        width = first.shape[2]
+        total = mul(hits[s, :, : 8 * FIRST], first.reshape(8 * FIRST, width))
+        total = total + mul(hits[s, :, 8 * FIRST :], second.reshape(8 * SECOND, width))
+        if d == 0:
+            land[pl.ds(s, 1)] = total.astype(BF16)[None]
+        else:
+            parts[d - 1] = total.astype(BF16)
+            waits.append(moves.push(parts.at[d - 1], land.at[me], line[d - 1]).wait_recv)
+    return waits
 
 
 def gelu_parts(g):
@@ -469,244 +628,194 @@
 
 
 def experts_kernel(
-    sent, gates_in, dy_in, gate_up, down, back, gate_back, outs, up_grad, down_grad,
-    rows, gates, dys, grads, gu, dn, mixed, ghid, grow, eout, dots,
-    send, recv, tsend, trecv, bsend, brecv, dsend, drecv, gsem, wsem, osem, own,
+    hot_a_in, hot_b_in, nf_a_in, nf_b_in, dy1_in, dy2_in, gate_up, down,
+    back_a1, back_a2, back_b1, back_b2, out1, out2, up_out, down_out,
+    hot_a, hot_b, nf_a, nf_b, sa1, sa2, sb1, sb2, rows1, rows2, dy1, dy2,
+    gu, dn, grads, mixed, ghid, grow1, grow2, eo1, eo2, up_grad, down_grad,
+    send, recv, local, load_sem,
 ):
-    y, z, c, x = place()
+    at = place()
+    y, z, c, x = at
     me = (y * 4 + z) * 2 + c
-    weights = [
-        pltpu.make_async_copy(gate_up.at[0], gu, wsem.at[0]),
-        pltpu.make_async_copy(down.at[0], dn, wsem.at[1]),
+    loads = [
+        pltpu.make_async_copy(src, dst, load_sem.at[i])
+        for i, (src, dst) in enumerate(
+            (
+                (hot_a_in, hot_a), (nf_a_in, nf_a), (hot_b_in, hot_b), (nf_b_in, nf_b),
+                (gate_up.at[0], gu), (dy1_in, dy1), (down.at[0], dn), (dy2_in, dy2),
+            )
+        )
     ]
-    slots = []
-    for s, (dy, dz) in enumerate(NEAREST):
-        for b in (0, 1):
-            core = c if b == 0 else 1 - c
-            source = device((y + dy) % 4, (z + dz) % 4, core, x)
-            target = device((y + 4 - dy) % 4, (z + 4 - dz) % 4, core, x)
-            slots.append((2 * s + b, source, target))
-    greet([source for _, source, _ in slots[1:]])
-    links, tile_links, back_links, dot_links = [], [], [], []
-
-    def move(src, dst, where, i, sends, recvs, k):
-        if i == 0:
-            copy = pltpu.make_async_copy(src, dst, own.at[k])
-        else:
-            copy = pltpu.make_async_remote_copy(
-                src_ref=src, dst_ref=dst, send_sem=sends.at[i],
-                recv_sem=recvs.at[i], device_id=where, device_id_type=MESH,
-            )
-        copy.start()
-        return copy
-
-    for i, source, target in slots:
-        tile_links.append(
-            move(gates_in.at[target[0]], gates.at[i], target, i, tsend, trecv, 0)
-        )
-        links.append(
-            move(sent.at[target[0]], rows.at[pl.ds(i * CAP, CAP)], target, i, send, recv, 1)
-        )
-    incoming = []
-    for copy in weights:
-        copy.start()
-    for i, source, target in slots:
-        copy = pltpu.make_async_copy(
-            dy_in.at[source[0]], dys.at[pl.ds(i * CAP, CAP)], gsem.at[i]
-        )
-        copy.start()
-        incoming.append(copy)
-    for copy in weights:
-        copy.wait()
-    leaving = []
-    per = len(slots) // CHUNKS
-    diagonal = lax.broadcasted_iota(jnp.int32, (CAP, 128), 0) == lax.broadcasted_iota(
-        jnp.int32, (CAP, 128), 1
-    )
-    for k in range(CHUNKS):
-        part = slots[k * per : (k + 1) * per]
-        for i, source, target in part:
-            incoming[i].wait()
-            if i == 0:
-                tile_links[0].wait()
-                links[0].wait()
-            else:
-                tile_links[i].wait_recv()
-                links[i].wait_recv()
-        base = k * CHUNK
-        block = pl.ds(base, CHUNK)
-
-        def scale_block(i, carry):
-            at = pl.ds(pl.multiple_of(i * CAP, CAP), CAP)
-            column = jnp.sum(jnp.where(diagonal, gates[i, 0:1, :], 0.0), axis=1, keepdims=True)
-            grads[at, :] = (dys[at, :].astype(F32) * column).astype(BF16)
+    for load in loads:
+        load.start()
+    greet(cross(*at))
+    moves = Moves(send, recv, local)
+    for load in loads[:4]:
+        load.wait()
+    to_slots(hot_a, nf_a, sa1, 0)
+    to_slots(hot_b, nf_b, sb1, 0)
+    waits1 = deliver(moves, at, sa1, sb1, rows1, WIDE_A)
+    to_slots(hot_a, nf_a, sa2, 1)
+    to_slots(hot_b, nf_b, sb2, 1)
+    waits2 = deliver(moves, at, sa2, sb2, rows2, WIDE_A)
+    for load in loads[4:]:
+        load.wait()
+    back_waits = []
+
+    def work(rows, dy, grow, eo, n, start, blocks):
+        small = 512 // n
+
+        def at_small(i):
+            return i // 8, i % 8
+
+        def gate_of(zz, q):
+            lanes = iota((n, LANES), 1)
+            mine = (lanes == me) | (lanes == me + EXPERTS) | (lanes == me + 2 * EXPERTS)
+            held = rows[zz, q, :, 0:LANES].astype(F32)
+            return jnp.sum(jnp.where(mine, held, 0.0), axis=1, keepdims=True)
+
+        def scale_step(i, carry):
+            zz, q = at_small(i)
+            base = pl.multiple_of(start + i * n, n)
+            grads[pl.ds(base, n), :] = (dy[zz, q].astype(F32) * gate_of(zz, q)).astype(BF16)
             return carry
 
-        lax.fori_loop(k * per, (k + 1) * per, scale_block, 0)
-
-        def hidden_tile(j, carry, block=block):
-            lanes = pl.ds(pl.multiple_of(j * TILE, TILE), TILE)
-            upper = pl.ds(pl.multiple_of(FF + j * TILE, TILE), TILE)
-            g = jnp.dot(rows[block, :], gu[:, lanes], preferred_element_type=F32)
-            act, slope = gelu_parts(g)
-            u = jnp.dot(rows[block, :], gu[:, upper], preferred_element_type=F32)
-            mixed[block, lanes] = (act * u).astype(BF16)
-            m = lax.dot_general(
-                grads[block, :], dn[lanes, :], (((1,), (1,)), ((), ())),
-                preferred_element_type=F32,
-            )
-            ghid[block, lanes] = (m * u * slope).astype(BF16)
-            ghid[block, upper] = (m * act).astype(BF16)
+        lax.fori_loop(0, blocks * small, scale_step, 0)
+        per = 4 // blocks
+        for b in range(blocks):
+            zs = slice(b * per, (b + 1) * per)
+            block = slice(start + b * 512, start + (b + 1) * 512)
+
+            def hidden_tile(j, carry, zs=zs, block=block):
+                lanes = pl.ds(pl.multiple_of(j * TILE, TILE), TILE)
+                upper = pl.ds(pl.multiple_of(FF + j * TILE, TILE), TILE)
+                g = mul(rows[zs, :, :, LANES:].reshape(512, D), gu[:, lanes])
+                act, slope = gelu_parts(g)
+                u = mul(rows[zs, :, :, LANES:].reshape(512, D), gu[:, upper])
+                mixed[block, lanes] = (act * u).astype(BF16)
+                m = mul(grads[block, :], dn[lanes, :], NT)
+                ghid[block, lanes] = (m * u * slope).astype(BF16)
+                ghid[block, upper] = (m * act).astype(BF16)
+                return carry
+
+            lax.fori_loop(0, FF // TILE, hidden_tile, 0)
+
+            def rows_tile(j, carry, zs=zs, block=block):
+                lanes = pl.ds(pl.multiple_of(j * TILE, TILE), TILE)
+                into = pl.ds(pl.multiple_of(LANES + j * TILE, LANES), TILE)
+                part = mul(ghid[block, :], gu[lanes, :], NT).astype(BF16)
+                grow[zs, :, :, into] = part.reshape(per, 8, n, TILE)
+                return carry
+
+            lax.fori_loop(0, D // TILE, rows_tile, 0)
+        back_b = back_b1 if n == FIRST else back_b2
+        back_waits.extend(give_back_b(moves, at, grow, back_b, WIDE_A))
+        for b in range(blocks):
+            zs = slice(b * per, (b + 1) * per)
+            block = slice(start + b * 512, start + (b + 1) * 512)
+
+            def out_tile(j, carry, zs=zs, block=block):
+                lanes = pl.ds(pl.multiple_of(j * TILE, TILE), TILE)
+                part = mul(mixed[block, :], dn[:, lanes]).astype(BF16)
+                eo[zs, :, :, lanes] = part.reshape(per, 8, n, TILE)
+                return carry
+
+            lax.fori_loop(0, D // TILE, out_tile, 0)
+
+        def gate_step(i, carry):
+            zz, q = at_small(i)
+            out = eo[zz, q].astype(F32)
+            slope = jnp.sum(out * dy[zz, q].astype(F32), axis=1, keepdims=True)
+            lanes = iota((n, LANES), 1)
+            held = jnp.zeros((n, LANES), F32)
+            for k, third in enumerate(thirds(slope)):
+                held = jnp.where(lanes == me + k * EXPERTS, third.astype(F32), held)
+            grow[zz, q, :, 0:LANES] = held.astype(BF16)
+            eo[zz, q] = (out * gate_of(zz, q)).astype(BF16)
             return carry
 
-        lax.fori_loop(0, FF // TILE, hidden_tile, 0)
-
-        def rows_tile(j, carry, block=block):
-            lanes = pl.ds(pl.multiple_of(j * TILE, TILE), TILE)
-            grow[block, lanes] = lax.dot_general(
-                ghid[block, :], gu[lanes, :], (((1,), (1,)), ((), ())),
-                preferred_element_type=F32,
-            ).astype(BF16)
-            return carry
-
-        lax.fori_loop(0, D // TILE, rows_tile, 0)
-        for i, source, target in part:
-            back_links.append(
-                move(grow.at[pl.ds(i * CAP, CAP)], back.at[me], source, i, bsend, brecv, 2)
-            )
-
-        def out_tile(j, carry, block=block):
-            lanes = pl.ds(pl.multiple_of(j * TILE, TILE), TILE)
-            eout[block, lanes] = jnp.dot(
-                mixed[block, :], dn[:, lanes], preferred_element_type=F32
-            ).astype(BF16)
-            return carry
-
-        lax.fori_loop(0, D // TILE, out_tile, 0)
-        for i, source, target in part:
-            copy = pltpu.make_async_copy(
-                eout.at[pl.ds(i * CAP, CAP)], outs.at[source[0]], osem.at[i]
-            )
-            copy.start()
-            leaving.append(copy)
-
-        def dot_block(i, carry):
-            at = pl.ds(pl.multiple_of(i * CAP, CAP), CAP)
-            column = jnp.sum(
-                eout[at, :].astype(F32) * dys[at, :].astype(F32), axis=1, keepdims=True
-            )
-            row = jnp.sum(jnp.where(diagonal, column, 0.0), axis=0, keepdims=True)
-            dots[i] = jnp.broadcast_to(row, (8, 128))
-            return carry
-
-        lax.fori_loop(k * per, (k + 1) * per, dot_block, 0)
-        for i, source, target in part:
-            dot_links.append(
-                move(dots.at[i], gate_back.at[me], source, i, dsend, drecv, 3)
-            )
+        lax.fori_loop(0, blocks * small, gate_step, 0)
+        back_a = back_a1 if n == FIRST else back_a2
+        back_waits.extend(give_back_a(moves, at, grow, back_a, WIDE_A))
+
+    for wait in waits1:
+        wait()
+    work(rows1, dy1, grow1, eo1, FIRST, 0, 2)
+    back_waits.append(moves.keep(eo1, out1).wait)
+    for wait in waits2:
+        wait()
+    work(rows2, dy2, grow2, eo2, SECOND, 1024, 1)
+    back_waits.append(moves.keep(eo2, out2).wait)
 
     def up_tile(j, carry):
         lanes = pl.ds(pl.multiple_of(j * TILE, TILE), TILE)
-        up_grad[lanes, :] = lax.dot_general(
-            rows[:, lanes], ghid[...], (((0,), (0,)), ((), ())), preferred_element_type=F32
-        ).astype(BF16)
+        held = pl.ds(pl.multiple_of(LANES + j * TILE, LANES), TILE)
+        part = mul(rows1[:, :, :, held].reshape(1024, TILE), ghid[0:1024, :], TN)
+        part = part + mul(rows2[:, :, :, held].reshape(512, TILE), ghid[1024:, :], TN)
+        up_grad[lanes, :] = part.astype(BF16)
         return carry
 
     lax.fori_loop(0, D // TILE, up_tile, 0)
+    back_waits.append(moves.keep(up_grad, up_out).wait)
 
     def down_tile(j, carry):
         lanes = pl.ds(pl.multiple_of(j * TILE, TILE), TILE)
-        down_grad[lanes, :] = lax.dot_general(
-            mixed[:, lanes], grads[...], (((0,), (0,)), ((), ())), preferred_element_type=F32
-        ).astype(BF16)
+        down_grad[lanes, :] = mul(mixed[:, lanes], grads[...], TN).astype(BF16)
         return carry
 
     lax.fori_loop(0, FF // TILE, down_tile, 0)
-    for copy in leaving:
-        copy.wait()
-    back_links[0].wait()
-    dot_links[0].wait()
-    for copy in back_links[1:] + dot_links[1:]:
-        copy.wait_recv()
-    for copy in tile_links[1:] + links[1:] + back_links[1:] + dot_links[1:]:
-        copy.wait_send()
-
-
-def run_experts(sent, gates_in, dy_in, gate_up, down):
+    back_waits.append(moves.keep(down_grad, down_out).wait)
+    for wait in back_waits:
+        wait()
+    moves.drain()
+
+
+def pieces(*lead, width):
+    return [(*lead, n, width) for n in PIECES]
+
+
+def run_experts(*operands):
     anywhere = pl.BlockSpec(memory_space=pl.ANY)
-    inside = pl.BlockSpec(memory_space=pltpu.VMEM)
-    blocks = jax.ShapeDtypeStruct((EXPERTS, CAP, D), BF16)
     vmem, dma = pltpu.VMEM, pltpu.SemaphoreType.DMA
+    outs = (
+        pieces(8, 4, width=WIDE_A)
+        + pieces(8, 4, width=WIDE_B)
+        + pieces(4, 8, width=D)
+        + [(D, 2 * FF), (FF, D)]
+    )
+    held = (
+        [(4, COUNT, SLOTS)] * 2
+        + [(4, COUNT, WIDE_A), (4, COUNT, WIDE_B)]
+        + pieces(8, 4, width=WIDE_A)
+        + pieces(8, 4, width=WIDE_B)
+        + pieces(4, 8, width=WIDE)
+        + pieces(4, 8, width=D)
+        + [(D, 2 * FF), (FF, D), (ROWS, D), (ROWS, FF), (ROWS, 2 * FF)]
+        + pieces(4, 8, width=WIDE)
+        + pieces(4, 8, width=D)
+        + [(D, 2 * FF), (FF, D)]
+    )
     return pl.pallas_call(
         experts_kernel,
         name="experts",
-        out_shape=(
-            blocks,
-            jax.ShapeDtypeStruct((EXPERTS, 8, 128), F32),
-            blocks,
-            jax.ShapeDtypeStruct((D, 2 * FF), BF16),
-            jax.ShapeDtypeStruct((FF, D), BF16),
-        ),
-        in_specs=[anywhere] * 5,
-        out_specs=(anywhere, anywhere, anywhere, inside, inside),
-        scratch_shapes=[
-            vmem((ROWS, D), BF16),
-            vmem((EXPERTS, 8, 128), F32),
-            vmem((ROWS, D), BF16),
-            vmem((ROWS, D), BF16),
-            vmem((D, 2 * FF), BF16),
-            vmem((FF, D), BF16),
-            vmem((ROWS, FF), BF16),
-            vmem((ROWS, 2 * FF), BF16),
-            vmem((ROWS, D), BF16),
-            vmem((ROWS, D), BF16),
-            vmem((EXPERTS, 8, 128), F32),
-        ]
-        + [dma((EXPERTS,))] * 8
-        + [dma((EXPERTS,)), dma((2,)), dma((EXPERTS,)), dma((4,))],
+        out_shape=tuple(jax.ShapeDtypeStruct(shape, BF16) for shape in outs),
+        in_specs=[anywhere] * 8,
+        out_specs=(anywhere,) * 8,
+        scratch_shapes=[vmem(shape, BF16) for shape in held]
+        + [dma((56,)), dma((56,)), dma((12,)), dma((8,))],
         compiler_params=pltpu.CompilerParams(
-            collective_id=2, has_side_effects=True, vmem_limit_bytes=58 * 1024 * 1024
+            collective_id=2, has_side_effects=True, vmem_limit_bytes=60 * 1024 * 1024
         ),
         cost_estimate=pl.CostEstimate(
             flops=33_000_000_000, bytes_accessed=60_000_000, transcendentals=1_200_000
         ),
-    )(sent, gates_in, dy_in, gate_up, down)
+    )(*operands)
 
 
 UP_PART = D // 4
 UP_HALF = UP_PART // 2
 DOWN_PART = D // 4
 DOWN_HALF = FF // 2
-SCALE = HEAD_DIM ** (-0.5)
-GROUP_ROWS = 1024
-COUNT = 256
-NT = (((1,), (1,)), ((), ()))
-TN = (((0,), (0,)), ((), ()))
-
-
-def mul(a, b, dims=None):
-    if dims is None:
-        return jnp.dot(a, b, preferred_element_type=F32)
-    return lax.dot_general(a, b, dims, preferred_element_type=F32)
-
-
-def thirds(v):
-    high = v.astype(BF16)
-    rest = v - high.astype(F32)
-    middle = rest.astype(BF16)
-    return high, middle, (rest - middle.astype(F32)).astype(BF16)
-
-
-def exact(v, one_hot, dims=None):
-    return sum(mul(part, one_hot, dims) for part in thirds(v))
-
-
-def iota(shape, axis):
-    return lax.broadcasted_iota(jnp.int32, shape, axis)
-
-
-def hot(same):
-    return jnp.where(same, 1.0, 0.0).astype(BF16)
 
 
 def read_gains(small):
@@ -738,20 +847,29 @@
 
 
 def forward_kernel(
-    lengths, tokens, wq_in, wb_in, any_slot, named, cosd, sind,
-    q_out, kv_out, attended, middle, normed, tops, totals, gates_out, tiles, dispatch,
-    wq, wb, kv, own_kv, bias, vt, nf, send, recv, local,
+    lengths, tokens, wq_in, wb_in, named, cosd, sind, hot_a_in, hot_b_in, dy_a_in, dy_b_in,
+    q_out, kv_out, attended_out, middle_out, normed_out, tops, totals, gates_out,
+    nf_a, nf_b, dy1, dy2,
+    wq, wb, kv, own_kv, bias, vt, q, attended, middle, normed, nf,
+    hot_a, hot_b, dy_a, dy_b, sa1, sa2, sb1, sb2, send, recv, local, load_sem,
 ):
-    y, z, c, x = place()
+    at = place()
+    y, z, c, x = at
+    line_y, line_z = lines(y, z, c, x)
     peers = [device(y, z, c, (x + d) % 4) for d in (1, 2, 3)]
     loads = [
-        pltpu.make_async_copy(wq_in.at[:, pl.ds(D, 512)], wq.at[:, pl.ds(D, 512)], local.at[0]),
-        pltpu.make_async_copy(wq_in.at[:, pl.ds(0, D)], wq.at[:, pl.ds(0, D)], local.at[1]),
-        pltpu.make_async_copy(wb_in, wb, local.at[2]),
+        pltpu.make_async_copy(wq_in.at[:, pl.ds(D, 512)], wq.at[:, pl.ds(D, 512)], load_sem.at[0]),
+        pltpu.make_async_copy(wq_in.at[:, pl.ds(0, D)], wq.at[:, pl.ds(0, D)], load_sem.at[1]),
+        pltpu.make_async_copy(wb_in, wb, load_sem.at[2]),
+    ]
+    pairs = ((hot_a_in, hot_a), (dy_a_in, dy_a), (hot_b_in, hot_b), (dy_b_in, dy_b))
+    loads += [
+        pltpu.make_async_copy(src, dst, load_sem.at[3 + i]) for i, (src, dst) in enumerate(pairs)
     ]
     for load in loads:
         load.start()
-    greet(peers)
+    greet(cross(*at) + peers)
+    moves = Moves(send, recv, local)
     loads[2].wait()
     small = wb[:, D:]
     gains, _ = read_gains(small)
@@ -768,16 +886,23 @@
         else:
             own_kv[:, 256:512] = part.astype(BF16)
     rows = pl.ds(pl.multiple_of(x * COUNT, COUNT), COUNT)
-    link = Links(send, recv)
-    pushes = [link.push(own_kv, kv.at[rows], peer) for peer in peers]
+    pushes = [moves.push(own_kv, kv.at[rows], peer) for peer in peers]
     kv[rows, :] = own_kv[...]
+    for load in loads[3:]:
+        load.wait()
+    to_slots(hot_a, dy_a, sa1, 0)
+    to_slots(hot_b, dy_b, sb1, 0)
+    to_slots(hot_a, dy_a, sa2, 1)
+    to_slots(hot_b, dy_b, sb2, 1)
+    dy_waits = deliver(moves, at, sa1, sb1, dy1, HALF)
+    dy_waits += deliver(moves, at, sa2, sb2, dy2, HALF)
     fill_bias(lengths, bias, x)
     loads[1].wait()
 
     def query_tile(j, carry):
         lanes = pl.ds(pl.multiple_of(j * 256, 256), 256)
         part = mul(normed[...], wq[:, lanes])
-        q_out[:, lanes] = jnp.concatenate(
+        q[:, lanes] = jnp.concatenate(
             [turn(part[:, h * 128 : (h + 1) * 128], cosd[...], sind[...]) for h in range(2)],
             axis=1,
         ).astype(BF16)
@@ -789,17 +914,9 @@
     weight = jnp.exp(logits - jnp.max(logits, axis=1, keepdims=True))
     gates = weight / jnp.sum(weight, axis=1, keepdims=True)
     gates_out[...] = gates
-    expand = hot(iota((128, ROWS), 0) == iota((128, ROWS), 1) // CAP)
-    spread = exact(gates, expand)
-    slot_gates = jnp.sum(any_slot[...].astype(F32) * spread, axis=0, keepdims=True)
-    expert_of = iota((EXPERTS, ROWS), 1) // CAP == iota((EXPERTS, ROWS), 0)
-    fold = hot(iota((128, ROWS), 1) % CAP == iota((128, ROWS), 0))
-    tile = exact(jnp.where(expert_of, slot_gates, 0.0), fold, NT)
-    tiles[...] = jnp.broadcast_to(tile[:, None, :], (EXPERTS, 8, 128))
-
     for push in pushes:
         push.wait_recv()
-    kv_out[...] = kv[...]
+    stays = [moves.keep(q, q_out), moves.keep(normed, normed_out), moves.keep(kv, kv_out)]
     for g in range(HEADS_KV):
         vt[g] = kv[:, 256 + g * 128 : 384 + g * 128].T
     for g in range(HEADS_KV):
@@ -807,7 +924,7 @@
         def head(i, carry, g=g):
             h = g * REPEAT + i
             lanes = pl.ds(pl.multiple_of(h * HEAD_DIM, HEAD_DIM), HEAD_DIM)
-            s = mul(kv[:, g * 128 : (g + 1) * 128], q_out[:, lanes], NT) * SCALE + bias[...]
+            s = mul(kv[:, g * 128 : (g + 1) * 128], q[:, lanes], NT) * SCALE + bias[...]
             top = jnp.max(s, axis=0, keepdims=True)
             p = jnp.exp(s - top)
             total = jnp.sum(p, axis=0, keepdims=True)
@@ -827,18 +944,25 @@
     lax.fori_loop(0, D // 256, out_tile, 0)
     m = middle[...]
     inverse = lax.rsqrt(jnp.mean(m * m, axis=1, keepdims=True) + norm_eps)
-    nf[...] = (m * inverse * gains[1:2, :]).astype(BF16)
-
-    def dispatch_tile(j, carry):
-        lanes = pl.ds(pl.multiple_of(j * 256, 256), 256)
-        dispatch[lanes, :] = mul(any_slot[:, lanes], nf[...], TN).astype(BF16)
-        return carry
-
-    lax.fori_loop(0, ROWS // 256, dispatch_tile, 0)
-    link.drain()
-
-
-def run_forward(lengths, tokens, wq, wb, any_slot, named, cosd, sind):
+    stays += [moves.keep(attended, attended_out), moves.keep(middle, middle_out)]
+    high, mid, low = (third.astype(F32) for third in thirds(gates))
+    held = high + pltpu.roll(mid, EXPERTS, 1) + pltpu.roll(low, 2 * EXPERTS, 1)
+    nf[:, 0:LANES] = held.astype(BF16)
+    nf[:, LANES:] = (m * inverse * gains[1:2, :]).astype(BF16)
+    half_a, half_b = nf.at[:, pl.ds(0, WIDE_A)], nf.at[:, pl.ds(WIDE_A, WIDE_B)]
+    last = [moves.push(half_a, nf_a.at[y], peer) for peer in line_y]
+    last += [moves.push(half_b, nf_b.at[z], peer) for peer in line_z]
+    stays += [moves.keep(half_a, nf_a.at[y]), moves.keep(half_b, nf_b.at[z])]
+    for push in last:
+        push.wait_recv()
+    for stay in stays:
+        stay.wait()
+    for wait in dy_waits:
+        wait()
+    moves.drain()
+
+
+def run_forward(*operands):
     anywhere = pl.BlockSpec(memory_space=pl.ANY)
     inside = pl.BlockSpec(memory_space=pltpu.VMEM)
     vmem, dma = pltpu.VMEM, pltpu.SemaphoreType.DMA
@@ -855,11 +979,14 @@
             shape((16, COUNT), F32),
             shape((16, COUNT), F32),
             shape((COUNT, 128), F32),
-            shape((EXPERTS, 8, 128), F32),
-            shape((ROWS, D), BF16),
+            shape((4, COUNT, WIDE_A), BF16),
+            shape((4, COUNT, WIDE_B), BF16),
+            *(shape(piece, BF16) for piece in pieces(4, 8, width=D)),
         ),
-        in_specs=[pl.BlockSpec(memory_space=pltpu.SMEM), inside, anywhere, anywhere] + [inside] * 4,
-        out_specs=(inside,) * 10,
+        in_specs=[pl.BlockSpec(memory_space=pltpu.SMEM), inside, anywhere, anywhere]
+        + [inside] * 3
+        + [anywhere] * 4,
+        out_specs=(anywhere,) * 5 + (inside,) * 3 + (anywhere,) * 4,
         scratch_shapes=[
             vmem((D, WA), BF16),
             vmem((D, WB), BF16),
@@ -868,9 +995,19 @@
             vmem((GROUP_ROWS, COUNT), F32),
             vmem((HEADS_KV, HEAD_DIM, GROUP_ROWS), BF16),
             vmem((COUNT, D), BF16),
-            dma((3,)),
-            dma((3,)),
-            dma((3,)),
+            vmem((COUNT, D), BF16),
+            vmem((COUNT, D), F32),
+            vmem((COUNT, D), BF16),
+            vmem((COUNT, WIDE), BF16),
+            vmem((4, COUNT, SLOTS), BF16),
+            vmem((4, COUNT, SLOTS), BF16),
+            vmem((4, COUNT, HALF), BF16),
+            vmem((4, COUNT, HALF), BF16),
+            *(vmem(piece, BF16) for piece in pieces(8, 4, width=HALF) * 2),
+            dma((3 + 28 + 6,)),
+            dma((3 + 28 + 6,)),
+            dma((4 + 7,)),
+            dma((7,)),
         ],
         compiler_params=pltpu.CompilerParams(
             collective_id=3, has_side_effects=True, vmem_limit_bytes=48 * 1024 * 1024
@@ -878,7 +1015,7 @@
         cost_estimate=pl.CostEstimate(
             flops=6_000_000_000, bytes_accessed=30_000_000, transcendentals=3_200_000
         ),
-    )(lengths, tokens, wq, wb, any_slot, named, cosd, sind)
+    )(*operands)
 
 
 def norm_grad(values, gain, grad):
@@ -890,22 +1027,40 @@
 
 
 def backward_kernel(
-    lengths, tokens, cotangent, any_slot, gates, gate_back, queries, kv_in, attended, middle,
-    normed, tops, totals, cosd, sind, wq_in, wb_in, back_in, up_in, down_in,
-    grad_tokens, grad_qkv, grad_out, grad_small, up_far, down_far,
-    wq, wb, back, bias, kt, gn, gmid, gb, gatt, gp, dk, dv, leave, land, send, recv, local,
+    lengths, tokens_in, cotangent_in, gates, queries_in, kv_src, attended_in, middle_in, normed_in,
+    tops, totals, cosd, sind, wq_in, wb_in, hot_a_in, hot_b_in,
+    back_a1_in, back_a2_in, back_b1_in, back_b2_in, out1, out2, up_in, down_in,
+    output, grad_tokens, grad_qkv_out, grad_out_out, grad_small, up_far, down_far,
+    far_a1, far_a2, far_b1, far_b2,
+    tokens, cotangent, queries, kv_in, attended, middle, normed,
+    wq, wb, hot_a, hot_b, back_a1, back_a2, back_b1, back_b2,
+    part_a, part_b, land_a, land_b, late_a, late_b,
+    bias, kt, gn, gmid, gb, gatt, gp, dk, dv, leave, land, grad_qkv,
+    send, recv, local, load_sem,
 ):
-    y, z, c, x = place()
+    at = place()
+    y, z, c, x = at
+    line_y, line_z = lines(y, z, c, x)
     peers = [device(y, z, c, (x + d) % 4) for d in (1, 2, 3)]
+    pairs = (
+        (back_a1_in, back_a1), (back_a2_in, back_a2), (hot_a_in, hot_a),
+        (back_b1_in, back_b1), (back_b2_in, back_b2), (hot_b_in, hot_b),
+        (kv_src, kv_in), (wb_in, wb), (middle_in, middle), (cotangent_in, cotangent),
+        (queries_in, queries), (attended_in, attended), (tokens_in, tokens),
+        (normed_in, normed), (wq_in, wq),
+    )
     loads = [
-        pltpu.make_async_copy(back_in, back, local.at[0]),
-        pltpu.make_async_copy(wb_in, wb, local.at[1]),
-        pltpu.make_async_copy(wq_in, wq, local.at[2]),
+        pltpu.make_async_copy(src, dst, load_sem.at[i]) for i, (src, dst) in enumerate(pairs)
     ]
     for load in loads:
         load.start()
-    greet(peers)
-    link = Links(send, recv)
+    greet(cross(*at) + peers)
+    link = Moves(send, recv, local)
+    for load in loads[:6]:
+        load.wait()
+    part_waits = add_up(hot_a, back_a1, back_a2, part_a, land_a, y, line_y, link)
+    part_waits += add_up(hot_b, back_b1, back_b2, part_b, land_b, z, line_z, link)
+    part_drain = list(link.made)
     facing = (x + 2) % 4
     pushes = []
     for half, peer in ((0, peers[2]), (1, peers[0])):
@@ -915,17 +1070,25 @@
         down_rows = pl.ds(half * DOWN_HALF, DOWN_HALF)
         pushes.append(link.push(down_in.at[down_rows, lanes], down_far.at[half], peer))
     fill_bias(lengths, bias, x)
+    for load in loads[6:]:
+        load.wait()
     for g in range(HEADS_KV):
         kt[g] = kv_in[:, g * 128 : (g + 1) * 128].T
-    loads[0].wait()
-
-    def ffn_tile(j, carry):
-        lanes = pl.ds(pl.multiple_of(j * 256, 256), 256)
-        gn[:, lanes] = mul(any_slot[...], back[:, lanes])
-        return carry
-
-    lax.fori_loop(0, D // 256, ffn_tile, 0)
-    loads[1].wait()
+    for wait in part_waits:
+        wait()
+    out_waits = give_back_a(link, at, out1, far_a1, HALF)
+    out_waits += give_back_b(link, at, out1, far_b1, HALF)
+    out_waits += give_back_a(link, at, out2, far_a2, HALF)
+    out_waits += give_back_b(link, at, out2, far_b2, HALF)
+    total = land_a[0].astype(F32)
+    for s in range(1, 4):
+        total = total + land_a[s].astype(F32)
+    slopes = total[:, 0:LANES]
+    gn[:, 0 : WIDE_A - LANES] = total[:, LANES:]
+    total = land_b[0].astype(F32)
+    for s in range(1, 4):
+        total = total + land_b[s].astype(F32)
+    gn[:, WIDE_A - LANES :] = total
     gains, select = read_gains(wb[:, D:])
     moved, ffn_gain = norm_grad(middle[...], gains[1:2, :], gn[...])
     gm = cotangent[...].astype(F32) + moved
@@ -965,23 +1128,40 @@
 
     def out_tile(j, carry):
         lanes = pl.ds(pl.multiple_of(j * 256, 256), 256)
-        grad_out[lanes, :] = mul(gb[:, lanes], attended[...], TN).astype(BF16)
+        grad_qkv[lanes, 0:D] = mul(gb[:, lanes], attended[...], TN).astype(BF16)
         return carry
 
     lax.fori_loop(0, D // 256, out_tile, 0)
 
-    expert_of = iota((EXPERTS, ROWS), 1) // CAP == iota((EXPERTS, ROWS), 0)
-    fold = hot(iota((128, ROWS), 1) % CAP == iota((128, ROWS), 0))
-    wide = exact(gate_back[:, 0, :], fold)
-    slot_grads = jnp.sum(jnp.where(expert_of, wide, 0.0), axis=0, keepdims=True)
-    expand = hot(iota((128, ROWS), 0) == iota((128, ROWS), 1) // CAP)
-    gate_grad = exact(any_slot[...].astype(F32) * slot_grads, expand, NT)
+    out_kept = link.keep(grad_qkv.at[:, pl.ds(0, D)], grad_out_out)
+
+    gate_grad = slopes + pltpu.roll(slopes, 128 - EXPERTS, 1) + pltpu.roll(
+        slopes, 128 - 2 * EXPERTS, 1
+    )
     weighted = gates[...] * gate_grad
     logit_grad = weighted - gates[...] * jnp.sum(weighted, axis=1, keepdims=True)
     parts = thirds(logit_grad)
     router_grad = sum(mul(tokens[...], part, TN) for part in parts)
     small = wb[:, D:]
 
+    for wait in out_waits:
+        wait()
+    pairs = ((far_a1, back_a1), (far_a2, back_a2), (far_b1, back_b1), (far_b2, back_b2))
+    again = [
+        link.keep(src, dst.at[:, :, :, pl.ds(0, HALF)] if dst.shape[3] > HALF else dst)
+        for src, dst in pairs
+    ]
+    for copy in again:
+        copy.wait()
+    for copy in part_drain:
+        copy.wait_send()
+    width = pl.ds(0, HALF)
+    late = add_up(
+        hot_a, back_a1, back_a2, part_a, late_a, y, line_y, link
+    ) + add_up(
+        hot_b, back_b1.at[:, :, :, width], back_b2.at[:, :, :, width],
+        part_b.at[:, :, width], late_b, z, line_z, link,
+    )
     for push in kv_pushes:
         push.wait_recv()
     mine = pl.ds(pl.multiple_of(x * COUNT, COUNT), COUNT)
@@ -993,7 +1173,7 @@
             total[:, 0:128], cosd[...], -sind[...]
         ).astype(BF16)
         gp[:, D + 256 + g * 128 : D + 384 + g * 128] = total[:, 128:256].astype(BF16)
-    loads[2].wait()
+    out_kept.wait()
 
     def qkv_tile(j, carry):
         lanes = pl.ds(pl.multiple_of(j * 256, 256), 256)
@@ -1002,6 +1182,7 @@
         return carry
 
     lax.fori_loop(0, D // 256, qkv_tile, 0)
+    stays = [link.keep(grad_qkv, grad_qkv_out)]
     moved, attn_gain = norm_grad(tokens[...].astype(F32), gains[0:1, :], gn[...])
     from_router = sum(mul(part, small, NT) for part in parts)
     grad_tokens[...] = (gmid[...] + moved + from_router).astype(BF16)
@@ -1010,9 +1191,19 @@
     )
     gain_columns = sum(mul(part, select, TN) for part in thirds(both))
     grad_small[...] = (router_grad + gain_columns).astype(BF16)
+    for wait in late:
+        wait()
+    for half, landed in enumerate((late_a, late_b)):
+        lanes = slice(half * HALF, (half + 1) * HALF)
+        total = middle[:, lanes]
+        for s in range(4):
+            total = total + landed[s].astype(F32)
+        output[:, lanes] = total.astype(BF16)
     for push in pushes:
         push.wait_recv()
-    link.drain()
+    for stay in stays:
+        stay.wait()
+    link.drain(skip=part_drain)
 
 
 def run_backward(*operands):
@@ -1025,18 +1216,41 @@
         name="backward",
         out_shape=(
             shape((COUNT, D), BF16),
+            shape((COUNT, D), BF16),
             shape((D, WA), BF16),
             shape((D, D), BF16),
             shape((D, SMALL), BF16),
             shape((2, UP_HALF, 2 * FF), BF16),
             shape((2, DOWN_HALF, DOWN_PART), BF16),
+            *(shape(piece, BF16) for piece in pieces(8, 4, width=HALF) * 2),
         ),
-        in_specs=[pl.BlockSpec(memory_space=pltpu.SMEM)] + [inside] * 14 + [anywhere] * 5,
-        out_specs=(inside,) * 4 + (anywhere,) * 2,
+        in_specs=[pl.BlockSpec(memory_space=pltpu.SMEM)]
+        + [anywhere] * 2
+        + [inside]
+        + [anywhere] * 5
+        + [inside] * 4
+        + [anywhere] * 12,
+        out_specs=(inside, inside, anywhere, anywhere, inside) + (anywhere,) * 6,
         scratch_shapes=[
+            vmem((COUNT, D), BF16),
+            vmem((COUNT, D), BF16),
+            vmem((COUNT, D), BF16),
+            vmem((GROUP_ROWS, 512), BF16),
+            vmem((COUNT, D), BF16),
+            vmem((COUNT, D), F32),
+            vmem((COUNT, D), BF16),
             vmem((D, WA), BF16),
             vmem((D, WB), BF16),
-            vmem((ROWS, D), BF16),
+            vmem((4, COUNT, SLOTS), BF16),
+            vmem((4, COUNT, SLOTS), BF16),
+            *(vmem(piece, BF16) for piece in pieces(8, 4, width=WIDE_A)),
+            *(vmem(piece, BF16) for piece in pieces(8, 4, width=WIDE_B)),
+            vmem((3, COUNT, WIDE_A), BF16),
+            vmem((3, COUNT, WIDE_B), BF16),
+            vmem((4, COUNT, WIDE_A), BF16),
+            vmem((4, COUNT, WIDE_B), BF16),
+            vmem((4, COUNT, HALF), BF16),
+            vmem((4, COUNT, HALF), BF16),
             vmem((GROUP_ROWS, COUNT), F32),
             vmem((HEADS_KV, HEAD_DIM, GROUP_ROWS), BF16),
             vmem((COUNT, D), F32),
@@ -1048,12 +1262,14 @@
             vmem((GROUP_ROWS, HEAD_DIM), F32),
             vmem((HEADS_KV, GROUP_ROWS, 256), BF16),
             vmem((HEADS_KV, 3, COUNT, 256), BF16),
-            dma((10,)),
-            dma((10,)),
-            dma((3,)),
+            vmem((D, WA), BF16),
+            dma((6 + 4 + 28 + 6 + 6,)),
+            dma((6 + 4 + 28 + 6 + 6,)),
+            dma((4 + 4 + 2,)),
+            dma((15,)),
         ],
         compiler_params=pltpu.CompilerParams(
-            collective_id=4, has_side_effects=True, vmem_limit_bytes=58 * 1024 * 1024
+            collective_id=4, has_side_effects=True, vmem_limit_bytes=60 * 1024 * 1024
         ),
         cost_estimate=pl.CostEstimate(
             flops=13_000_000_000, bytes_accessed=50_000_000, transcendentals=3_200_000
@@ -1074,12 +1290,6 @@
         jnp.where(seq_ends[None, :] <= row_ids[:, None], seq_lens[None, :], 0), axis=1
     )
     return (segment, row_ids - seq_start)
-
-
-def exchange(rows):
-    return lax.all_to_all(
-        rows.reshape(EXPERTS, CAP, D), "expert", split_axis=0, concat_axis=0, tiled=True
-    ).reshape(EXPERTS * CAP, D)
 
 
 def body(
@@ -1105,24 +1315,23 @@
     cosd = jnp.concatenate([cosine, cosine], axis=1)
     sind = jnp.concatenate([-sine, sine], axis=1)
 
-    full_a, full_b, named, any_slot, dy_rows = gather_weights(pack, top_experts, cotangent)
-    dy_rows = exchange(dy_rows)
+    full_a, full_b, named, hot_a, hot_b, dy_a, dy_b = gather_weights(
+        pack, top_experts, cotangent
+    )
     wq = full_a.reshape(D, WA)
     wb = full_b.reshape(D, WB)
-    queries, kv, attended, middle, normed, tops, totals, gates, tiles, dispatch = run_forward(
-        lengths, tokens, wq, wb, any_slot, named, cosd, sind
-    )
-    back, gate_back, expert_out, up_local, down_local = run_experts(
-        dispatch.reshape(EXPERTS, CAP, D),
-        tiles,
-        dy_rows.reshape(EXPERTS, CAP, D),
-        gate_up,
-        down_proj,
-    )
-    returned = exchange(expert_out)
-    grad_tokens, grad_qkv, grad_out, grad_small, up_far, down_far = run_backward(
-        lengths, tokens, cotangent, any_slot, gates, gate_back, queries, kv, attended, middle,
-        normed, tops, totals, cosd, sind, wq, wb, back.reshape(ROWS, D), up_local, down_local,
+    (
+        queries, kv, attended, middle, normed, tops, totals, gates, nf_a, nf_b, dy1, dy2,
+    ) = run_forward(
+        lengths, tokens, wq, wb, named, cosd, sind, hot_a, hot_b, dy_a, dy_b
+    )
+    back_a1, back_a2, back_b1, back_b2, out1, out2, up_local, down_local = run_experts(
+        hot_a, hot_b, nf_a, nf_b, dy1, dy2, gate_up, down_proj
+    )
+    output, grad_tokens, grad_qkv, grad_out, grad_small, up_far, down_far, *_ = run_backward(
+        lengths, tokens, cotangent, gates, queries, kv, attended, middle, normed, tops, totals,
+        cosd, sind, wq, wb, hot_a, hot_b, back_a1, back_a2, back_b1, back_b2, out1, out2,
+        up_local, down_local,
     )
     sum_a, sum_b, up_sum, down_sum = scatter_sums(
         grad_qkv.reshape(4, 4, 2, BLOCK, WA),
@@ -1135,11 +1344,6 @@
     )
     sum_b = sum_b[:PIECE]
 
-    expand = jnp.arange(ROWS) // CAP == jnp.arange(128)[:, None]
-    mix = jnp.dot(gates.astype(BF16), expand.astype(BF16), preferred_element_type=F32)
-    mix = (mix * any_slot.astype(F32)).astype(BF16)
-    combined = jnp.dot(mix, returned, preferred_element_type=F32)
-    output = (middle + combined).astype(BF16)
     return (
         output,
         grad_tokens,

time: 420 us -> 383 us (0.912)
  starting transfers between devices: 26.2 us -> 0 us
  waiting for transfers between devices: 10.1 us -> 0 us
  Pallas kernels: 344 us -> 354 us
  local copies, waits for them, and re-layouts: 31.9 us -> 24.7 us
  matrix products: 5.57 us -> 0 us
    pallas_call x1, Pallas kernels: 144 us -> 84.6 us  [run_experts(): pl.pallas_call(experts_kernel, name='experts', out_shape=tuple((jax.Shape...]
    pallas_call x1, Pallas kernels: 50.6 us -> 84.5 us  [run_backward(): pl.pallas_call(backward_kernel, name='backward', out_shape=(shape((COUNT,...]
    all_to_all x2 -> x0, starting transfers between devices: 26.2 us -> none  [exchange(): lax.all_to_all(rows.reshape(EXPERTS, CAP, D), 'expert', split_axis=0, con...]
    pallas_call x1, Pallas kernels: 52.3 us -> 71.8 us  [gather_weights(): pl.pallas_call(gather_kernel, name='gather_weights', out_shape=(jax.Shape...]
    pallas_call x1, Pallas kernels: 41.5 us -> 59.9 us  [run_forward(): pl.pallas_call(forward_kernel, name='forward', out_shape=(shape((COUNT, D...]
    all_to_all x2 -> x0, waiting for transfers between devices: 10.1 us -> none  [exchange(): lax.all_to_all(rows.reshape(EXPERTS, CAP, D), 'expert', split_axis=0, con...]
    unnamed x51 -> x54, local copies, waits for them, and re-layouts: 27.5 us -> 20.3 us
    dot_general x1 -> x0, matrix products: 5.57 us -> none  [body(): combined = jnp.dot(mix, returned, preferred_element_type=F32)]
  transfers between devices with their start and end apart: 2 -> 0, of which waited for: 1 -> 0; matrix products, arithmetic and copies ran while one was open for 1% -> 0% of each run, Pallas kernels for 35% -> 0%
where the time goes in v4:
time: 383 us; the launch traced here: 382 us
  Pallas kernels  354 us (92%)
  local copies, waits for them, and re-layouts  24.7 us (6%)
    pallas_call x1, Pallas kernels, run_experts(): pl.pallas_call(experts_kernel, name='experts', out_shape=tuple((jax.Shape...  84.6 us
    pallas_call x1, Pallas kernels, run_backward(): pl.pallas_call(backward_kernel, name='backward', out_shape=(shape((COUNT,...  84.5 us
    pallas_call x1, Pallas kernels, gather_weights(): pl.pallas_call(gather_kernel, name='gather_weights', out_shape=(jax.Shape...  71.8 us
    pallas_call x1, Pallas kernels, run_forward(): pl.pallas_call(forward_kernel, name='forward', out_shape=(shape((COUNT, D...  59.9 us
    pallas_call x1, Pallas kernels, scatter_sums(): pl.pallas_call(scatter_kernel, name='scatter_sums', out_shape=(jax.ShapeD...  53.5 us
    unnamed x54, local copies, waits for them, and re-layouts  20.3 us

profile of v4, /device:TPU:0, one launch (start us, length us, event | category | flops | bytes accessed | tf_op | source)
XLA Modules:
  0.0 382.4 jit_solution(15120310817259693599)
XLA Ops:
  0.6 0.0 copy-start.8
  0.7 0.0 copy-start.3
  0.7 0.0 copy-start.13
  0.7 0.9 reduce-window.8
  1.6 0.7 select_reduce_fusion
  2.4 0.7 copy.26
  3.1 0.8 copy.27
  3.9 1.0 concatenate.9
  4.9 0.8 copy.28.top_experts
  5.7 0.5 fusion
  6.3 0.1 pad_maximum_fusion
  6.4 0.0 copy-start.6
  6.4 0.0 copy-start.7
  6.4 0.0 copy-done.3
  6.4 71.8 %gather_weights.1 = (bf16[4,4,2,48,2048]{4,3,2,1,0:T(8,128)(2,1)S(1)}, bf16[4,4,2,48,1664]{4,3,2,1,0:T(8,128)(2,1)S(1)}, f32[256,128]{1,0:T(8,128)S(1)}, bf16[4,...) custom-call(bf16[16,3712]{1,0:T(8,128)(2,1)S(1)} %pad.4.pack, ...), custom_call_target="tpu_custom_call" | custom-call | bytes 24000000 | tf_op jit(solution)/shard_map/gather_weights/pallas_call | solution.py:262
  78.3 0.0 copy-start.9
  78.3 2.7 copy-done.9
  80.9 2.2 copy-done.10
  83.2 1.1 copy-done.11
  84.3 1.1 copy-done.12
  85.4 0.0 copy-done.8
  85.4 0.0 copy-done.13
  85.4 59.9 %forward.1 = (bf16[256,1536]{1,0:T(8,128)(2,1)S(1)}, bf16[1024,512]{1,0:T(8,128)(2,1)}, bf16[256,1536]{1,0:T(8,128)(2,1)S(1)}, f32[256,1536]{1,0:T(8,128)}, bf16...) custom-call(s32[1,4]{1,0:T(1,128)S(1)} %copy-done.8, ...), custom_call_target="tpu_custom_call" | custom-call | flops 6000000000 | bytes 30000000 | tf_op jit(solution)/shard_map/forward/pallas_call | solution.py:970
  145.4 0.0 copy-done.6
  145.4 0.0 copy-done.7
  145.4 0.0 copy-done.14
  145.4 0.0 copy-done.15
  145.4 0.0 copy-start.17
  145.5 0.9 copy-done.17
  146.3 0.9 copy-done.18
  147.2 84.6 %experts.1 = (bf16[8,4,32,768]{3,2,1,0:T(8,128)(2,1)}, bf16[8,4,16,768]{3,2,1,0:T(8,128)(2,1)}, bf16[8,4,32,896]{3,2,1,0:T(8,128)(2,1)}, bf16[8,4,16,896]{3,2,1,...) custom-call(bf16[4,256,384]{2,1,0:T(8,128)(2,1)} %copy-done.14, ...), custom_call_target="tpu_custom_call" | custom-call | flops 32999999488 | bytes 60000000 | tf_op jit(solution)/shard_map/experts/pallas_call | solution.py:798
  231.9 84.5 %backward.1 = (bf16[256,1536]{1,0:T(8,128)(2,1)}, bf16[256,1536]{1,0:T(8,128)(2,1)}, bf16[1536,2048]{1,0:T(8,128)(2,1)}, bf16[1536,1536]{1,0:T(8,128)(2,1)}, bf1...) custom-call(s32[1,4]{1,0:T(1,128)} %lengths.3, ...), custom_call_target="tpu_custom_call" | custom-call | flops 12999999488 | bytes 50000000 | tf_op jit(solution)/shard_map/backward/pallas_call | solution.py:1214
  316.4 0.0 copy-done.1
  316.4 0.0 copy-start
  316.4 2.3 copy-done
  318.7 1.3 copy-done.2
  320.0 1.1 copy-done.4
  321.0 1.0 copy-done.5
  322.0 53.5 %scatter_sums.1 = (f32[16,2048]{1,0:T(8,128)S(1)}, f32[16,1664]{1,0:T(8,128)S(1)}, f32[384,1536]{1,0:T(8,128)S(1)}, f32[768,384]{1,0:T(8,128)S(1)}) custom-call(bf16[4,4,2,48,2048]{4,3,2,1,0:T(8,128)(2,1)} %bitcast.27, bf16[4,4,2,48,1536]{4,3,2,1,0:T(8,128)(2,1)S(1)} %bitcast.16, bf16[4,4,2,48,128]{4,3,2,1,0:T(8,128)(2,1)S(1)} %bitcast.19, ...), custom_call_target="tpu_custom_call" | custom-call | bytes 24000000 | tf_op jit(solution)/shard_map/scatter_sums/pallas_call | solution.py:486
  375.6 0.0 copy-start.22
  375.6 0.7 slice_reduce_fusion
  376.3 0.6 slice.24
  376.9 0.6 slice_bitcast_fusion
  377.5 0.9 copy.34
  378.4 0.9 copy.35
  379.3 0.7 copy.36
  380.0 1.4 copy.37
  381.4 1.0 copy.38
  (26 shorter events, 0.1 us)
Async XLA Ops:
  0.6 84.8 %copy-start.8 = (s32[1,4]{1,0:T(1,128)S(1)}, s32[1,4]{1,0:T(1,128)}, u32[]{:S(2)}) copy-start(s32[1,4]{1,0:T(1,128)} %lengths.3) | copy-start | bytes 52
  0.7 5.8 %copy-start.3 = (bf16[256,1536]{1,0:T(8,128)(2,1)S(1)}, bf16[256,1536]{1,0:T(8,128)(2,1)}, u32[]{:S(2)}) copy-start(bf16[256,1536]{1,0:T(8,128)(2,1)} %cotangent_in.1) | copy-start | bytes 2359300
  0.7 84.8 %copy-start.13 = (bf16[256,1536]{1,0:T(8,128)(2,1)S(1)}, bf16[256,1536]{1,0:T(8,128)(2,1)}, u32[]{:S(2)}) copy-start(bf16[256,1536]{1,0:T(8,128)(2,1)} %tokens_in.1) | copy-start | bytes 2359300
  6.4 139.0 %copy-start.6 = (f32[256,128]{1,0:T(8,128)}, f32[256,128]{1,0:T(8,128)S(1)}, u32[]{:S(2)}) copy-start(f32[256,128]{1,0:T(8,128)S(1)} %get-tuple-element.90.cosd) | copy-start | bytes 393220
  6.4 139.0 %copy-start.7 = (f32[256,128]{1,0:T(8,128)}, f32[256,128]{1,0:T(8,128)S(1)}, u32[]{:S(2)}) copy-start(f32[256,128]{1,0:T(8,128)S(1)} %get-tuple-element.91.sind) | copy-start | bytes 393220
  78.3 2.7 copy-start.9
  80.9 2.2 copy-start.10
  83.2 1.1 copy-start.11
  84.3 1.1 copy-start.12
  85.4 60.0 %copy-start.14 = (bf16[4,256,384]{2,1,0:T(8,128)(2,1)}, bf16[4,256,384]{2,1,0:T(8,128)(2,1)S(1)}, u32[]{:S(2)}) copy-start(bf16[4,256,384]{2,1,0:T(8,128)(2,1)S(1)} %get-tuple-element.50.hot_a_in) | copy-start | bytes 2359300
  85.4 60.0 %copy-start.15 = (bf16[4,256,384]{2,1,0:T(8,128)(2,1)}, bf16[4,256,384]{2,1,0:T(8,128)(2,1)S(1)}, u32[]{:S(2)}) copy-start(bf16[4,256,384]{2,1,0:T(8,128)(2,1)S(1)} %get-tuple-element.51.hot_b_in) | copy-start | bytes 2359300
  145.4 0.9 copy-start.17
  146.3 0.9 copy-start.18
  147.2 84.6 %copy-start.16 = (bf16[256,1536]{1,0:T(8,128)(2,1)}, bf16[256,1536]{1,0:T(8,128)(2,1)S(1)}, u32[]{:S(2)}) copy-start(bf16[256,1536]{1,0:T(8,128)(2,1)S(1)} %get-tuple-element.55.queries_in) | copy-start | bytes 2359300
  147.2 84.6 %copy-start.19 = (f32[256,128]{1,0:T(8,128)}, f32[256,128]{1,0:T(8,128)S(1)}, u32[]{:S(2)}) copy-start(f32[256,128]{1,0:T(8,128)S(1)} %get-tuple-element.54.gates) | copy-start | bytes 393220
  147.2 84.6 %copy-start.20 = (f32[16,256]{1,0:T(8,128)}, f32[16,256]{1,0:T(8,128)S(1)}, u32[]{:S(2)}) copy-start(f32[16,256]{1,0:T(8,128)S(1)} %get-tuple-element.60.tops) | copy-start | bytes 49156
  147.2 84.6 %copy-start.21 = (f32[16,256]{1,0:T(8,128)}, f32[16,256]{1,0:T(8,128)S(1)}, u32[]{:S(2)}) copy-start(f32[16,256]{1,0:T(8,128)S(1)} %get-tuple-element.61.totals) | copy-start | bytes 49156
  231.8 84.5 %copy-start.1 = (bf16[768,1536]{1,0:T(8,128)(2,1)S(1)}, bf16[768,1536]{1,0:T(8,128)(2,1)}, u32[]{:S(2)}) copy-start(bf16[768,1536]{1,0:T(8,128)(2,1)} %get-tuple-element.73.down_in) | copy-start | bytes 7077892
  316.4 2.3 copy-start
  318.7 1.3 copy-start.2
  320.0 1.1 copy-start.4
  321.0 1.0 copy-start.5
  322.0 55.5 %copy-start.23 = (bf16[256,1536]{1,0:T(8,128)(2,1)S(1)}, bf16[256,1536]{1,0:T(8,128)(2,1)}, u32[]{:S(2)}) copy-start(bf16[256,1536]{1,0:T(8,128)(2,1)} %get-tuple-element.101) | copy-start | bytes 2359300
  375.6 2.8 copy-start.22

commit v5 on v4

--- a/solution.py
+++ b/solution.py
@@ -68,10 +68,9 @@
         self.made.append(copy)
         return copy
 
-    def drain(self, skip=()):
+    def drain(self):
         for copy in self.made:
-            if not any(copy is done for done in skip):
-                copy.wait_send()
+            copy.wait_send()
 
 
 def neighbours(y, z, c, x):
@@ -129,9 +128,9 @@
 
 def slot_hits(slot_of, hits, experts):
     p = iota((1, SLOTS), 1)
-    q = p - 8 * FIRST
-    wanted = jnp.where(p < 8 * FIRST, p % FIRST, FIRST + q % SECOND).astype(F32)
-    local = jnp.where(p < 8 * FIRST, p // FIRST, q // SECOND)
+    q = p % PIECE_SLOTS
+    wanted = ((p // PIECE_SLOTS) * PART + q % PART).astype(F32)
+    local = q // PART
     expand = hot(iota((128, SLOTS), 0) == experts(local))
 
     def step(s, carry):
@@ -152,6 +151,17 @@
     link = Links(send, recv)
     first = [link.push(pack, xbuf.at[x], near["x"][d]) for d in range(3)]
     xbuf[pl.ds(x, 1)] = pack[...][None]
+    half_a, half_b = cotangent.at[:, pl.ds(0, HALF)], cotangent.at[:, pl.ds(HALF, HALF)]
+    kept = [
+        pltpu.make_async_copy(half_a, dy_a.at[y], local.at[2]),
+        pltpu.make_async_copy(half_b, dy_b.at[z], local.at[3]),
+    ]
+    for copy in kept:
+        copy.start()
+    dys = [
+        around(link, half_a, dy_a, y, *near["y"]),
+        around(link, half_b, dy_b, z, *near["z"]),
+    ]
     for copy in first:
         copy.wait_recv()
     select = pick_rows(BLOCK, 4 * PADDED, PIECE, PADDED)
@@ -212,15 +222,7 @@
         j["up"] = link.push(line, line, plus)
         j["down"] = link.push(line, line, minus)
         j["core"].append(link.push(block, block, near["core"]))
-    half_a, half_b = cotangent.at[:, pl.ds(0, HALF)], cotangent.at[:, pl.ds(HALF, HALF)]
-    kept = [
-        pltpu.make_async_copy(half_a, dy_a.at[y], local.at[2]),
-        pltpu.make_async_copy(half_b, dy_b.at[z], local.at[3]),
-    ]
-    for copy in kept:
-        copy.start()
-    dys = [link.push(half_a, dy_a.at[y], peer) for peer in line_y]
-    dys += [link.push(half_b, dy_b.at[z], peer) for peer in line_z]
+    dys = dys[0]() + dys[1]()
     for copy in slots:
         copy.wait_recv()
     slot_hits(slot_y, hot_a, lambda e: y * 8 + e)
@@ -248,8 +250,8 @@
     for j in jobs:
         for copy in j["core"]:
             copy.wait_recv()
-    for copy in dys:
-        copy.wait_recv()
+    for wait in dys:
+        wait()
     for copy in kept:
         copy.wait()
     link.drain()
@@ -257,8 +259,8 @@
 
 def gather_weights(pack, top_experts, cotangent):
     inside = pl.BlockSpec(memory_space=pltpu.VMEM)
-    anywhere = pl.BlockSpec(memory_space=pl.ANY)
-    copies = 3 + 2 * 16 + 12
+    anywhere = pl.BlockSpec(memory_space=pltpu.HBM)
+    copies = 3 + 2 * 16 + 6 + 8
     return pl.pallas_call(
         gather_kernel,
         name="gather_weights",
@@ -271,7 +273,7 @@
             jax.ShapeDtypeStruct((4, COUNT, HALF), BF16),
             jax.ShapeDtypeStruct((4, COUNT, HALF), BF16),
         ),
-        in_specs=[inside, inside, anywhere],
+        in_specs=[inside, inside, inside],
         out_specs=(anywhere, anywhere, inside, inside, inside, anywhere, anywhere),
         scratch_shapes=[
             pltpu.VMEM((4, PADDED, WA + WB), BF16),
@@ -285,7 +287,7 @@
             pltpu.SemaphoreType.DMA((4,)),
         ],
         compiler_params=pltpu.CompilerParams(
-            collective_id=0, has_side_effects=True, vmem_limit_bytes=24 * 1024 * 1024
+            collective_id=0, has_side_effects=True, vmem_limit_bytes=60 * 1024 * 1024
         ),
         cost_estimate=pl.CostEstimate(flops=0, bytes_accessed=24_000_000, transcendentals=0),
     )(pack, top_experts, cotangent)
@@ -303,15 +305,17 @@
 
 
 def scatter_kernel(
-    ga, gb, gs, up_in, down_in, up_far, down_far, out_a, out_b, up_out, down_out,
+    ga, gb, gs, up_in, down_in, up_far, down_far, late_a, late_b, came_a, came_b, middle,
+    out_a, out_b, up_out, down_out, output,
     core_a, core_b, mine_a, mine_b, one_a, one_b, two_a, two_b,
     half_a0, half_a1, half_b0, half_b1, last_a, last_b, xout, xin,
-    ups, downs, up_got, down_got, up_land, down_land,
+    ups, downs, up_got, down_got, up_land, down_land, mid, land_a, land_b,
     send, recv, local,
 ):
     y, z, c, x = place()
     near = neighbours(y, z, c, x)
-    greet(everyone_near(near))
+    line_y, line_z = lines(y, z, c, x)
+    greet(everyone_near(near) + [line_y[1], line_z[1]])
     link = Links(send, recv)
     other = 1 - c
     jobs = [
@@ -340,18 +344,30 @@
                 kept.start()
                 j[step].append((pushed, kept))
 
+    late = []
+    first, second = pl.ds(0, COUNT // 2), pl.ds(COUNT // 2, COUNT // 2)
+    for src, dst, me, line in ((late_a, land_a, y, line_y), (late_b, land_b, z, line_z)):
+        for d in (1, 2, 3):
+            late.append(link.push(src.at[(me + d) % 4], dst.at[me, second], line[d - 1]))
     fetches = []
     for i, d in enumerate((3, 1, 0)):
         part = (x + d) % 4
         up_rows = pl.ds(pl.multiple_of(part * UP_PART, UP_PART), UP_PART)
         lanes = pl.ds(pl.multiple_of(part * DOWN_PART, 128), DOWN_PART)
-        fetches.append(pltpu.make_async_copy(up_in.at[up_rows], ups.at[i], local.at[slots]))
-        fetches.append(
-            pltpu.make_async_copy(down_in.at[:, lanes], downs.at[i], local.at[slots + 1])
-        )
-        slots += 2
-    fetches.append(pltpu.make_async_copy(up_far, up_got, local.at[slots]))
-    fetches.append(pltpu.make_async_copy(down_far, down_got, local.at[slots + 1]))
+        fetches.append((up_in.at[up_rows], ups.at[i]))
+        fetches.append((down_in.at[:, lanes], downs.at[i]))
+    fetches += [
+        (up_far, up_got),
+        (down_far, down_got),
+        (middle, mid),
+        (came_a, land_a.at[:, first]),
+        (came_b, land_b.at[:, first]),
+        (late_a.at[y], land_a.at[y, second]),
+        (late_b.at[z], land_b.at[z, second]),
+    ]
+    fetches = [
+        pltpu.make_async_copy(src, dst, local.at[slots + i]) for i, (src, dst) in enumerate(fetches)
+    ]
     for fetch in fetches:
         fetch.start()
     for fetch in fetches:
@@ -455,11 +471,19 @@
         push.wait_recv()
     up_out[...] = ups[2].astype(F32) + up_land[0].astype(F32) + up_land[1].astype(F32)
     down_out[...] = downs[2].astype(F32) + down_land[0].astype(F32) + down_land[1].astype(F32)
+    for push in late:
+        push.wait_recv()
+    for half, landed in enumerate((land_a, land_b)):
+        lanes = slice(half * HALF, (half + 1) * HALF)
+        total = mid[:, lanes]
+        for s in range(4):
+            total = total + landed[s].astype(F32)
+        output[:, lanes] = total.astype(BF16)
     link.drain()
 
 
 def scatter_sums(*operands):
-    copies = 2 * (4 + 4 + 4) + 4 + 3 + 4
+    copies = 2 * (4 + 4 + 4) + 4 + 3 + 6 + 4
     vmem = pltpu.VMEM
     scratch = []
     for shape in ((4, 4), (4, 4), (2, 2), (2, 4)):
@@ -479,9 +503,12 @@
         vmem((2, DOWN_HALF, DOWN_PART), BF16),
         vmem((2, UP_PART, 2 * FF), BF16),
         vmem((2, FF, DOWN_PART), BF16),
+        vmem((COUNT, D), F32),
+        vmem((4, COUNT, HALF), BF16),
+        vmem((4, COUNT, HALF), BF16),
         pltpu.SemaphoreType.DMA((copies,)),
         pltpu.SemaphoreType.DMA((copies,)),
-        pltpu.SemaphoreType.DMA((20,)),
+        pltpu.SemaphoreType.DMA((12 + 13,)),
     ]
     return pl.pallas_call(
         scatter_kernel,
@@ -491,12 +518,13 @@
             jax.ShapeDtypeStruct((PADDED, WB), F32),
             jax.ShapeDtypeStruct((UP_PART, 2 * FF), F32),
             jax.ShapeDtypeStruct((FF, DOWN_PART), F32),
+            jax.ShapeDtypeStruct((COUNT, D), BF16),
         ),
-        in_specs=[pl.BlockSpec(memory_space=pl.ANY)] * 7,
-        out_specs=(pl.BlockSpec(memory_space=pltpu.VMEM),) * 4,
+        in_specs=[pl.BlockSpec(memory_space=pltpu.HBM)] * 12,
+        out_specs=(pl.BlockSpec(memory_space=pltpu.VMEM),) * 5,
         scratch_shapes=scratch,
         compiler_params=pltpu.CompilerParams(
-            collective_id=1, has_side_effects=True, vmem_limit_bytes=40 * 1024 * 1024
+            collective_id=1, has_side_effects=True, vmem_limit_bytes=60 * 1024 * 1024
         ),
         cost_estimate=pl.CostEstimate(flops=0, bytes_accessed=24_000_000, transcendentals=0),
     )(*operands)
@@ -504,10 +532,11 @@
 
 ROWS = EXPERTS * CAP
 TILE = 256
-FIRST = 32
-SECOND = 16
-PIECES = (FIRST, SECOND)
+PARTS = 3
+PART = CAP // PARTS
 SLOTS = 8 * CAP
+PIECE_SLOTS = 8 * PART
+PIECE_ROWS = EXPERTS * PART
 HALF = D // 2
 LANES = 128
 WIDE = D + LANES
@@ -559,64 +588,61 @@
 
 
 def to_slots(hits, rows, stage, piece):
-    n = PIECES[piece]
-    columns = slice(0, 8 * FIRST) if piece == 0 else slice(8 * FIRST, SLOTS)
+    columns = slice(piece * PIECE_SLOTS, (piece + 1) * PIECE_SLOTS)
     for s in range(4):
         taken = mul(hits[s, :, columns], rows[s], TN).astype(BF16)
-        stage[:, s] = taken.reshape(8, n, taken.shape[1])
-
-
-def deliver(moves, at, stage_a, stage_b, rows, split):
+        stage[piece, :, s] = taken.reshape(8, PART, taken.shape[1])
+
+
+def deliver(moves, at, stage_a, stage_b, rows, split, piece):
     y, z, c, x = at
     along_z, along_y = faces(y, z, c, x)
-    width = rows.shape[3]
+    width = rows.shape[4]
     waits = []
     for i, (where, zt, ct) in enumerate(along_z):
-        dst = rows.at[z, pl.ds(c * 4, 4), :, pl.ds(0, split)]
-        waits.append(moves.send_or_keep(i, stage_a.at[zt * 2 + ct], dst, where))
+        dst = rows.at[piece, z, pl.ds(c * 4, 4), :, pl.ds(0, split)]
+        waits.append(moves.send_or_keep(i, stage_a.at[piece, zt * 2 + ct], dst, where))
     for i, (where, yt, ct) in enumerate(along_y):
-        dst = rows.at[:, c * 4 + y, :, pl.ds(split, width - split)]
-        waits.append(moves.send_or_keep(i, stage_b.at[yt * 2 + ct], dst, where))
+        dst = rows.at[piece, :, c * 4 + y, :, pl.ds(split, width - split)]
+        waits.append(moves.send_or_keep(i, stage_b.at[piece, yt * 2 + ct], dst, where))
     return waits
 
 
-def give_back_a(moves, at, rows, back_a, split):
+def give_back(moves, at, rows, back_a, back_b, split, piece):
     y, z, c, x = at
-    along_z, _ = faces(y, z, c, x)
-    return [
-        moves.send_or_keep(
-            i, rows.at[zt, pl.ds(ct * 4, 4), :, pl.ds(0, split)], back_a.at[z * 2 + c], where
-        )
-        for i, (where, zt, ct) in enumerate(along_z)
-    ]
-
-
-def give_back_b(moves, at, rows, back_b, split):
-    y, z, c, x = at
-    _, along_y = faces(y, z, c, x)
-    width = rows.shape[3]
-    return [
-        moves.send_or_keep(
-            i, rows.at[:, ct * 4 + yt, :, pl.ds(split, width - split)], back_b.at[y * 2 + c], where
-        )
-        for i, (where, yt, ct) in enumerate(along_y)
-    ]
-
-
-def add_up(hits, back_1, back_2, parts, land, me, line, moves):
+    along_z, along_y = faces(y, z, c, x)
+    width = rows.shape[4]
     waits = []
-    for d in (1, 2, 3, 0):
-        s = (me + d) % 4
-        first, second = back_1[:, s], back_2[:, s]
-        width = first.shape[2]
-        total = mul(hits[s, :, : 8 * FIRST], first.reshape(8 * FIRST, width))
-        total = total + mul(hits[s, :, 8 * FIRST :], second.reshape(8 * SECOND, width))
-        if d == 0:
-            land[pl.ds(s, 1)] = total.astype(BF16)[None]
-        else:
-            parts[d - 1] = total.astype(BF16)
-            waits.append(moves.push(parts.at[d - 1], land.at[me], line[d - 1]).wait_recv)
+    for i, (where, zt, ct) in enumerate(along_z):
+        src = rows.at[piece, zt, pl.ds(ct * 4, 4), :, pl.ds(0, split)]
+        dst = back_a.at[piece, z * 2 + c, :, :, pl.ds(0, split)]
+        waits.append(moves.send_or_keep(i, src, dst, where))
+    for i, (where, yt, ct) in enumerate(along_y):
+        src = rows.at[piece, :, ct * 4 + yt, :, pl.ds(split, width - split)]
+        dst = back_b.at[piece, y * 2 + c, :, :, pl.ds(0, width - split)]
+        waits.append(moves.send_or_keep(i, src, dst, where))
     return waits
+
+
+def add_up(hits, back, s, width):
+    rows = back[:, :, s, :, 0:width].reshape(SLOTS, width)
+    return mul(hits[s], rows).astype(BF16)
+
+
+def around(link, own, land, me, plus, minus):
+    up = link.push(own, land.at[me], plus)
+    down = link.push(own, land.at[me], minus)
+
+    def forward():
+        half = COUNT // 2
+        up.wait_recv()
+        block = land.at[(me + 3) % 4, pl.ds(0, half)]
+        waits = [link.push(block, block, plus).wait_recv]
+        down.wait_recv()
+        block = land.at[(me + 1) % 4, pl.ds(half, half)]
+        return waits + [link.push(block, block, minus).wait_recv]
+
+    return forward
 
 
 def gelu_parts(g):
@@ -628,10 +654,10 @@
 
 
 def experts_kernel(
-    hot_a_in, hot_b_in, nf_a_in, nf_b_in, dy1_in, dy2_in, gate_up, down,
-    back_a1, back_a2, back_b1, back_b2, out1, out2, up_out, down_out,
-    hot_a, hot_b, nf_a, nf_b, sa1, sa2, sb1, sb2, rows1, rows2, dy1, dy2,
-    gu, dn, grads, mixed, ghid, grow1, grow2, eo1, eo2, up_grad, down_grad,
+    hot_a_in, hot_b_in, nf_a_in, nf_b_in, dy_in, gate_up, down,
+    back_a, back_b, out, up_out, down_out,
+    hot_a, hot_b, nf_a, nf_b, stage_a, stage_b, rows, dy,
+    gu, dn, raw, mixed, ghid, grow, eo, up_grad, down_grad,
     send, recv, local, load_sem,
 ):
     at = place()
@@ -642,7 +668,7 @@
         for i, (src, dst) in enumerate(
             (
                 (hot_a_in, hot_a), (nf_a_in, nf_a), (hot_b_in, hot_b), (nf_b_in, nf_b),
-                (gate_up.at[0], gu), (dy1_in, dy1), (down.at[0], dn), (dy2_in, dy2),
+                (dy_in, dy), (down.at[0], dn), (gate_up.at[0], gu),
             )
         )
     ]
@@ -652,106 +678,78 @@
     moves = Moves(send, recv, local)
     for load in loads[:4]:
         load.wait()
-    to_slots(hot_a, nf_a, sa1, 0)
-    to_slots(hot_b, nf_b, sb1, 0)
-    waits1 = deliver(moves, at, sa1, sb1, rows1, WIDE_A)
-    to_slots(hot_a, nf_a, sa2, 1)
-    to_slots(hot_b, nf_b, sb2, 1)
-    waits2 = deliver(moves, at, sa2, sb2, rows2, WIDE_A)
+    waits = []
+    for piece in range(PARTS):
+        to_slots(hot_a, nf_a, stage_a, piece)
+        to_slots(hot_b, nf_b, stage_b, piece)
+        waits.append(deliver(moves, at, stage_a, stage_b, rows, WIDE_A, piece))
     for load in loads[4:]:
         load.wait()
+
+    def raw_tile(j, carry):
+        lanes = pl.ds(pl.multiple_of(j * TILE, TILE), TILE)
+        raw[:, lanes] = mul(dy[...].reshape(ROWS, D), dn[lanes, :], NT)
+        return carry
+
+    lax.fori_loop(0, FF // TILE, raw_tile, 0)
     back_waits = []
-
-    def work(rows, dy, grow, eo, n, start, blocks):
-        small = 512 // n
-
-        def at_small(i):
-            return i // 8, i % 8
-
-        def gate_of(zz, q):
-            lanes = iota((n, LANES), 1)
-            mine = (lanes == me) | (lanes == me + EXPERTS) | (lanes == me + 2 * EXPERTS)
-            held = rows[zz, q, :, 0:LANES].astype(F32)
-            return jnp.sum(jnp.where(mine, held, 0.0), axis=1, keepdims=True)
-
-        def scale_step(i, carry):
-            zz, q = at_small(i)
-            base = pl.multiple_of(start + i * n, n)
-            grads[pl.ds(base, n), :] = (dy[zz, q].astype(F32) * gate_of(zz, q)).astype(BF16)
+    for piece in range(PARTS):
+        for wait in waits[piece]:
+            wait()
+        block = slice(piece * PIECE_ROWS, (piece + 1) * PIECE_ROWS)
+        gate_lanes = iota((PIECE_ROWS, LANES), 1)
+        mine = (
+            (gate_lanes == me)
+            | (gate_lanes == me + EXPERTS)
+            | (gate_lanes == me + 2 * EXPERTS)
+        )
+        held = rows[piece, :, :, :, 0:LANES].reshape(PIECE_ROWS, LANES).astype(F32)
+        gate = jnp.sum(jnp.where(mine, held, 0.0), axis=1, keepdims=True)
+
+        def hidden_tile(j, slope_sum, piece=piece, block=block, gate=gate):
+            lanes = pl.ds(pl.multiple_of(j * TILE, TILE), TILE)
+            upper = pl.ds(pl.multiple_of(FF + j * TILE, TILE), TILE)
+            g = mul(rows[piece, :, :, :, LANES:].reshape(PIECE_ROWS, D), gu[:, lanes])
+            act, slope = gelu_parts(g)
+            u = mul(rows[piece, :, :, :, LANES:].reshape(PIECE_ROWS, D), gu[:, upper])
+            m = raw[block, lanes]
+            both = act * u
+            mixed[block, lanes] = (both * gate).astype(BF16)
+            slope_sum = slope_sum + jnp.sum(both * m, axis=1, keepdims=True)
+            m = m * gate
+            ghid[block, lanes] = (m * u * slope).astype(BF16)
+            ghid[block, upper] = (m * act).astype(BF16)
+            return slope_sum
+
+        slopes = lax.fori_loop(0, FF // TILE, hidden_tile, jnp.zeros((PIECE_ROWS, 1), F32))
+        held = jnp.zeros((PIECE_ROWS, LANES), F32)
+        for k, third in enumerate(thirds(slopes)):
+            held = jnp.where(gate_lanes == me + k * EXPERTS, third.astype(F32), held)
+        grow[piece, :, :, :, 0:LANES] = held.astype(BF16).reshape(4, 8, PART, LANES)
+
+        def rows_tile(j, carry, piece=piece, block=block):
+            lanes = pl.ds(pl.multiple_of(j * TILE, TILE), TILE)
+            into = pl.ds(pl.multiple_of(LANES + j * TILE, LANES), TILE)
+            part = mul(ghid[block, :], gu[lanes, :], NT).astype(BF16)
+            grow[piece, :, :, :, into] = part.reshape(4, 8, PART, TILE)
             return carry
 
-        lax.fori_loop(0, blocks * small, scale_step, 0)
-        per = 4 // blocks
-        for b in range(blocks):
-            zs = slice(b * per, (b + 1) * per)
-            block = slice(start + b * 512, start + (b + 1) * 512)
-
-            def hidden_tile(j, carry, zs=zs, block=block):
-                lanes = pl.ds(pl.multiple_of(j * TILE, TILE), TILE)
-                upper = pl.ds(pl.multiple_of(FF + j * TILE, TILE), TILE)
-                g = mul(rows[zs, :, :, LANES:].reshape(512, D), gu[:, lanes])
-                act, slope = gelu_parts(g)
-                u = mul(rows[zs, :, :, LANES:].reshape(512, D), gu[:, upper])
-                mixed[block, lanes] = (act * u).astype(BF16)
-                m = mul(grads[block, :], dn[lanes, :], NT)
-                ghid[block, lanes] = (m * u * slope).astype(BF16)
-                ghid[block, upper] = (m * act).astype(BF16)
-                return carry
-
-            lax.fori_loop(0, FF // TILE, hidden_tile, 0)
-
-            def rows_tile(j, carry, zs=zs, block=block):
-                lanes = pl.ds(pl.multiple_of(j * TILE, TILE), TILE)
-                into = pl.ds(pl.multiple_of(LANES + j * TILE, LANES), TILE)
-                part = mul(ghid[block, :], gu[lanes, :], NT).astype(BF16)
-                grow[zs, :, :, into] = part.reshape(per, 8, n, TILE)
-                return carry
-
-            lax.fori_loop(0, D // TILE, rows_tile, 0)
-        back_b = back_b1 if n == FIRST else back_b2
-        back_waits.extend(give_back_b(moves, at, grow, back_b, WIDE_A))
-        for b in range(blocks):
-            zs = slice(b * per, (b + 1) * per)
-            block = slice(start + b * 512, start + (b + 1) * 512)
-
-            def out_tile(j, carry, zs=zs, block=block):
-                lanes = pl.ds(pl.multiple_of(j * TILE, TILE), TILE)
-                part = mul(mixed[block, :], dn[:, lanes]).astype(BF16)
-                eo[zs, :, :, lanes] = part.reshape(per, 8, n, TILE)
-                return carry
-
-            lax.fori_loop(0, D // TILE, out_tile, 0)
-
-        def gate_step(i, carry):
-            zz, q = at_small(i)
-            out = eo[zz, q].astype(F32)
-            slope = jnp.sum(out * dy[zz, q].astype(F32), axis=1, keepdims=True)
-            lanes = iota((n, LANES), 1)
-            held = jnp.zeros((n, LANES), F32)
-            for k, third in enumerate(thirds(slope)):
-                held = jnp.where(lanes == me + k * EXPERTS, third.astype(F32), held)
-            grow[zz, q, :, 0:LANES] = held.astype(BF16)
-            eo[zz, q] = (out * gate_of(zz, q)).astype(BF16)
-            return carry
-
-        lax.fori_loop(0, blocks * small, gate_step, 0)
-        back_a = back_a1 if n == FIRST else back_a2
-        back_waits.extend(give_back_a(moves, at, grow, back_a, WIDE_A))
-
-    for wait in waits1:
-        wait()
-    work(rows1, dy1, grow1, eo1, FIRST, 0, 2)
-    back_waits.append(moves.keep(eo1, out1).wait)
-    for wait in waits2:
-        wait()
-    work(rows2, dy2, grow2, eo2, SECOND, 1024, 1)
-    back_waits.append(moves.keep(eo2, out2).wait)
+        lax.fori_loop(0, D // TILE, rows_tile, 0)
+        back_waits += give_back(moves, at, grow, back_a, back_b, WIDE_A, piece)
+
+    def out_tile(j, carry):
+        lanes = pl.ds(pl.multiple_of(j * TILE, TILE), TILE)
+        part = mul(mixed[...], dn[:, lanes]).astype(BF16)
+        eo[:, :, :, :, lanes] = part.reshape(PARTS, 4, 8, PART, TILE)
+        return carry
+
+    lax.fori_loop(0, D // TILE, out_tile, 0)
+    back_waits.append(moves.keep(eo, out).wait)
 
     def up_tile(j, carry):
         lanes = pl.ds(pl.multiple_of(j * TILE, TILE), TILE)
         held = pl.ds(pl.multiple_of(LANES + j * TILE, LANES), TILE)
-        part = mul(rows1[:, :, :, held].reshape(1024, TILE), ghid[0:1024, :], TN)
-        part = part + mul(rows2[:, :, :, held].reshape(512, TILE), ghid[1024:, :], TN)
+        part = mul(rows[:, :, :, :, held].reshape(ROWS, TILE), ghid[...], TN)
         up_grad[lanes, :] = part.astype(BF16)
         return carry
 
@@ -760,7 +758,8 @@
 
     def down_tile(j, carry):
         lanes = pl.ds(pl.multiple_of(j * TILE, TILE), TILE)
-        down_grad[lanes, :] = mul(mixed[:, lanes], grads[...], TN).astype(BF16)
+        part = mul(mixed[:, lanes], dy[...].reshape(ROWS, D), TN)
+        down_grad[lanes, :] = part.astype(BF16)
         return carry
 
     lax.fori_loop(0, FF // TILE, down_tile, 0)
@@ -770,39 +769,43 @@
     moves.drain()
 
 
-def pieces(*lead, width):
-    return [(*lead, n, width) for n in PIECES]
-
-
 def run_experts(*operands):
-    anywhere = pl.BlockSpec(memory_space=pl.ANY)
+    anywhere = pl.BlockSpec(memory_space=pltpu.HBM)
     vmem, dma = pltpu.VMEM, pltpu.SemaphoreType.DMA
     outs = (
-        pieces(8, 4, width=WIDE_A)
-        + pieces(8, 4, width=WIDE_B)
-        + pieces(4, 8, width=D)
-        + [(D, 2 * FF), (FF, D)]
+        (PARTS, 8, 4, PART, WIDE_A),
+        (PARTS, 8, 4, PART, WIDE_B),
+        (PARTS, 4, 8, PART, D),
+        (D, 2 * FF),
+        (FF, D),
     )
     held = (
-        [(4, COUNT, SLOTS)] * 2
-        + [(4, COUNT, WIDE_A), (4, COUNT, WIDE_B)]
-        + pieces(8, 4, width=WIDE_A)
-        + pieces(8, 4, width=WIDE_B)
-        + pieces(4, 8, width=WIDE)
-        + pieces(4, 8, width=D)
-        + [(D, 2 * FF), (FF, D), (ROWS, D), (ROWS, FF), (ROWS, 2 * FF)]
-        + pieces(4, 8, width=WIDE)
-        + pieces(4, 8, width=D)
-        + [(D, 2 * FF), (FF, D)]
+        (4, COUNT, SLOTS),
+        (4, COUNT, SLOTS),
+        (4, COUNT, WIDE_A),
+        (4, COUNT, WIDE_B),
+        (PARTS, 8, 4, PART, WIDE_A),
+        (PARTS, 8, 4, PART, WIDE_B),
+        (PARTS, 4, 8, PART, WIDE),
+        (PARTS, 4, 8, PART, D),
+        (D, 2 * FF),
+        (FF, D),
+        None,
+        (ROWS, FF),
+        (ROWS, 2 * FF),
+        (PARTS, 4, 8, PART, WIDE),
+        (PARTS, 4, 8, PART, D),
+        (D, 2 * FF),
+        (FF, D),
     )
     return pl.pallas_call(
         experts_kernel,
         name="experts",
         out_shape=tuple(jax.ShapeDtypeStruct(shape, BF16) for shape in outs),
-        in_specs=[anywhere] * 8,
-        out_specs=(anywhere,) * 8,
-        scratch_shapes=[vmem(shape, BF16) for shape in held]
-        + [dma((56,)), dma((56,)), dma((12,)), dma((8,))],
+        in_specs=[anywhere] * 7,
+        out_specs=(anywhere,) * 5,
+        scratch_shapes=[vmem(shape, BF16) if shape else vmem((ROWS, FF), F32) for shape in held]
+        + [dma((84,)), dma((84,)), dma((15,)), dma((7,))],
         compiler_params=pltpu.CompilerParams(
             collective_id=2, has_side_effects=True, vmem_limit_bytes=60 * 1024 * 1024
         ),
@@ -849,9 +852,9 @@
 def forward_kernel(
     lengths, tokens, wq_in, wb_in, named, cosd, sind, hot_a_in, hot_b_in, dy_a_in, dy_b_in,
     q_out, kv_out, attended_out, middle_out, normed_out, tops, totals, gates_out,
-    nf_a, nf_b, dy1, dy2,
+    nf_a, nf_b, dy_rows,
     wq, wb, kv, own_kv, bias, vt, q, attended, middle, normed, nf,
-    hot_a, hot_b, dy_a, dy_b, sa1, sa2, sb1, sb2, send, recv, local, load_sem,
+    hot_a, hot_b, dy_a, dy_b, stage_a, stage_b, send, recv, local, load_sem,
 ):
     at = place()
     y, z, c, x = at
@@ -890,12 +893,10 @@
     kv[rows, :] = own_kv[...]
     for load in loads[3:]:
         load.wait()
-    to_slots(hot_a, dy_a, sa1, 0)
-    to_slots(hot_b, dy_b, sb1, 0)
-    to_slots(hot_a, dy_a, sa2, 1)
-    to_slots(hot_b, dy_b, sb2, 1)
-    dy_waits = deliver(moves, at, sa1, sb1, dy1, HALF)
-    dy_waits += deliver(moves, at, sa2, sb2, dy2, HALF)
+    for piece in range(PARTS):
+        to_slots(hot_a, dy_a, stage_a, piece)
+        to_slots(hot_b, dy_b, stage_b, piece)
+    dy_waits = deliver(moves, at, stage_a, stage_b, dy_rows, HALF, slice(None))
     fill_bias(lengths, bias, x)
     loads[1].wait()
 
@@ -950,11 +951,13 @@
     nf[:, 0:LANES] = held.astype(BF16)
     nf[:, LANES:] = (m * inverse * gains[1:2, :]).astype(BF16)
     half_a, half_b = nf.at[:, pl.ds(0, WIDE_A)], nf.at[:, pl.ds(WIDE_A, WIDE_B)]
-    last = [moves.push(half_a, nf_a.at[y], peer) for peer in line_y]
-    last += [moves.push(half_b, nf_b.at[z], peer) for peer in line_z]
+    last = [
+        around(moves, half_a, nf_a, y, line_y[0], line_y[2]),
+        around(moves, half_b, nf_b, z, line_z[0], line_z[2]),
+    ]
     stays += [moves.keep(half_a, nf_a.at[y]), moves.keep(half_b, nf_b.at[z])]
-    for push in last:
-        push.wait_recv()
+    for wait in last[0]() + last[1]():
+        wait()
     for stay in stays:
         stay.wait()
     for wait in dy_waits:
@@ -963,7 +966,7 @@
 
 
 def run_forward(*operands):
-    anywhere = pl.BlockSpec(memory_space=pl.ANY)
+    anywhere = pl.BlockSpec(memory_space=pltpu.HBM)
     inside = pl.BlockSpec(memory_space=pltpu.VMEM)
     vmem, dma = pltpu.VMEM, pltpu.SemaphoreType.DMA
     shape = jax.ShapeDtypeStruct
@@ -981,12 +984,12 @@
             shape((COUNT, 128), F32),
             shape((4, COUNT, WIDE_A), BF16),
             shape((4, COUNT, WIDE_B), BF16),
-            *(shape(piece, BF16) for piece in pieces(4, 8, width=D)),
+            shape((PARTS, 4, 8, PART, D), BF16),
         ),
         in_specs=[pl.BlockSpec(memory_space=pltpu.SMEM), inside, anywhere, anywhere]
         + [inside] * 3
         + [anywhere] * 4,
-        out_specs=(anywhere,) * 5 + (inside,) * 3 + (anywhere,) * 4,
+        out_specs=(anywhere,) * 5 + (inside,) * 3 + (anywhere,) * 3,
         scratch_shapes=[
             vmem((D, WA), BF16),
             vmem((D, WB), BF16),
@@ -1003,14 +1006,14 @@
             vmem((4, COUNT, SLOTS), BF16),
             vmem((4, COUNT, HALF), BF16),
             vmem((4, COUNT, HALF), BF16),
-            *(vmem(piece, BF16) for piece in pieces(8, 4, width=HALF) * 2),
-            dma((3 + 28 + 6,)),
-            dma((3 + 28 + 6,)),
-            dma((4 + 7,)),
+            *(vmem((PARTS, 8, 4, PART, HALF), BF16),) * 2,
+            dma((3 + 14 + 8,)),
+            dma((3 + 14 + 8,)),
+            dma((2 + 7,)),
             dma((7,)),
         ],
         compiler_params=pltpu.CompilerParams(
-            collective_id=3, has_side_effects=True, vmem_limit_bytes=48 * 1024 * 1024
+            collective_id=3, has_side_effects=True, vmem_limit_bytes=60 * 1024 * 1024
         ),
         cost_estimate=pl.CostEstimate(
             flops=6_000_000_000, bytes_accessed=30_000_000, transcendentals=3_200_000
@@ -1029,22 +1032,21 @@
 def backward_kernel(
     lengths, tokens_in, cotangent_in, gates, queries_in, kv_src, attended_in, middle_in, normed_in,
     tops, totals, cosd, sind, wq_in, wb_in, hot_a_in, hot_b_in,
-    back_a1_in, back_a2_in, back_b1_in, back_b2_in, out1, out2, up_in, down_in,
-    output, grad_tokens, grad_qkv_out, grad_out_out, grad_small, up_far, down_far,
-    far_a1, far_a2, far_b1, far_b2,
+    back_a_in, back_b_in, out_in, up_in, down_in,
+    grad_tokens, grad_qkv_out, grad_out_out, grad_small, up_far, down_far,
+    late_a, late_b, came_a, came_b,
     tokens, cotangent, queries, kv_in, attended, middle, normed,
-    wq, wb, hot_a, hot_b, back_a1, back_a2, back_b1, back_b2,
-    part_a, part_b, land_a, land_b, late_a, late_b,
+    wq, wb, hot_a, hot_b, back_a, back_b,
+    part_a, part_b, land_a, land_b,
     bias, kt, gn, gmid, gb, gatt, gp, dk, dv, leave, land, grad_qkv,
-    send, recv, local, load_sem,
+    send, recv, local, load_sem, empty,
 ):
     at = place()
     y, z, c, x = at
     line_y, line_z = lines(y, z, c, x)
     peers = [device(y, z, c, (x + d) % 4) for d in (1, 2, 3)]
     pairs = (
-        (back_a1_in, back_a1), (back_a2_in, back_a2), (hot_a_in, hot_a),
-        (back_b1_in, back_b1), (back_b2_in, back_b2), (hot_b_in, hot_b),
+        (back_a_in, back_a), (hot_a_in, hot_a), (back_b_in, back_b), (hot_b_in, hot_b),
         (kv_src, kv_in), (wb_in, wb), (middle_in, middle), (cotangent_in, cotangent),
         (queries_in, queries), (attended_in, attended), (tokens_in, tokens),
         (normed_in, normed), (wq_in, wq),
@@ -1056,11 +1058,20 @@
         load.start()
     greet(cross(*at) + peers)
     link = Moves(send, recv, local)
-    for load in loads[:6]:
+    for load in loads[:4]:
         load.wait()
-    part_waits = add_up(hot_a, back_a1, back_a2, part_a, land_a, y, line_y, link)
-    part_waits += add_up(hot_b, back_b1, back_b2, part_b, land_b, z, line_z, link)
-    part_drain = list(link.made)
+    part_waits = []
+    for hits, back, parts, land_here, me, line, width in (
+        (hot_a, back_a, part_a, land_a, y, line_y, WIDE_A),
+        (hot_b, back_b, part_b, land_b, z, line_z, WIDE_B),
+    ):
+        for d in (1, 2, 3):
+            parts[d - 1] = add_up(hits, back, (me + d) % 4, width)
+            push = link.push(parts.at[d - 1], land_here.at[me], line[d - 1])
+            part_waits.append(push.wait_recv)
+        land_here[pl.ds(me, 1)] = add_up(hits, back, me, width)[None]
+    for peer in cross(*at):
+        pl.semaphore_signal(empty, inc=1, device_id=peer, device_id_type=MESH)
     facing = (x + 2) % 4
     pushes = []
     for half, peer in ((0, peers[2]), (1, peers[0])):
@@ -1070,16 +1081,14 @@
         down_rows = pl.ds(half * DOWN_HALF, DOWN_HALF)
         pushes.append(link.push(down_in.at[down_rows, lanes], down_far.at[half], peer))
     fill_bias(lengths, bias, x)
-    for load in loads[6:]:
+    for load in loads[4:]:
         load.wait()
     for g in range(HEADS_KV):
         kt[g] = kv_in[:, g * 128 : (g + 1) * 128].T
     for wait in part_waits:
         wait()
-    out_waits = give_back_a(link, at, out1, far_a1, HALF)
-    out_waits += give_back_b(link, at, out1, far_b1, HALF)
-    out_waits += give_back_a(link, at, out2, far_a2, HALF)
-    out_waits += give_back_b(link, at, out2, far_b2, HALF)
+    pl.semaphore_wait(empty, 13)
+    out_waits = give_back(link, at, out_in, back_a, back_b, HALF, slice(None))
     total = land_a[0].astype(F32)
     for s in range(1, 4):
         total = total + land_a[s].astype(F32)
@@ -1126,6 +1135,23 @@
             away = pl.ds(pl.multiple_of(((x + d) % 4) * COUNT, COUNT), COUNT)
             kv_pushes.append(link.push(leave.at[g, away], land.at[g, d - 1], peers[d - 1]))
 
+    for wait in out_waits:
+        wait()
+    for s in range(4):
+        land_a[s, :, 0:HALF] = add_up(hot_a, back_a, s, HALF)
+        land_b[s, :, 0:HALF] = add_up(hot_b, back_b, s, HALF)
+    first, second, lanes = pl.ds(0, COUNT // 2), pl.ds(COUNT // 2, COUNT // 2), pl.ds(0, HALF)
+    late, stays = [], []
+    for parts, came, left, me, line in (
+        (land_a, came_a, late_a, y, line_y),
+        (land_b, came_b, late_b, z, line_z),
+    ):
+        for d in (1, 2, 3):
+            push = link.push(parts.at[(me + d) % 4, first, lanes], came.at[me], line[d - 1])
+            late.append(push.wait_recv)
+        stays.append(link.keep(parts.at[me, first, lanes], came.at[me]))
+        stays.append(link.keep(parts.at[:, second, lanes], left))
+
     def out_tile(j, carry):
         lanes = pl.ds(pl.multiple_of(j * 256, 256), 256)
         grad_qkv[lanes, 0:D] = mul(gb[:, lanes], attended[...], TN).astype(BF16)
@@ -1144,24 +1170,6 @@
     router_grad = sum(mul(tokens[...], part, TN) for part in parts)
     small = wb[:, D:]
 
-    for wait in out_waits:
-        wait()
-    pairs = ((far_a1, back_a1), (far_a2, back_a2), (far_b1, back_b1), (far_b2, back_b2))
-    again = [
-        link.keep(src, dst.at[:, :, :, pl.ds(0, HALF)] if dst.shape[3] > HALF else dst)
-        for src, dst in pairs
-    ]
-    for copy in again:
-        copy.wait()
-    for copy in part_drain:
-        copy.wait_send()
-    width = pl.ds(0, HALF)
-    late = add_up(
-        hot_a, back_a1, back_a2, part_a, late_a, y, line_y, link
-    ) + add_up(
-        hot_b, back_b1.at[:, :, :, width], back_b2.at[:, :, :, width],
-        part_b.at[:, :, width], late_b, z, line_z, link,
-    )
     for push in kv_pushes:
         push.wait_recv()
     mine = pl.ds(pl.multiple_of(x * COUNT, COUNT), COUNT)
@@ -1182,7 +1190,7 @@
         return carry
 
     lax.fori_loop(0, D // 256, qkv_tile, 0)
-    stays = [link.keep(grad_qkv, grad_qkv_out)]
+    stays.append(link.keep(grad_qkv, grad_qkv_out))
     moved, attn_gain = norm_grad(tokens[...].astype(F32), gains[0:1, :], gn[...])
     from_router = sum(mul(part, small, NT) for part in parts)
     grad_tokens[...] = (gmid[...] + moved + from_router).astype(BF16)
@@ -1191,23 +1199,17 @@
     )
     gain_columns = sum(mul(part, select, TN) for part in thirds(both))
     grad_small[...] = (router_grad + gain_columns).astype(BF16)
+    for push in pushes:
+        push.wait_recv()
     for wait in late:
         wait()
-    for half, landed in enumerate((late_a, late_b)):
-        lanes = slice(half * HALF, (half + 1) * HALF)
-        total = middle[:, lanes]
-        for s in range(4):
-            total = total + landed[s].astype(F32)
-        output[:, lanes] = total.astype(BF16)
-    for push in pushes:
-        push.wait_recv()
     for stay in stays:
         stay.wait()
-    link.drain(skip=part_drain)
+    link.drain()
 
 
 def run_backward(*operands):
-    anywhere = pl.BlockSpec(memory_space=pl.ANY)
+    anywhere = pl.BlockSpec(memory_space=pltpu.HBM)
     inside = pl.BlockSpec(memory_space=pltpu.VMEM)
     vmem, dma = pltpu.VMEM, pltpu.SemaphoreType.DMA
     shape = jax.ShapeDtypeStruct
@@ -1216,21 +1218,20 @@
         name="backward",
         out_shape=(
             shape((COUNT, D), BF16),
-            shape((COUNT, D), BF16),
             shape((D, WA), BF16),
             shape((D, D), BF16),
             shape((D, SMALL), BF16),
             shape((2, UP_HALF, 2 * FF), BF16),
             shape((2, DOWN_HALF, DOWN_PART), BF16),
-            *(shape(piece, BF16) for piece in pieces(8, 4, width=HALF) * 2),
+            *(shape((4, COUNT // 2, HALF), BF16),) * 4,
         ),
         in_specs=[pl.BlockSpec(memory_space=pltpu.SMEM)]
         + [anywhere] * 2
         + [inside]
         + [anywhere] * 5
         + [inside] * 4
-        + [anywhere] * 12,
-        out_specs=(inside, inside, anywhere, anywhere, inside) + (anywhere,) * 6,
+        + [anywhere] * 9,
+        out_specs=(inside, anywhere, anywhere, inside) + (anywhere,) * 6,
         scratch_shapes=[
             vmem((COUNT, D), BF16),
             vmem((COUNT, D), BF16),
@@ -1243,14 +1244,12 @@
             vmem((D, WB), BF16),
             vmem((4, COUNT, SLOTS), BF16),
             vmem((4, COUNT, SLOTS), BF16),
-            *(vmem(piece, BF16) for piece in pieces(8, 4, width=WIDE_A)),
-            *(vmem(piece, BF16) for piece in pieces(8, 4, width=WIDE_B)),
+            vmem((PARTS, 8, 4, PART, WIDE_A), BF16),
+            vmem((PARTS, 8, 4, PART, WIDE_B), BF16),
             vmem((3, COUNT, WIDE_A), BF16),
             vmem((3, COUNT, WIDE_B), BF16),
             vmem((4, COUNT, WIDE_A), BF16),
             vmem((4, COUNT, WIDE_B), BF16),
-            vmem((4, COUNT, HALF), BF16),
-            vmem((4, COUNT, HALF), BF16),
             vmem((GROUP_ROWS, COUNT), F32),
             vmem((HEADS_KV, HEAD_DIM, GROUP_ROWS), BF16),
             vmem((COUNT, D), F32),
@@ -1263,10 +1262,11 @@
             vmem((HEADS_KV, GROUP_ROWS, 256), BF16),
             vmem((HEADS_KV, 3, COUNT, 256), BF16),
             vmem((D, WA), BF16),
-            dma((6 + 4 + 28 + 6 + 6,)),
-            dma((6 + 4 + 28 + 6 + 6,)),
-            dma((4 + 4 + 2,)),
-            dma((15,)),
+            dma((6 + 4 + 14 + 6 + 6,)),
+            dma((6 + 4 + 14 + 6 + 6,)),
+            dma((2 + 4 + 2,)),
+            dma((13,)),
+            pltpu.SemaphoreType.REGULAR,
         ],
         compiler_params=pltpu.CompilerParams(
             collective_id=4, has_side_effects=True, vmem_limit_bytes=60 * 1024 * 1024
@@ -1321,26 +1321,25 @@
     wq = full_a.reshape(D, WA)
     wb = full_b.reshape(D, WB)
     (
-        queries, kv, attended, middle, normed, tops, totals, gates, nf_a, nf_b, dy1, dy2,
+        queries, kv, attended, middle, normed, tops, totals, gates, nf_a, nf_b, dy_rows,
     ) = run_forward(
         lengths, tokens, wq, wb, named, cosd, sind, hot_a, hot_b, dy_a, dy_b
     )
-    back_a1, back_a2, back_b1, back_b2, out1, out2, up_local, down_local = run_experts(
-        hot_a, hot_b, nf_a, nf_b, dy1, dy2, gate_up, down_proj
-    )
-    output, grad_tokens, grad_qkv, grad_out, grad_small, up_far, down_far, *_ = run_backward(
+    back_a, back_b, expert_out, up_local, down_local = run_experts(
+        hot_a, hot_b, nf_a, nf_b, dy_rows, gate_up, down_proj
+    )
+    grad_tokens, grad_qkv, grad_out, grad_small, *passed_on = run_backward(
         lengths, tokens, cotangent, gates, queries, kv, attended, middle, normed, tops, totals,
-        cosd, sind, wq, wb, hot_a, hot_b, back_a1, back_a2, back_b1, back_b2, out1, out2,
-        up_local, down_local,
-    )
-    sum_a, sum_b, up_sum, down_sum = scatter_sums(
+        cosd, sind, wq, wb, hot_a, hot_b, back_a, back_b, expert_out, up_local, down_local,
+    )
+    sum_a, sum_b, up_sum, down_sum, output = scatter_sums(
         grad_qkv.reshape(4, 4, 2, BLOCK, WA),
         grad_out.reshape(4, 4, 2, BLOCK, D),
         grad_small.reshape(4, 4, 2, BLOCK, SMALL),
         up_local,
         down_local,
-        up_far,
-        down_far,
+        *passed_on,
+        middle,
     )
     sum_b = sum_b[:PIECE]
 

time: 383 us -> 340 us (0.89)
  Pallas kernels: 354 us -> 320 us
  local copies, waits for them, and re-layouts: 24.7 us -> 15.7 us
    pallas_call x1, Pallas kernels: 84.6 us -> 66.2 us  [run_experts(): pl.pallas_call(experts_kernel, name='experts', out_shape=tuple((jax.Shape...]
    unnamed x54 -> x14, local copies, waits for them, and re-layouts: 20.3 us -> 8.2 us
    pallas_call x1, Pallas kernels: 84.5 us -> 72.6 us  [run_backward(): pl.pallas_call(backward_kernel, name='backward', out_shape=(shape((COUNT,...]
    pallas_call x1, Pallas kernels: 53.5 us -> 61.4 us  [scatter_sums(): pl.pallas_call(scatter_kernel, name='scatter_sums', out_shape=(jax.ShapeD...]
    pallas_call x1, Pallas kernels: 71.8 us -> 64.5 us  [gather_weights(): pl.pallas_call(gather_kernel, name='gather_weights', out_shape=(jax.Shape...]
    pallas_call x1, Pallas kernels: 59.9 us -> 55.4 us  [run_forward(): pl.pallas_call(forward_kernel, name='forward', out_shape=(shape((COUNT, D...]
where the time goes in v5:
time: 340 us; the launch traced here: 339 us
  Pallas kernels  320 us (94%)
  local copies, waits for them, and re-layouts  15.7 us (5%)
    pallas_call x1, Pallas kernels, run_backward(): pl.pallas_call(backward_kernel, name='backward', out_shape=(shape((COUNT,...  72.6 us
    pallas_call x1, Pallas kernels, run_experts(): pl.pallas_call(experts_kernel, name='experts', out_shape=tuple((jax.Shape...  66.2 us
    pallas_call x1, Pallas kernels, gather_weights(): pl.pallas_call(gather_kernel, name='gather_weights', out_shape=(jax.Shape...  64.5 us
    pallas_call x1, Pallas kernels, scatter_sums(): pl.pallas_call(scatter_kernel, name='scatter_sums', out_shape=(jax.ShapeD...  61.4 us
    pallas_call x1, Pallas kernels, run_forward(): pl.pallas_call(forward_kernel, name='forward', out_shape=(shape((COUNT, D...  55.4 us
    unnamed x14, local copies, waits for them, and re-layouts  8.2 us

profile of v5, /device:TPU:0, one launch (start us, length us, event | category | flops | bytes accessed | tf_op | source)
XLA Modules:
  0.0 339.5 jit_solution(3717221815057339988)
XLA Ops:
  0.6 0.8 reduce-window.8
  1.5 0.7 select_reduce_fusion
  2.2 0.7 copy.26
  3.0 0.8 copy.27
  3.7 1.0 concatenate.9
  4.7 0.7 pad.4.pack
  5.4 1.5 copy.28.top_experts
  6.9 0.5 fusion
  7.4 0.8 pad_maximum_fusion
  8.2 64.5 %gather_weights.1 = (bf16[4,4,2,48,2048]{4,3,2,1,0:T(8,128)(2,1)}, bf16[4,4,2,48,1664]{4,3,2,1,0:T(8,128)(2,1)}, f32[256,128]{1,0:T(8,128)}, bf16[4,256,384]{2,1...) custom-call(bf16[16,3712]{1,0:T(8,128)(2,1)} %pad.4.pack, ...), custom_call_target="tpu_custom_call" | custom-call | bytes 24000000 | tf_op jit(solution)/shard_map/gather_weights/pallas_call | solution.py:264
  72.8 55.4 %forward.1 = (bf16[256,1536]{1,0:T(8,128)(2,1)}, bf16[1024,512]{1,0:T(8,128)(2,1)}, bf16[256,1536]{1,0:T(8,128)(2,1)}, f32[256,1536]{1,0:T(8,128)}, bf16[256,153...) custom-call(s32[1,4]{1,0:T(1,128)} %lengths.3, ...), custom_call_target="tpu_custom_call" | custom-call | flops 6000000000 | bytes 30000000 | tf_op jit(solution)/shard_map/forward/pallas_call | solution.py:973
  128.2 66.2 %experts.1 = (bf16[3,8,4,16,768]{4,3,2,1,0:T(8,128)(2,1)}, bf16[3,8,4,16,896]{4,3,2,1,0:T(8,128)(2,1)}, bf16[3,4,8,16,1536]{4,3,2,1,0:T(8,128)(2,1)}, bf16[1536,1536]{1,0:T(8,128)(2,1)}, bf16[768,1536]{1,0:T(8,128)(2,1)}) custom-call(bf16[4,256,384]{2,1,0:T(8,128)(2,1)} %get-tuple-element.50.hot_a_in, bf16[4,256,384]{2,1,0:T(8,128)(2,1)} %get-tuple-element.51.hot_b_in, ...), custom_call_target="tpu_custom_call" | custom-call | flops 32999999488 | bytes 60000000 | tf_op jit(solution)/shard_map/experts/pallas_call | solution.py:801
  194.4 72.6 %backward.1 = (bf16[256,1536]{1,0:T(8,128)(2,1)}, bf16[1536,2048]{1,0:T(8,128)(2,1)}, bf16[1536,1536]{1,0:T(8,128)(2,1)}, bf16[1536,128]{1,0:T(8,128)(2,1)}, bf1...) custom-call(s32[1,4]{1,0:T(1,128)} %lengths.3, ...), custom_call_target="tpu_custom_call" | custom-call | flops 12999999488 | bytes 50000000 | tf_op jit(solution)/shard_map/backward/pallas_call | solution.py:1216
  267.0 0.0 copy-start.2
  267.0 61.4 %scatter_sums.1 = (f32[16,2048]{1,0:T(8,128)}, f32[16,1664]{1,0:T(8,128)}, f32[384,1536]{1,0:T(8,128)}, f32[768,384]{1,0:T(8,128)}, bf16[256,1536]{1,0:T(8,128)(2,1)}) custom-call(bf16[4,4,2,48,2048]{4,3,2,1,0:T(8,128)(2,1)} %bitcast.16, bf16[4,4,2,48,1536]{4,3,2,1,0:T(8,128)(2,1)} %bitcast.17, bf16[4,4,2,48,128]{4,3,2,1,0:T(8,128)(2,1)} %bitcast.20, ...), custom_call_target="tpu_custom_call" | custom-call | bytes 24000000 | tf_op jit(solution)/shard_map/scatter_sums/pallas_call | solution.py:513
  328.3 0.0 copy-start.3
  328.4 0.0 copy-start
  328.4 1.6 slice_reduce_fusion
  329.9 1.3 slice.24
  331.2 1.5 slice_bitcast_fusion
  332.8 2.1 copy.34
  334.8 0.0 copy-done.2
  334.8 0.9 copy.35
  335.7 0.0 copy-done.3
  335.7 0.7 copy.36
  336.4 0.0 copy-done
  336.4 0.0 copy-start.1
  336.4 1.4 copy.37
  337.8 0.7 copy-done.1
  338.5 1.0 copy.38
  (4 shorter events, 0.0 us)
Async XLA Ops:
  267.0 67.9 %copy-start.2 = (bf16[256,1536]{1,0:T(8,128)(2,1)S(1)}, bf16[256,1536]{1,0:T(8,128)(2,1)}, u32[]{:S(2)}) copy-start(bf16[256,1536]{1,0:T(8,128)(2,1)} %get-tuple-element.102) | copy-start | bytes 2359300
  328.3 7.4 %copy-start.3 = (f32[16,2048]{1,0:T(8,128)S(1)}, f32[16,2048]{1,0:T(8,128)}, u32[]{:S(2)}) copy-start(f32[16,2048]{1,0:T(8,128)} %get-tuple-element.81) | copy-start | bytes 393220
  328.4 8.0 %copy-start = (f32[384,1536]{1,0:T(8,128)S(1)}, f32[384,1536]{1,0:T(8,128)}, u32[]{:S(2)}) copy-start(f32[384,1536]{1,0:T(8,128)} %get-tuple-element.83) | copy-start | bytes 7077892
  336.4 2.1 copy-start.1
